TPU v7x, 32 devices: a whole 2x2x4 slice. The times are simulated.
32 devices in a mesh: row: 4 (over z), col: 8 (over y, x, core).
Axes of the slice: x: 2, y: 2, z: 4, core: 2. Of those that a mesh axis runs over, the one named last changes fastest.
Arguments:
- density: float32 [1024, 1024], P('row', 'col'), may hold values from -0.21875 to 0.21875
- hamiltonian: float32 [1024, 1024], P('row', 'col'), may hold values from -6 to 6
- block_mask: int32 [8, 8], replicated, may hold values from 0 to 1, as said below
Outputs:
- hp_product: float32 [1024, 1024], P('row', 'col')
- php_product: float32 [1024, 1024], P('row', 'col')
- gradient: float32 [1024, 1024], P('row', 'col')
Inputs may be any that keep to these rules, and one draw needn't show every extreme that they name: block_mask is symmetric with ones on the diagonal.
All inputs are finite; a program needn't handle non-finite values.
Results may differ from a plain program's by a relative error of at most 0.000098.
Values sent between devices are 32-bit elements; how exact they have to be, the bound alone decides.
No kernel may reach another device: no remote copies, remote signals or barrier semaphores. Data moves between devices by JAX's collectives and lax.ppermute only.
A program may use at most 64 MiB of HBM per device.

v0:
```python
import jax
import jax.numpy as jnp
from jax import lax
from jax.sharding import PartitionSpec as P

BLK = 128


highest = lax.Precision.HIGHEST


def product(leading, second):
    return jnp.dot(leading, second, precision=highest, preferred_element_type=jnp.float32)


def expand_pattern(block_mask, row_index, col_index, tile_rows, tile_cols):
    block_ids = jnp.arange(block_mask.shape[0], dtype=jnp.int32)
    row_blocks = (row_index * tile_rows + jnp.arange(tile_rows, dtype=jnp.int32)) // BLK
    col_blocks = (col_index * tile_cols + jnp.arange(tile_cols, dtype=jnp.int32)) // BLK
    row_hot = (row_blocks[:, None] == block_ids[None, :]).astype(jnp.float32)
    col_hot = (col_blocks[:, None] == block_ids[None, :]).astype(jnp.float32)
    mask_table = block_mask.astype(jnp.float32)
    row_links = product(row_hot, mask_table)
    pattern = product(row_links, col_hot.T)
    col_links = product(mask_table, col_hot.T)
    inner_block = jnp.sum(row_links, axis=0) * jnp.sum(col_links, axis=1)
    inner_live = jnp.repeat(inner_block, BLK)
    return (pattern, inner_live)


def fold_term(left_part, right_part):
    return product(left_part, right_part)


def body(density, hamiltonian, block_mask):
    row_index = lax.axis_index("row")
    col_index = lax.axis_index("col")
    tile_rows, tile_cols = density.shape
    pattern, inner_live = expand_pattern(block_mask, row_index, col_index, tile_rows, tile_cols)
    kept_density = density * pattern
    kept_hamiltonian = hamiltonian * pattern
    density_rows = lax.all_gather(kept_density, "col", axis=1, tiled=True)
    density_strip, hamiltonian_strip = (
        lax.all_gather(kept_density, "row", axis=0, tiled=True),
        lax.all_gather(kept_hamiltonian, "row", axis=0, tiled=True),
    )

    def add_with_density(segment):
        return fold_term(segment, density_strip)

    hp_product = (
        add_with_density(lax.all_gather(kept_hamiltonian, "col", axis=1, tiled=True)) * pattern
    )
    ph_product = product(density_rows, hamiltonian_strip) * pattern
    hp_strip, ph_strip = (
        lax.all_gather(hp_product, "row", axis=0, tiled=True),
        lax.all_gather(ph_product, "row", axis=0, tiled=True),
    )
    php_product = product(density_rows, hp_strip) * pattern
    pph_product = product(density_rows, ph_strip) * pattern
    hpp_product = add_with_density(lax.all_gather(hp_product, "col", axis=1, tiled=True)) * pattern
    gradient = pattern * (
        3.0 * (hp_product + ph_product) - 2.0 * (php_product + pph_product + hpp_product)
    )
    return (hp_product, php_product, gradient)


def solution(mesh):
    placed = (P("row", "col"), P("row", "col"), P())
    return jax.shard_map(
        body,
        mesh=mesh,
        in_specs=placed,
        out_specs=(P("row", "col"), P("row", "col"), P("row", "col")),
        check_vma=False,
    )
```

profile of v0, /device:TPU:0, one launch (start us, length us, event | category | flops | bytes accessed | tf_op | source)
XLA Modules:
  0.0 102.5 jit_solution(14525580169633358403)
XLA Ops:
  7.2 0.0 copy-start.5
  7.2 0.0 all-gather.4.cloned.1.call-start
  7.3 0.9 fusion.5
  8.2 0.0 copy-done.5
  8.2 1.9 %fusion.10 = (f32[256,128]{1,0:T(8,128)}, f32[256,128]{1,0:T(8,128)}, f32[256,128]{1,0:T(8,128)S(1)}) fusion(f32[256,128]{1,0:T(8,128)S(1)} %copy-done.5, f32[256,128]{1,0:T(8,128)} %param.4, f32[256,8]{1,0:T(8,128)S(1)} %fusion.5, s32[128]{0:T(128)S(1)} %and_select_fusion), kind=kOutput, calls=%fused_computation.25 | convolution fusion | flops 3212288 | bytes 664064 | tf_op jit(solution)/shard_map/dot_general | solution.py:13
  10.1 0.0 copy-start.2
  10.1 0.0 all-gather.4.cloned.1.call-update
  10.2 0.0 all-gather.6.cloned.1.call-start
  10.2 0.7 all-gather.6.cloned.1.call-update
  10.9 0.0 all-gather.8.cloned.1.call-start
  11.0 0.1 copy-done.2
  11.0 17.4 %all_gather.22 = f32[1024,128]{1,0:T(8,128)S(1)} all-gather(f32[256,128]{1,0:T(8,128)S(1)} %copy-done.2), channel_id=1, replica_groups=mesh['row'=4,'col'=8] {'row'}, dimensions={0}, use_global_device_ids=true | all-gather | bytes 655360 | tf_op jit(solution)/shard_map/all_gather | solution.py:44
  28.4 8.4 %all-gather.4.cloned.1.call-done = f32[256,1024]{1,0:T(8,128)} async-done(((f32[256,128]{1,0:T(8,128)}), f32[256,1024]{1,0:T(8,128)}) %all-gather.4.cloned.1.call-update) | async-done | bytes 1048592 | tf_op jit(solution)/shard_map/all_gather | solution.py:52
  36.8 2.9 %convolution_multiply_fusion.4 = f32[256,128]{1,0:T(8,128)} fusion(f32[256,128]{1,0:T(8,128)S(1)} %get-tuple-element.5, f32[256,1024]{1,0:T(8,128)} %all-gather.4.cloned.1.call-done, f32[1024,128]{1,0:T(8,128)S(1)} %all_gather.22), kind=kOutput, calls=%fused_computation.9 | convolution fusion | flops 402685952 | bytes 1835008 | tf_op jit(solution)/shard_map/dot_general | solution.py:13
  39.6 0.0 copy-start.3
  39.6 0.0 all-gather.8.cloned.1.call-update
  39.7 0.9 copy-done.3
  40.5 0.0 copy-start.1
  40.5 16.2 %all_gather.25 = f32[1024,128]{1,0:T(8,128)S(1)} all-gather(f32[256,128]{1,0:T(8,128)S(1)} %copy-done.3), channel_id=1, replica_groups=mesh['row'=4,'col'=8] {'row'}, dimensions={0}, use_global_device_ids=true | all-gather | bytes 655360 | tf_op jit(solution)/shard_map/all_gather | solution.py:45
  56.7 0.0 copy-done.1
  56.7 16.0 %all_gather.24 = f32[1024,128]{1,0:T(8,128)S(1)} all-gather(f32[256,128]{1,0:T(8,128)S(1)} %copy-done.1), channel_id=1, replica_groups=mesh['row'=4,'col'=8] {'row'}, dimensions={0}, use_global_device_ids=true | all-gather | bytes 655360 | tf_op jit(solution)/shard_map/all_gather | solution.py:56
  72.7 0.0 all-gather.6.cloned.1.call-done
  72.7 0.0 copy-start
  72.7 2.3 %convolution_multiply_fusion.2 = f32[256,128]{1,0:T(8,128)S(1)} fusion(f32[256,128]{1,0:T(8,128)S(1)} %get-tuple-element.5, f32[256,1024]{1,0:T(8,128)} %all-gather.6.cloned.1.call-done, f32[1024,128]{1,0:T(8,128)S(1)} %all_gather.25), kind=kOutput, calls=%fused_computation.7 | convolution fusion | flops 402685952 | bytes 1835008 | tf_op jit(solution)/shard_map/dot_general | solution.py:13
  75.0 16.0 %all_gather.26 = f32[1024,128]{1,0:T(8,128)S(1)} all-gather(f32[256,128]{1,0:T(8,128)S(1)} %convolution_multiply_fusion.2), channel_id=1, replica_groups=mesh['row'=4,'col'=8] {'row'}, dimensions={0}, use_global_device_ids=true | all-gather | bytes 655360 | tf_op jit(solution)/shard_map/all_gather | solution.py:57
  91.1 0.0 copy-done
  91.1 1.0 convolution_multiply_fusion.3
  92.1 0.0 copy-start.4
  92.1 1.0 fusion.4
  93.1 0.0 copy-done.4
  93.1 0.0 all-gather.8.cloned.1.call-done
  93.1 2.9 %fusion.3 = f32[256,128]{1,0:T(8,128)} fusion(f32[256,128]{1,0:T(8,128)S(1)} %get-tuple-element.5, f32[256,128]{1,0:T(8,128)S(1)} %fusion.4, f32[256,1024]{1,0:T(8,128)} %all-gather.8.cloned.1.call-done, f32[1024,128]{1,0:T(8,128)S(1)} %all_gather.22, f32[256,128]{1,0:T(8,128)S(1)} %copy-done.1, f32[256,128]{1,0:T(8,128)S(1)} %convolution_multiply_fusion.2), kind=kOutput, calls=%fused_computation.4 | convolution fusion | flops 402882560 | bytes 2228224 | tf_op jit(solution)/shard_map/dot_general | solution.py:13
  (2 shorter events, 0.0 us)
Async XLA Ops:
  7.2 1.1 %copy-start.5 = (f32[256,128]{1,0:T(8,128)S(1)}, f32[256,128]{1,0:T(8,128)}, u32[]{:S(2)}) copy-start(f32[256,128]{1,0:T(8,128)} %param.3) | copy-start | bytes 393220
  7.2 29.6 %all-gather.4.cloned.1.call-start = ((), (), s32[]{:S(2)}) async-start(), calls=%async_computation | async-start | bytes 1179648 | tf_op jit(solution)/shard_map/all_gather | solution.py:52
  10.1 0.9 copy-start.2
  10.2 62.6 %all-gather.6.cloned.1.call-start = ((), (), s32[]{:S(2)}) async-start(), calls=%async_computation.1 | async-start | bytes 1179648 | tf_op jit(solution)/shard_map/all_gather | solution.py:42
  10.9 82.2 %all-gather.8.cloned.1.call-start = ((), (), s32[]{:S(2)}) async-start(), calls=%async_computation.2 | async-start | bytes 1179648 | tf_op jit(solution)/shard_map/all_gather | solution.py:61
  39.6 0.9 copy-start.3
  40.5 16.2 %copy-start.1 = (f32[256,128]{1,0:T(8,128)S(1)}, f32[256,128]{1,0:T(8,128)}, u32[]{:S(2)}) copy-start(f32[256,128]{1,0:T(8,128)} %convolution_multiply_fusion.4) | copy-start | bytes 393220
  72.7 18.3 %copy-start = (f32[256,1024]{1,0:T(8,128)S(1)}, f32[256,1024]{1,0:T(8,128)}, u32[]{:S(2)}) copy-start(f32[256,1024]{1,0:T(8,128)} %all-gather.6.cloned.1.call-done) | copy-start | bytes 3145732
  92.1 1.0 copy-start.4
Sparse Core Ops, SparseCore 0:
  10.5 26.2 all-gather.3
  39.2 23.5 all-gather.5
  65.3 23.5 all-gather.7
where the time goes:
time: 103 us
  blocking collectives  65.6 us (64%)
  between operations  13.8 us (13%)
  matrix products  12.9 us (13%)
  waiting for transfers between devices  9.12 us (9%)
    all_gather x1, blocking collectives, body(): lax.all_gather(kept_density, 'row', axis=0, tiled=True)  17.4 us
    all_gather x1, blocking collectives, body(): lax.all_gather(kept_hamiltonian, 'row', axis=0, tiled=True)  16.2 us
    all_gather x1, blocking collectives, body(): lax.all_gather(ph_product, 'row', axis=0, tiled=True)  16 us
    all_gather x1, blocking collectives, body(): lax.all_gather(hp_product, 'row', axis=0, tiled=True)  16 us
    dot_general x7, matrix products, product(): jnp.dot(leading, second, precision=highest, preferred_element_type=jnp.fl...  12.9 us
    all_gather x1, waiting for transfers between devices, body(): lax.all_gather(kept_hamiltonian, 'col', axis=1, tiled=True)  8.37 us
  transfers between devices with their start and end apart: 3, of which 1 were waited for; matrix products, arithmetic and copies ran while one was open for 7% of the time, Pallas kernels for 0%

commit v1 on v0

v1 whole, which is shorter than its diff:
```python
import functools

import jax
import jax.numpy as jnp
from jax import lax
from jax.experimental import pallas as pl
from jax.experimental.pallas import tpu as pltpu
from jax.sharding import PartitionSpec as P

BLK = 128
VMEM_LIMIT = 40 * 1024 * 1024

highest = lax.Precision.HIGHEST


def product(leading, second):
    return jnp.dot(leading, second, precision=highest, preferred_element_type=jnp.float32)


def tile_pattern(block_mask, row_index, col_index, tile_rows, tile_cols):
    row_blocks = (row_index * tile_rows + jnp.arange(tile_rows, dtype=jnp.int32)) // BLK
    col_blocks = (col_index * tile_cols + jnp.arange(tile_cols, dtype=jnp.int32)) // BLK
    block_ids = jnp.arange(block_mask.shape[0], dtype=jnp.int32)
    row_hot = (row_blocks[:, None] == block_ids[None, :]).astype(jnp.float32)
    col_hot = (col_blocks[:, None] == block_ids[None, :]).astype(jnp.float32)
    return product(product(row_hot, block_mask.astype(jnp.float32)), col_hot.T)


def strips_body(density, hamiltonian, block_mask):
    row_index = lax.axis_index("row")
    col_index = lax.axis_index("col")
    pattern = tile_pattern(block_mask, row_index, col_index, *density.shape)
    kept_density = density * pattern
    kept_hamiltonian = hamiltonian * pattern
    density_rows = lax.all_gather(kept_density, "col", axis=1, tiled=True)
    hamiltonian_rows = lax.all_gather(kept_hamiltonian, "col", axis=1, tiled=True)
    density_strip = lax.all_gather(kept_density, "row", axis=0, tiled=True)
    hamiltonian_strip = lax.all_gather(kept_hamiltonian, "row", axis=0, tiled=True)
    hp_product = product(hamiltonian_rows, density_strip) * pattern
    ph_product = product(density_rows, hamiltonian_strip) * pattern
    hp_strip = lax.all_gather(hp_product, "row", axis=0, tiled=True)
    ph_strip = lax.all_gather(ph_product, "row", axis=0, tiled=True)
    hp_rows = lax.all_gather(hp_product, "col", axis=1, tiled=True)
    php_product = product(density_rows, hp_strip) * pattern
    pph_product = product(density_rows, ph_strip) * pattern
    hpp_product = product(hp_rows, density_strip) * pattern
    gradient = pattern * (
        3.0 * (hp_product + ph_product) - 2.0 * (php_product + pph_product + hpp_product)
    )
    return (hp_product, php_product, gradient)


ROWS, COLS = 4, 8


def swap(x, axis, mask):
    size = ROWS if axis == "row" else COLS
    return lax.ppermute(x, axis, [(i, i ^ mask) for i in range(size)])


def after(value, *others):
    return lax.optimization_barrier((value, *others))[0]


def split(x):
    high = x.astype(jnp.bfloat16)
    return high, (x - high.astype(jnp.float32)).astype(jnp.bfloat16)


def dot3(a, b):
    mul = functools.partial(jnp.dot, preferred_element_type=jnp.float32)
    return mul(a[0], b[0]) + (mul(a[0], b[1]) + mul(a[1], b[0]))


def place(r, col_block):
    band = jnp.bitwise_xor(lax.shift_right_logical(col_block, 1), r)
    start = band * (2 * BLK) + jnp.bitwise_and(col_block, 1) * BLK
    return pl.multiple_of(start, BLK)


def block_at(r, position):
    return 2 * jnp.bitwise_xor(position // 2, r) + position % 2


def pattern_of(mask_ref, row_blocks, col_blocks):
    rows = []
    for i in row_blocks:
        rows.append(
            jnp.concatenate(
                [jnp.full((BLK, BLK), mask_ref[i, j].astype(jnp.float32)) for j in col_blocks],
                axis=1,
            )
        )
    return jnp.concatenate(rows, axis=0)


def band_blocks(r, m):
    return [block_at(r, 2 * m), block_at(r, 2 * m + 1)]


def hp_kernel(mask_ref, hs, ho, p0, p1, p2, p3, hp_ref, hrow_hi, hrow_lo):
    r, c = lax.axis_index("row"), lax.axis_index("col")
    for j in range(4):
        for flip, ref in ((0, hs), (1, ho)):
            spot = place(r, jnp.bitwise_xor(c, 2 * j + flip))
            high, low = split(ref[j])
            hrow_hi[:, pl.ds(spot, BLK)] = high
            hrow_lo[:, pl.ds(spot, BLK)] = low
    total = jnp.zeros(hp_ref.shape, jnp.float32)
    for m, ref in enumerate((p0, p1, p2, p3)):
        at = pl.ds(m * 2 * BLK, 2 * BLK)
        total += dot3((hrow_hi[:, at], hrow_lo[:, at]), split(ref[...]))
    hp_ref[...] = total * pattern_of(mask_ref, band_blocks(r, 0), [c])


def z_kernel(
    mask_ref, hrow_hi, hrow_lo, a_s, a_o, b_s, b_o, h0, h1, h2, h3, hp_ref,
    z_ref, prow_hi, prow_lo, pw_hi, pw_lo,
):
    r, c = lax.axis_index("row"), lax.axis_index("col")
    band = 2 * BLK
    for j in range(4):
        for flip, first, rest in ((0, a_s, b_s), (1, a_o, b_o)):
            spot = pl.ds(place(r, jnp.bitwise_xor(c, 2 * j + flip)), BLK)
            high, low = split(first[j])
            pw_hi[0:band, spot] = high
            pw_lo[0:band, spot] = low
            high, low = split(rest[j])
            pw_hi[band:, spot] = high
            pw_lo[band:, spot] = low
    prow_hi[...] = pw_hi[0:band, :]
    prow_lo[...] = pw_lo[0:band, :]
    own = pattern_of(mask_ref, band_blocks(r, 0), [c])
    pcol = [split(a_s[0])] + [split(b_s[0, (m - 1) * band : m * band]) for m in (1, 2, 3)]
    hcol = [split(ref[...]) for ref in (h0, h1, h2, h3)]
    second = jnp.zeros((band, BLK), jnp.float32)
    ph = None
    for m in range(4):
        at = pl.ds(m * band, band)
        hp_rows = dot3((hrow_hi[...], hrow_lo[...]), (pw_hi[:, at], pw_lo[:, at]))
        hp_rows = hp_rows * pattern_of(mask_ref, band_blocks(r, 0), band_blocks(r, m))
        second += dot3(split(hp_rows), pcol[m])
        ph_rows = jnp.zeros((band, BLK), jnp.float32)
        for k in range(4):
            inner = pl.ds(k * band, band)
            ph_rows += dot3((pw_hi[at, inner], pw_lo[at, inner]), hcol[k])
        ph_rows = ph_rows * pattern_of(mask_ref, band_blocks(r, m), [c])
        if m == 0:
            ph = ph_rows
        second += dot3((pw_hi[0:band, at], pw_lo[0:band, at]), split(ph_rows))
    z_ref[...] = own * (3.0 * (hp_ref[...] + ph) - 2.0 * second)


def php_kernel(mask_ref, prow_hi, prow_lo, q0, q1, q2, q3, z_ref, php_ref, grad_ref):
    r, c = lax.axis_index("row"), lax.axis_index("col")
    total = jnp.zeros(php_ref.shape, jnp.float32)
    for m, ref in enumerate((q0, q1, q2, q3)):
        at = pl.ds(m * 2 * BLK, 2 * BLK)
        total += dot3((prow_hi[:, at], prow_lo[:, at]), split(ref[...]))
    php = total * pattern_of(mask_ref, band_blocks(r, 0), [c])
    php_ref[...] = php
    grad_ref[...] = z_ref[...] - 2.0 * php


def call(kernel, outs, scratch, flops, *args):
    smem, vmem = pl.BlockSpec(memory_space=pltpu.SMEM), pl.BlockSpec(memory_space=pltpu.VMEM)
    moved = sum(a.size * a.dtype.itemsize for a in (*args, *outs))
    return pl.pallas_call(
        kernel,
        out_shape=outs,
        in_specs=[smem] + [vmem] * (len(args) - 1),
        out_specs=tuple(vmem for _ in outs),
        scratch_shapes=scratch,
        cost_estimate=pl.CostEstimate(flops=flops, bytes_accessed=moved, transcendentals=0),
        compiler_params=pltpu.CompilerParams(vmem_limit_bytes=VMEM_LIMIT),
    )(*args)


def gather_row(x):
    return [swap(x, "row", m) for m in (1, 2, 3)]


def whole_body(density, hamiltonian, block_mask):
    r, c = lax.axis_index("row"), lax.axis_index("col")
    f32, bf16 = jnp.float32, jnp.bfloat16
    rows, cols = density.shape
    order = rows * ROWS
    tile = jax.ShapeDtypeStruct((rows, cols), f32)
    part = jax.ShapeDtypeStruct((rows, order), bf16)

    links = lax.dynamic_slice(block_mask, (2 * r, c), (2, 1)).astype(f32)
    pattern = jnp.broadcast_to(links[:, :, None], (2, BLK, cols)).reshape(rows, cols)
    p0, h0 = density * pattern, hamiltonian * pattern

    p1, p2, p3 = gather_row(p0)
    hx, hy, hd = swap(h0, "col", 2), swap(h0, "col", 4), swap(h0, "col", 6)
    hs = jnp.stack([h0, hx, hy, hd])
    ho = swap(hs, "col", 1)
    hp, hrow_hi, hrow_lo = call(
        hp_kernel, (tile, part, part), [], 6 * rows * order * cols,
        block_mask, hs, ho, p0, p1, p2, p3,
    )

    pa = after(p0, hx, hy, hd)
    ax, ay, ad = swap(pa, "col", 2), swap(pa, "col", 4), swap(pa, "col", 6)
    a_s = jnp.stack([p0, ax, ay, ad])
    a_o = swap(a_s, "col", 1)
    b = jnp.concatenate([p1, p2, p3], axis=0)
    b = after(b, ax, ay, ad)
    bx, by = swap(b, "col", 2), swap(b, "col", 4)
    half = b.shape[0] // 2
    bd_top = swap(bx[:half], "col", 4)
    bd_low = swap(by[half:], "col", 2)
    b_s = jnp.stack([b, bx, by, jnp.concatenate([bd_top, bd_low], axis=0)])
    b_o = swap(b_s, "col", 1)

    h1, h2, h3 = gather_row(after(h0, p1, p2, p3))
    q1, q2, q3 = gather_row(hp)
    z, prow_hi, prow_lo = call(
        z_kernel, (tile, part, part), [pltpu.VMEM((order, order), bf16)] * 2,
        6 * (rows * order * order + order * order * cols + 2 * rows * order * cols),
        block_mask, hrow_hi, hrow_lo, a_s, a_o, b_s, b_o, h0, h1, h2, h3, hp,
    )
    php, grad = call(
        php_kernel, (tile, tile), [], 6 * rows * order * cols,
        block_mask, prow_hi, prow_lo, hp, q1, q2, q3, z,
    )
    return hp, php, grad


def body(density, hamiltonian, block_mask, shape):
    tile_rows, tile_cols = density.shape
    if shape == (ROWS, COLS) and tile_rows == 2 * BLK and tile_cols == BLK:
        return whole_body(density, hamiltonian, block_mask)
    return strips_body(density, hamiltonian, block_mask)


def solution(mesh):
    placed = (P("row", "col"), P("row", "col"), P())
    return jax.shard_map(
        functools.partial(body, shape=(mesh.shape["row"], mesh.shape["col"])),
        mesh=mesh,
        in_specs=placed,
        out_specs=(P("row", "col"), P("row", "col"), P("row", "col")),
        check_vma=False,
    )
```

time: 103 us -> 75.7 us (0.73)
  the two profiles are of different devices: /device:TPU:0 before, /device:TPU:8 now
where the time goes in v1:
time: 75.7 us; the launch traced here: 75.5 us
  waiting for transfers between devices  28.6 us (38%)
  starting transfers between devices  28.5 us (38%)
  Pallas kernels  14.4 us (19%)
  other arithmetic  2.17 us (3%)
  local copies, waits for them, and re-layouts  1.03 us (1%)
  between operations  0.77 us (1%)
    ppermute x22, waiting for transfers between devices, swap(): return lax.ppermute(x, axis, [(i, i ^ mask) for i in range(size)])  28.6 us
    ppermute x22, starting transfers between devices, swap(): return lax.ppermute(x, axis, [(i, i ^ mask) for i in range(size)])  28.5 us
    pallas_call x3, Pallas kernels, call(): pl.pallas_call(kernel, out_shape=outs, in_specs=[smem] + [vmem] * (len(ar...  14.4 us
  transfers between devices with their start and end apart: 22, of which 10 were waited for; matrix products, arithmetic and copies ran while one was open for 0% of the time, Pallas kernels for 17%

profile of v1, /device:TPU:8, one launch (start us, length us, event | category | flops | bytes accessed | tf_op | source)
XLA Modules:
  0.0 75.5 jit_solution(18154230820024432228)
XLA Ops:
  0.6 0.9 %convert_reduce_fusion = f32[2]{0:T(128)S(1)} fusion(s32[8,8]{1,0:T(8,128)} %mask_ref.5, s32[]{:T(128)S(6)} %select_n.6, s32[]{:T(128)S(6)} %select_n.7), kind=kLoop, calls=%fused_computation.7 | loop fusion | flops 2 | bytes 24 | tf_op jit(solution)/shard_map/convert_element_type | solution.py:191
  1.5 0.1 broadcast_bitcast_fusion
  1.6 1.1 %broadcast_multiply_fusion = (f32[256,128]{1,0:T(8,128)S(1)}, f32[256,128]{1,0:T(8,128)S(1)}) fusion(f32[256,128]{1,0:T(8,128)} %param.3, f32[256]{0:T(256)S(1)} %broadcast_bitcast_fusion, f32[256,128]{1,0:T(8,128)} %param.4), kind=kLoop, calls=%fused_computation.5 | loop fusion | flops 65536 | bytes 525312 | tf_op jit(solution)/shard_map/mul | solution.py:193
  2.7 1.6 %collective-permute-start = (f32[256,128]{1,0:T(8,128)S(1)}, f32[256,128]{1,0:T(8,128)S(1)}, u32[]{:S(2)}, u32[]{:S(2)}) collective-permute-start(f32[256,128]{1,0:T(8,128)S(1)} %get-tuple-element.19.h0), channel_id=1, source_target_pairs={{0,2},{1,3},{2,0},{3,1},{4,6},{5,7},{6,4},{7,5},{8,10},{9,11},{10,... | collective-permute-start | bytes 393224 | tf_op jit(solution)/shard_map/ppermute | solution.py:58
  4.2 1.5 %collective-permute-start.1 = (f32[256,128]{1,0:T(8,128)S(1)}, f32[256,128]{1,0:T(8,128)S(1)}, u32[]{:S(2)}, u32[]{:S(2)}) collective-permute-start(f32[256,128]{1,0:T(8,128)S(1)} %get-tuple-element.19.h0), channel_id=1, source_target_pairs={{0,4},{1,5},{2,6},{3,7},{4,0},{5,1},{6,2},{7,3},{8,12},{9,13},{10,... | collective-permute-start | bytes 393224 | tf_op jit(solution)/shard_map/ppermute | solution.py:58
  5.7 0.5 collective-permute-start.2
  6.2 0.0 collective-permute-start.4
  6.2 3.0 %collective-permute-start.5 = (f32[256,128]{1,0:T(8,128)S(1)}, f32[256,128]{1,0:T(8,128)S(1)}, u32[]{:S(2)}, u32[]{:S(2)}) collective-permute-start(f32[256,128]{1,0:T(8,128)S(1)} %get-tuple-element.17.p0), channel_id=1, source_target_pairs={{0,16},{8,24},{16,0},{24,8},{1,17},{9,25},{17,1},{25,9},{2,18},{10... | collective-permute-start | bytes 393224 | tf_op jit(solution)/shard_map/ppermute | solution.py:58
  9.3 0.0 collective-permute-done
  9.3 0.7 collective-permute-start.6
  9.9 2.1 %collective-permute-done.1 = f32[256,128]{1,0:T(8,128)S(1)} collective-permute-done((f32[256,128]{1,0:T(8,128)S(1)}, f32[256,128]{1,0:T(8,128)S(1)}, u32[]{:S(2)}, u32[]{:S(2)}) %collective-permute-start.1) | collective-permute-done | bytes 131104 | tf_op jit(solution)/shard_map/ppermute | solution.py:58
  12.0 0.0 collective-permute-done.2
  12.0 1.2 %collective-permute-start.7 = (f32[256,128]{1,0:T(8,128)S(1)}, f32[256,128]{1,0:T(8,128)S(1)}, u32[]{:S(2)}, u32[]{:S(2)}) collective-permute-start(f32[256,128]{1,0:T(8,128)S(1)} %get-tuple-element.17.p0), channel_id=1, source_target_pairs={{0,2},{1,3},{2,0},{3,1},{4,6},{5,7},{6,4},{7,5},{8,10},{9,11},{10,... | collective-permute-start | bytes 393224 | tf_op jit(solution)/shard_map/ppermute | solution.py:58
  13.2 0.8 %collective-permute-start.8 = (f32[256,128]{1,0:T(8,128)S(1)}, f32[256,128]{1,0:T(8,128)S(1)}, u32[]{:S(2)}, u32[]{:S(2)}) collective-permute-start(f32[256,128]{1,0:T(8,128)S(1)} %get-tuple-element.17.p0), channel_id=1, source_target_pairs={{0,4},{1,5},{2,6},{3,7},{4,0},{5,1},{6,2},{7,3},{8,12},{9,13},{10,... | collective-permute-start | bytes 393224 | tf_op jit(solution)/shard_map/ppermute | solution.py:58
  14.0 0.0 collective-permute-done.4.p1
  14.0 1.4 %collective-permute-start.9 = (f32[256,128]{1,0:T(8,128)S(1)}, f32[256,128]{1,0:T(8,128)S(1)}, u32[]{:S(2)}, u32[]{:S(2)}) collective-permute-start(f32[256,128]{1,0:T(8,128)S(1)} %get-tuple-element.17.p0), channel_id=1, source_target_pairs={{0,6},{1,7},{2,4},{3,5},{4,2},{5,3},{6,0},{7,1},{8,14},{9,15},{10,... | collective-permute-start | bytes 393224 | tf_op jit(solution)/shard_map/ppermute | solution.py:58
  15.5 2.5 %collective-permute-done.5.p2 = f32[256,128]{1,0:T(8,128)S(1)} collective-permute-done((f32[256,128]{1,0:T(8,128)S(1)}, f32[256,128]{1,0:T(8,128)S(1)}, u32[]{:S(2)}, u32[]{:S(2)}) %collective-permute-start.5) | collective-permute-done | bytes 131104 | tf_op jit(solution)/shard_map/ppermute | solution.py:58
  18.0 2.3 %collective-permute-done.6.p3 = f32[256,128]{1,0:T(8,128)S(1)} collective-permute-done((f32[256,128]{1,0:T(8,128)S(1)}, f32[256,128]{1,0:T(8,128)S(1)}, u32[]{:S(2)}, u32[]{:S(2)}) %collective-permute-start.6) | collective-permute-done | bytes 131104 | tf_op jit(solution)/shard_map/ppermute | solution.py:58
  20.3 0.0 collective-permute-done.9
  20.3 1.6 %collective-permute-start.11 = (f32[768,128]{1,0:T(8,128)S(1)}, f32[768,128]{1,0:T(8,128)S(1)}, u32[]{:S(2)}, u32[]{:S(2)}) collective-permute-start(f32[768,128]{1,0:T(8,128)S(1)} %pad_maximum_fusion.3), channel_id=1, source_target_pairs={{0,2},{1,3},{2,0},{3,1},{4,6},{5,7},{6,4},{7,5},{8,10},{9,11},{10,... | collective-permute-start | bytes 1179656 | tf_op jit(solution)/shard_map/ppermute | solution.py:58
  21.9 1.5 %collective-permute-start.12 = (f32[768,128]{1,0:T(8,128)S(1)}, f32[768,128]{1,0:T(8,128)S(1)}, u32[]{:S(2)}, u32[]{:S(2)}) collective-permute-start(f32[768,128]{1,0:T(8,128)S(1)} %pad_maximum_fusion.3), channel_id=1, source_target_pairs={{0,4},{1,5},{2,6},{3,7},{4,0},{5,1},{6,2},{7,3},{8,12},{9,13},{10,... | collective-permute-start | bytes 1179656 | tf_op jit(solution)/shard_map/ppermute | solution.py:58
  23.4 6.7 %collective-permute-done.11 = f32[768,128]{1,0:T(8,128)S(1)} collective-permute-done((f32[768,128]{1,0:T(8,128)S(1)}, f32[768,128]{1,0:T(8,128)S(1)}, u32[]{:S(2)}, u32[]{:S(2)}) %collective-permute-start.11) | collective-permute-done | bytes 393248 | tf_op jit(solution)/shard_map/ppermute | solution.py:58
  30.1 1.6 %collective-permute-start.13 = (f32[384,128]{1,0:T(8,128)S(1)}, f32[384,128]{1,0:T(8,128)S(1)}, u32[]{:S(2)}, u32[]{:S(2)}) collective-permute-start(f32[384,128]{1,0:T(8,128)S(1)} %slice.8), channel_id=1, source_target_pairs={{0,4},{1,5},{2,6},{3,7},{4,0},{5,1},{6,2},{7,3},{8,12},{9,13},{10,... | collective-permute-start | bytes 589832 | tf_op jit(solution)/shard_map/ppermute | solution.py:58
  31.7 0.3 collective-permute-done.12
  32.0 1.2 %collective-permute-start.14 = (f32[384,128]{1,0:T(8,128)S(1)}, f32[384,128]{1,0:T(8,128)S(1)}, u32[]{:S(2)}, u32[]{:S(2)}) collective-permute-start(f32[384,128]{1,0:T(8,128)S(1)} %slice.9), channel_id=1, source_target_pairs={{0,2},{1,3},{2,0},{3,1},{4,6},{5,7},{6,4},{7,5},{8,10},{9,11},{10,... | collective-permute-start | bytes 589832 | tf_op jit(solution)/shard_map/ppermute | solution.py:58
  33.3 2.6 %collective-permute-done.13 = f32[384,128]{1,0:T(8,128)S(1)} collective-permute-done((f32[384,128]{1,0:T(8,128)S(1)}, f32[384,128]{1,0:T(8,128)S(1)}, u32[]{:S(2)}, u32[]{:S(2)}) %collective-permute-start.13) | collective-permute-done | bytes 196640 | tf_op jit(solution)/shard_map/ppermute | solution.py:58
  35.8 1.9 %collective-permute-done.14 = f32[384,128]{1,0:T(8,128)S(1)} collective-permute-done((f32[384,128]{1,0:T(8,128)S(1)}, f32[384,128]{1,0:T(8,128)S(1)}, u32[]{:S(2)}, u32[]{:S(2)}) %collective-permute-start.14) | collective-permute-done | bytes 196640 | tf_op jit(solution)/shard_map/ppermute | solution.py:58
  37.8 0.1 pad_maximum_fusion.b_s
  37.9 0.0 copy-start.1
  37.9 0.1 collective-permute-start.15
  38.0 0.6 collective-permute-start.3
  38.6 0.1 collective-permute-start.10
  38.7 0.1 collective-permute-start.16
  38.8 3.0 %collective-permute-start.17 = (f32[256,128]{1,0:T(8,128)S(1)}, f32[256,128]{1,0:T(8,128)S(1)}, u32[]{:S(2)}, u32[]{:S(2)}) collective-permute-start(f32[256,128]{1,0:T(8,128)S(1)} %get-tuple-element.19.h0), channel_id=1, source_target_pairs={{0,16},{8,24},{16,0},{24,8},{1,17},{9,25},{17,1},{25,9},{2,18},{10... | collective-permute-start | bytes 393224 | tf_op jit(solution)/shard_map/ppermute | solution.py:58
  41.8 0.3 collective-permute-done.3.ho
  42.1 1.6 %collective-permute-start.18 = (f32[256,128]{1,0:T(8,128)S(1)}, f32[256,128]{1,0:T(8,128)S(1)}, u32[]{:S(2)}, u32[]{:S(2)}) collective-permute-start(f32[256,128]{1,0:T(8,128)S(1)} %get-tuple-element.19.h0), channel_id=1, source_target_pairs={{0,24},{8,16},{16,8},{24,0},{1,25},{9,17},{17,9},{25,1},{2,26},{10... | collective-permute-start | bytes 393224 | tf_op jit(solution)/shard_map/ppermute | solution.py:58
  43.7 2.2 %shard_map.58 = (f32[256,128]{1,0:T(8,128)}, bf16[256,1024]{1,0:T(8,128)(2,1)S(1)}, bf16[256,1024]{1,0:T(8,128)(2,1)S(1)}) custom-call(s32[8,8]{1,0:T(8,128)S(1)} %copy-done.1, f32[4,256,128]{2,1,0:T(8,128)S(1)} %pad_maximum_fusion.1.hs, f32[4,256,128]{2,1,0:T(8,128)S(1)} %collective-permute-done.3.ho, f32[256,128]{1,0:T(8,128)S(1)} %get-tuple-element.17.p0, ...), custom_call_target="tpu_custom_call" | custom-call | flops 201326592 | bytes 2752768 | tf_op jit(solution)/shard_map/pallas_call | solution.py:168
  45.9 0.0 collective-permute-done.16.h1
  45.9 1.6 %collective-permute-start.19 = (f32[256,128]{1,0:T(8,128)}, f32[256,128]{1,0:T(8,128)S(1)}, u32[]{:S(2)}, u32[]{:S(2)}) collective-permute-start(f32[256,128]{1,0:T(8,128)} %get-tuple-element.11.hp_ref.q0), channel_id=1, source_target_pairs={{0,8},{8,0},{16,24},{24,16},{1,9},{9,1},{17,25},{25,17},{2,10},{10... | collective-permute-start | bytes 393224 | tf_op jit(solution)/shard_map/ppermute | solution.py:58
  47.5 3.9 %collective-permute-done.17.h2 = f32[256,128]{1,0:T(8,128)S(1)} collective-permute-done((f32[256,128]{1,0:T(8,128)S(1)}, f32[256,128]{1,0:T(8,128)S(1)}, u32[]{:S(2)}, u32[]{:S(2)}) %collective-permute-start.17) | collective-permute-done | bytes 131104 | tf_op jit(solution)/shard_map/ppermute | solution.py:58
  51.4 3.4 %collective-permute-start.20 = (f32[256,128]{1,0:T(8,128)}, f32[256,128]{1,0:T(8,128)S(1)}, u32[]{:S(2)}, u32[]{:S(2)}) collective-permute-start(f32[256,128]{1,0:T(8,128)} %get-tuple-element.11.hp_ref.q0), channel_id=1, source_target_pairs={{0,16},{8,24},{16,0},{24,8},{1,17},{9,25},{17,1},{25,9},{2,18},{10... | collective-permute-start | bytes 393224 | tf_op jit(solution)/shard_map/ppermute | solution.py:58
  54.8 6.0 %collective-permute-done.18.h3 = f32[256,128]{1,0:T(8,128)S(1)} collective-permute-done((f32[256,128]{1,0:T(8,128)S(1)}, f32[256,128]{1,0:T(8,128)S(1)}, u32[]{:S(2)}, u32[]{:S(2)}) %collective-permute-start.18) | collective-permute-done | bytes 131104 | tf_op jit(solution)/shard_map/ppermute | solution.py:58
  60.7 1.6 %collective-permute-start.21 = (f32[256,128]{1,0:T(8,128)}, f32[256,128]{1,0:T(8,128)S(1)}, u32[]{:S(2)}, u32[]{:S(2)}) collective-permute-start(f32[256,128]{1,0:T(8,128)} %get-tuple-element.11.hp_ref.q0), channel_id=1, source_target_pairs={{0,24},{8,16},{16,8},{24,0},{1,25},{9,17},{17,9},{25,1},{2,26},{10... | collective-permute-start | bytes 393224 | tf_op jit(solution)/shard_map/ppermute | solution.py:58
  62.3 0.0 collective-permute-done.10.a_o
  62.3 0.0 collective-permute-done.15.b_o
  62.3 0.9 %copy-done = f32[256,128]{1,0:T(8,128)S(1)} copy-done((f32[256,128]{1,0:T(8,128)S(1)}, f32[256,128]{1,0:T(8,128)}, u32[]{:S(2)}) %copy-start) | copy-done | bytes 131096
  63.2 10.4 %shard_map.59 = (f32[256,128]{1,0:T(8,128)S(1)}, bf16[256,1024]{1,0:T(8,128)(2,1)S(1)}, bf16[256,1024]{1,0:T(8,128)(2,1)S(1)}) custom-call(s32[8,8]{1,0:T(8,128)S(1)} %copy-done.1, bf16[256,1024]{1,0:T(8,128)(2,1)S(1)} %get-tuple-element.15.hrow_hi, bf16[256,1024]{1,0:T(8,128)(2,1)S(1)} %get-tuple-element.16.hrow_lo, ...), custom_call_target="tpu_custom_call" | custom-call | flops 2818572288 | bytes 7078144 | tf_op jit(solution)/shard_map/pallas_call | solution.py:168
  73.6 1.9 %shard_map.60 = (f32[256,128]{1,0:T(8,128)}, f32[256,128]{1,0:T(8,128)}) custom-call(s32[8,8]{1,0:T(8,128)S(1)} %copy-done.1, bf16[256,1024]{1,0:T(8,128)(2,1)S(1)} %get-tuple-element.20.prow_hi, bf16[256,1024]{1,0:T(8,128)(2,1)S(1)} %get-tuple-element.21.prow_lo, f32[256,128]{1,0:T(8,128)S(1)} %copy-done, f32[256,128]{1,0:T(8,128)S(1)} %collective-permute-done.19.q1, ...), custom_call_target="tpu_custom_call" | custom-call | flops 201326592 | bytes 1966336 | tf_op jit(solution)/shard_map/pallas_call | solution.py:168
  (13 shorter events, 0.2 us)
Async XLA Ops:
  2.7 6.6 %collective-permute-start = (f32[256,128]{1,0:T(8,128)S(1)}, f32[256,128]{1,0:T(8,128)S(1)}, u32[]{:S(2)}, u32[]{:S(2)}) collective-permute-start(f32[256,128]{1,0:T(8,128)S(1)} %get-tuple-element.19.h0), channel_id=1, source_target_pairs={{0,2},{1,3},{2,0},{3,1},{4,6},{5,7},{6,4},{7,5},{8,10},{9,11},{10,... | collective-permute-start | bytes 393224 | tf_op jit(solution)/shard_map/ppermute | solution.py:58
  4.2 7.8 %collective-permute-start.1 = (f32[256,128]{1,0:T(8,128)S(1)}, f32[256,128]{1,0:T(8,128)S(1)}, u32[]{:S(2)}, u32[]{:S(2)}) collective-permute-start(f32[256,128]{1,0:T(8,128)S(1)} %get-tuple-element.19.h0), channel_id=1, source_target_pairs={{0,4},{1,5},{2,6},{3,7},{4,0},{5,1},{6,2},{7,3},{8,12},{9,13},{10,... | collective-permute-start | bytes 393224 | tf_op jit(solution)/shard_map/ppermute | solution.py:58
  5.7 6.3 %collective-permute-start.2 = (f32[256,128]{1,0:T(8,128)S(1)}, f32[256,128]{1,0:T(8,128)S(1)}, u32[]{:S(2)}, u32[]{:S(2)}) collective-permute-start(f32[256,128]{1,0:T(8,128)S(1)} %get-tuple-element.19.h0), channel_id=1, source_target_pairs={{0,6},{1,7},{2,4},{3,5},{4,2},{5,3},{6,0},{7,1},{8,14},{9,15},{10,... | collective-permute-start | bytes 393224 | tf_op jit(solution)/shard_map/ppermute | solution.py:58
  6.2 7.8 %collective-permute-start.4 = (f32[256,128]{1,0:T(8,128)S(1)}, f32[256,128]{1,0:T(8,128)S(1)}, u32[]{:S(2)}, u32[]{:S(2)}) collective-permute-start(f32[256,128]{1,0:T(8,128)S(1)} %get-tuple-element.17.p0), channel_id=1, source_target_pairs={{0,8},{8,0},{16,24},{24,16},{1,9},{9,1},{17,25},{25,17},{2,10},{10... | collective-permute-start | bytes 393224 | tf_op jit(solution)/shard_map/ppermute | solution.py:58
  6.2 11.7 %collective-permute-start.5 = (f32[256,128]{1,0:T(8,128)S(1)}, f32[256,128]{1,0:T(8,128)S(1)}, u32[]{:S(2)}, u32[]{:S(2)}) collective-permute-start(f32[256,128]{1,0:T(8,128)S(1)} %get-tuple-element.17.p0), channel_id=1, source_target_pairs={{0,16},{8,24},{16,0},{24,8},{1,17},{9,25},{17,1},{25,9},{2,18},{10... | collective-permute-start | bytes 393224 | tf_op jit(solution)/shard_map/ppermute | solution.py:58
  9.3 11.0 %collective-permute-start.6 = (f32[256,128]{1,0:T(8,128)S(1)}, f32[256,128]{1,0:T(8,128)S(1)}, u32[]{:S(2)}, u32[]{:S(2)}) collective-permute-start(f32[256,128]{1,0:T(8,128)S(1)} %get-tuple-element.17.p0), channel_id=1, source_target_pairs={{0,24},{8,16},{16,8},{24,0},{1,25},{9,17},{17,9},{25,1},{2,26},{10... | collective-permute-start | bytes 393224 | tf_op jit(solution)/shard_map/ppermute | solution.py:58
  12.0 8.3 %collective-permute-start.7 = (f32[256,128]{1,0:T(8,128)S(1)}, f32[256,128]{1,0:T(8,128)S(1)}, u32[]{:S(2)}, u32[]{:S(2)}) collective-permute-start(f32[256,128]{1,0:T(8,128)S(1)} %get-tuple-element.17.p0), channel_id=1, source_target_pairs={{0,2},{1,3},{2,0},{3,1},{4,6},{5,7},{6,4},{7,5},{8,10},{9,11},{10,... | collective-permute-start | bytes 393224 | tf_op jit(solution)/shard_map/ppermute | solution.py:58
  13.2 7.1 %collective-permute-start.8 = (f32[256,128]{1,0:T(8,128)S(1)}, f32[256,128]{1,0:T(8,128)S(1)}, u32[]{:S(2)}, u32[]{:S(2)}) collective-permute-start(f32[256,128]{1,0:T(8,128)S(1)} %get-tuple-element.17.p0), channel_id=1, source_target_pairs={{0,4},{1,5},{2,6},{3,7},{4,0},{5,1},{6,2},{7,3},{8,12},{9,13},{10,... | collective-permute-start | bytes 393224 | tf_op jit(solution)/shard_map/ppermute | solution.py:58
  14.0 6.3 %collective-permute-start.9 = (f32[256,128]{1,0:T(8,128)S(1)}, f32[256,128]{1,0:T(8,128)S(1)}, u32[]{:S(2)}, u32[]{:S(2)}) collective-permute-start(f32[256,128]{1,0:T(8,128)S(1)} %get-tuple-element.17.p0), channel_id=1, source_target_pairs={{0,6},{1,7},{2,4},{3,5},{4,2},{5,3},{6,0},{7,1},{8,14},{9,15},{10,... | collective-permute-start | bytes 393224 | tf_op jit(solution)/shard_map/ppermute | solution.py:58
  20.3 9.8 %collective-permute-start.11 = (f32[768,128]{1,0:T(8,128)S(1)}, f32[768,128]{1,0:T(8,128)S(1)}, u32[]{:S(2)}, u32[]{:S(2)}) collective-permute-start(f32[768,128]{1,0:T(8,128)S(1)} %pad_maximum_fusion.3), channel_id=1, source_target_pairs={{0,2},{1,3},{2,0},{3,1},{4,6},{5,7},{6,4},{7,5},{8,10},{9,11},{10,... | collective-permute-start | bytes 1179656 | tf_op jit(solution)/shard_map/ppermute | solution.py:58
  21.9 10.1 %collective-permute-start.12 = (f32[768,128]{1,0:T(8,128)S(1)}, f32[768,128]{1,0:T(8,128)S(1)}, u32[]{:S(2)}, u32[]{:S(2)}) collective-permute-start(f32[768,128]{1,0:T(8,128)S(1)} %pad_maximum_fusion.3), channel_id=1, source_target_pairs={{0,4},{1,5},{2,6},{3,7},{4,0},{5,1},{6,2},{7,3},{8,12},{9,13},{10,... | collective-permute-start | bytes 1179656 | tf_op jit(solution)/shard_map/ppermute | solution.py:58
  30.1 5.7 %collective-permute-start.13 = (f32[384,128]{1,0:T(8,128)S(1)}, f32[384,128]{1,0:T(8,128)S(1)}, u32[]{:S(2)}, u32[]{:S(2)}) collective-permute-start(f32[384,128]{1,0:T(8,128)S(1)} %slice.8), channel_id=1, source_target_pairs={{0,4},{1,5},{2,6},{3,7},{4,0},{5,1},{6,2},{7,3},{8,12},{9,13},{10,... | collective-permute-start | bytes 589832 | tf_op jit(solution)/shard_map/ppermute | solution.py:58
  32.0 5.7 %collective-permute-start.14 = (f32[384,128]{1,0:T(8,128)S(1)}, f32[384,128]{1,0:T(8,128)S(1)}, u32[]{:S(2)}, u32[]{:S(2)}) collective-permute-start(f32[384,128]{1,0:T(8,128)S(1)} %slice.9), channel_id=1, source_target_pairs={{0,2},{1,3},{2,0},{3,1},{4,6},{5,7},{6,4},{7,5},{8,10},{9,11},{10,... | collective-permute-start | bytes 589832 | tf_op jit(solution)/shard_map/ppermute | solution.py:58
  37.9 5.8 %copy-start.1 = (s32[8,8]{1,0:T(8,128)S(1)}, s32[8,8]{1,0:T(8,128)}, u32[]{:S(2)}) copy-start(s32[8,8]{1,0:T(8,128)} %mask_ref.5) | copy-start | bytes 772
  37.9 24.4 %collective-permute-start.15 = (f32[4,768,128]{2,1,0:T(8,128)S(1)}, f32[4,768,128]{2,1,0:T(8,128)S(1)}, u32[]{:S(2)}, u32[]{:S(2)}) collective-permute-start(f32[4,768,128]{2,1,0:T(8,128)S(1)} %pad_maximum_fusion.b_s), channel_id=1, source_target_pairs={{0,1},{1,0},{2,3},{3,2},{4,5},{5,4},{6,7},{7,6},{8,9},{9,8},{10,11... | collective-permute-start | bytes 4718600 | tf_op jit(solution)/shard_map/ppermute | solution.py:58
  38.0 4.1 %collective-permute-start.3 = (f32[4,256,128]{2,1,0:T(8,128)S(1)}, f32[4,256,128]{2,1,0:T(8,128)S(1)}, u32[]{:S(2)}, u32[]{:S(2)}) collective-permute-start(f32[4,256,128]{2,1,0:T(8,128)S(1)} %pad_maximum_fusion.1.hs), channel_id=1, source_target_pairs={{0,1},{1,0},{2,3},{3,2},{4,5},{5,4},{6,7},{7,6},{8,9},{9,8},{10,11... | collective-permute-start | bytes 1572872 | tf_op jit(solution)/shard_map/ppermute | solution.py:58
  38.6 23.7 %collective-permute-start.10 = (f32[4,256,128]{2,1,0:T(8,128)S(1)}, f32[4,256,128]{2,1,0:T(8,128)S(1)}, u32[]{:S(2)}, u32[]{:S(2)}) collective-permute-start(f32[4,256,128]{2,1,0:T(8,128)S(1)} %pad_maximum_fusion.2.a_s), channel_id=1, source_target_pairs={{0,1},{1,0},{2,3},{3,2},{4,5},{5,4},{6,7},{7,6},{8,9},{9,8},{10,11... | collective-permute-start | bytes 1572872 | tf_op jit(solution)/shard_map/ppermute | solution.py:58
  38.7 7.2 %collective-permute-start.16 = (f32[256,128]{1,0:T(8,128)S(1)}, f32[256,128]{1,0:T(8,128)S(1)}, u32[]{:S(2)}, u32[]{:S(2)}) collective-permute-start(f32[256,128]{1,0:T(8,128)S(1)} %get-tuple-element.19.h0), channel_id=1, source_target_pairs={{0,8},{8,0},{16,24},{24,16},{1,9},{9,1},{17,25},{25,17},{2,10},{10... | collective-permute-start | bytes 393224 | tf_op jit(solution)/shard_map/ppermute | solution.py:58
  38.8 12.6 %collective-permute-start.17 = (f32[256,128]{1,0:T(8,128)S(1)}, f32[256,128]{1,0:T(8,128)S(1)}, u32[]{:S(2)}, u32[]{:S(2)}) collective-permute-start(f32[256,128]{1,0:T(8,128)S(1)} %get-tuple-element.19.h0), channel_id=1, source_target_pairs={{0,16},{8,24},{16,0},{24,8},{1,17},{9,25},{17,1},{25,9},{2,18},{10... | collective-permute-start | bytes 393224 | tf_op jit(solution)/shard_map/ppermute | solution.py:58
  42.1 18.6 %collective-permute-start.18 = (f32[256,128]{1,0:T(8,128)S(1)}, f32[256,128]{1,0:T(8,128)S(1)}, u32[]{:S(2)}, u32[]{:S(2)}) collective-permute-start(f32[256,128]{1,0:T(8,128)S(1)} %get-tuple-element.19.h0), channel_id=1, source_target_pairs={{0,24},{8,16},{16,8},{24,0},{1,25},{9,17},{17,9},{25,1},{2,26},{10... | collective-permute-start | bytes 393224 | tf_op jit(solution)/shard_map/ppermute | solution.py:58
  45.9 27.7 %collective-permute-start.19 = (f32[256,128]{1,0:T(8,128)}, f32[256,128]{1,0:T(8,128)S(1)}, u32[]{:S(2)}, u32[]{:S(2)}) collective-permute-start(f32[256,128]{1,0:T(8,128)} %get-tuple-element.11.hp_ref.q0), channel_id=1, source_target_pairs={{0,8},{8,0},{16,24},{24,16},{1,9},{9,1},{17,25},{25,17},{2,10},{10... | collective-permute-start | bytes 393224 | tf_op jit(solution)/shard_map/ppermute | solution.py:58
  51.4 22.2 %collective-permute-start.20 = (f32[256,128]{1,0:T(8,128)}, f32[256,128]{1,0:T(8,128)S(1)}, u32[]{:S(2)}, u32[]{:S(2)}) collective-permute-start(f32[256,128]{1,0:T(8,128)} %get-tuple-element.11.hp_ref.q0), channel_id=1, source_target_pairs={{0,16},{8,24},{16,0},{24,8},{1,17},{9,25},{17,1},{25,9},{2,18},{10... | collective-permute-start | bytes 393224 | tf_op jit(solution)/shard_map/ppermute | solution.py:58
  60.7 12.9 %collective-permute-start.21 = (f32[256,128]{1,0:T(8,128)}, f32[256,128]{1,0:T(8,128)S(1)}, u32[]{:S(2)}, u32[]{:S(2)}) collective-permute-start(f32[256,128]{1,0:T(8,128)} %get-tuple-element.11.hp_ref.q0), channel_id=1, source_target_pairs={{0,24},{8,16},{16,8},{24,0},{1,25},{9,17},{17,9},{25,1},{2,26},{10... | collective-permute-start | bytes 393224 | tf_op jit(solution)/shard_map/ppermute | solution.py:58
  62.3 0.9 %copy-start = (f32[256,128]{1,0:T(8,128)S(1)}, f32[256,128]{1,0:T(8,128)}, u32[]{:S(2)}) copy-start(f32[256,128]{1,0:T(8,128)} %get-tuple-element.11.hp_ref.q0) | copy-start | bytes 393220

commit v2 on v1

v2 whole, which is shorter than its diff:
```python
import functools

import jax
import jax.numpy as jnp
from jax import lax
from jax.experimental import pallas as pl
from jax.experimental.pallas import tpu as pltpu
from jax.sharding import PartitionSpec as P

BLK = 128
VMEM_LIMIT = 40 * 1024 * 1024
AHEAD = 8

highest = lax.Precision.HIGHEST


def product(leading, second):
    return jnp.dot(leading, second, precision=highest, preferred_element_type=jnp.float32)


def tile_pattern(block_mask, row_index, col_index, tile_rows, tile_cols):
    row_blocks = (row_index * tile_rows + jnp.arange(tile_rows, dtype=jnp.int32)) // BLK
    col_blocks = (col_index * tile_cols + jnp.arange(tile_cols, dtype=jnp.int32)) // BLK
    block_ids = jnp.arange(block_mask.shape[0], dtype=jnp.int32)
    row_hot = (row_blocks[:, None] == block_ids[None, :]).astype(jnp.float32)
    col_hot = (col_blocks[:, None] == block_ids[None, :]).astype(jnp.float32)
    return product(product(row_hot, block_mask.astype(jnp.float32)), col_hot.T)


def strips_body(density, hamiltonian, block_mask):
    row_index = lax.axis_index("row")
    col_index = lax.axis_index("col")
    pattern = tile_pattern(block_mask, row_index, col_index, *density.shape)
    kept_density = density * pattern
    kept_hamiltonian = hamiltonian * pattern
    density_rows = lax.all_gather(kept_density, "col", axis=1, tiled=True)
    hamiltonian_rows = lax.all_gather(kept_hamiltonian, "col", axis=1, tiled=True)
    density_strip = lax.all_gather(kept_density, "row", axis=0, tiled=True)
    hamiltonian_strip = lax.all_gather(kept_hamiltonian, "row", axis=0, tiled=True)
    hp_product = product(hamiltonian_rows, density_strip) * pattern
    ph_product = product(density_rows, hamiltonian_strip) * pattern
    hp_strip = lax.all_gather(hp_product, "row", axis=0, tiled=True)
    ph_strip = lax.all_gather(ph_product, "row", axis=0, tiled=True)
    hp_rows = lax.all_gather(hp_product, "col", axis=1, tiled=True)
    php_product = product(density_rows, hp_strip) * pattern
    pph_product = product(density_rows, ph_strip) * pattern
    hpp_product = product(hp_rows, density_strip) * pattern
    gradient = pattern * (
        3.0 * (hp_product + ph_product) - 2.0 * (php_product + pph_product + hpp_product)
    )
    return (hp_product, php_product, gradient)


ROWS, COLS = 4, 8


def swap(x, axis, mask):
    size = ROWS if axis == "row" else COLS
    return lax.ppermute(x, axis, [(i, i ^ mask) for i in range(size)])


def after(value, *others):
    return lax.optimization_barrier((value, *others))[0]


def split(x):
    high = x.astype(jnp.bfloat16)
    return high, (x - high.astype(jnp.float32)).astype(jnp.bfloat16)


def stacked(x):
    return jnp.concatenate(split(x), axis=0)


def beside(x):
    return jnp.concatenate(split(x), axis=1)


def mul(a, b):
    return jnp.dot(a, b, preferred_element_type=jnp.float32)


def dot_parts(a, b):
    t = mul(a, b)
    m, n = t.shape[0] // 2, t.shape[1] // 2
    return (t[:m, :n] + (t[:m, n:] + t[m:, :n])) + t[m:, n:]


def dot_wide(a, b):
    t = mul(a, b[0])
    m = t.shape[0] // 2
    return t[:m] + (t[m:] + mul(a[:m], b[1]))


def dot_tall(a, b):
    t = mul(a[0], b)
    n = t.shape[1] // 2
    return t[:, :n] + (t[:, n:] + mul(a[1], b[:, :n]))


def place(r, col_block):
    band = jnp.bitwise_xor(lax.shift_right_logical(col_block, 1), r)
    start = band * (2 * BLK) + jnp.bitwise_and(col_block, 1) * BLK
    return pl.multiple_of(start, BLK)


def block_at(r, position):
    return 2 * jnp.bitwise_xor(position // 2, r) + position % 2


def pattern_of(mask_ref, row_blocks, col_blocks):
    rows = []
    for i in row_blocks:
        rows.append(
            jnp.concatenate(
                [jnp.full((BLK, BLK), mask_ref[i, j].astype(jnp.float32)) for j in col_blocks],
                axis=1,
            )
        )
    return jnp.concatenate(rows, axis=0)


def band_blocks(r, m):
    return [block_at(r, 2 * m), block_at(r, 2 * m + 1)]


BAND = 2 * BLK


def fill_rows(mask_ref, r, c, ss, so, first, out):
    for j in range(4):
        for flip, ref in ((0, ss), (1, so)):
            block = jnp.bitwise_xor(c, 2 * j + flip)
            part = ref[first + j] * pattern_of(mask_ref, band_blocks(r, 0), [block])
            out[:, pl.ds(place(r, block), BLK)] = stacked(part)


def fill_cols(mask_ref, r, c, parts, out):
    for m, part in enumerate(parts):
        kept = part * pattern_of(mask_ref, band_blocks(r, m), [c])
        out[m * BAND : (m + 1) * BAND, :] = beside(kept)


def hp_kernel(mask_ref, ss, so, p0, p1, p2, p3, hp_ref, send_ref, hrow, pcol):
    r, c = lax.axis_index("row"), lax.axis_index("col")
    fill_rows(mask_ref, r, c, ss, so, 0, hrow)
    fill_cols(mask_ref, r, c, (p0[...], p1[...], p2[...], p3[...]), pcol)
    own = pattern_of(mask_ref, band_blocks(r, 0), [c])
    tile = dot_parts(hrow[...], pcol[...]) * own
    hp_ref[...] = tile
    send_ref[0:BAND] = tile
    send_ref[BAND:] = ss[0] * own


def rows_kernel(mask_ref, ss, so, prow):
    r, c = lax.axis_index("row"), lax.axis_index("col")
    fill_rows(mask_ref, r, c, ss, so, 4, prow)


def is_middle(r):
    return jnp.logical_or(r == 1, r == 2)


def column_pairs(mask_ref, r, c, flip, first, rest):
    for j in (0, 2):
        blocks = [jnp.bitwise_xor(c, 2 * (j + i) + flip) for i in (0, 1)]
        bands = []
        for m in range(4):
            parts = []
            for i in (0, 1):
                if m == 0:
                    part = first[4 + j + i]
                else:
                    part = rest[j + i, (m - 1) * BAND : m * BAND]
                parts.append(part * pattern_of(mask_ref, band_blocks(r, m), [blocks[i]]))
            bands.append(jnp.concatenate(parts, axis=1))
        yield blocks, split(jnp.concatenate(bands, axis=0))


def rows_at(r, ref, blocks):
    return jnp.concatenate([ref[pl.ds(place(r, b), BLK), :] for b in blocks], axis=0)


def hpp_term(mask_ref, r, hrow, pcol, blocks, cols):
    hp_rows = dot_wide(hrow[...], cols)
    hp_rows = hp_rows * pattern_of(mask_ref, band_blocks(r, 0), blocks)
    return dot_parts(stacked(hp_rows), rows_at(r, pcol, blocks))


def far_rows(cols):
    return jnp.concatenate([part[BAND : 2 * BAND] for part in cols], axis=0)


def php_kernel(mask_ref, prow, q3, q1, q2, q0, php_ref, qcol, hcol):
    r, c = lax.axis_index("row"), lax.axis_index("col")
    for m, ref in enumerate((q0, q1, q2, q3)):
        qcol[m * BAND : (m + 1) * BAND, :] = beside(ref[0:BAND])
        fill = ref[BAND:] * pattern_of(mask_ref, band_blocks(r, m), [c])
        hcol[m * BAND : (m + 1) * BAND, :] = beside(fill)
    own = pattern_of(mask_ref, band_blocks(r, 0), [c])
    php_ref[...] = dot_parts(prow[...], qcol[...]) * (own * is_middle(r).astype(jnp.float32))


def own_kernel(mask_ref, hrow, hcol, pcol, ss, b_s, ph_ref, hpp_ref, far):
    r, c = lax.axis_index("row"), lax.axis_index("col")
    ph = jnp.zeros(ph_ref.shape, jnp.float32)
    hpp = jnp.zeros(hpp_ref.shape, jnp.float32)
    for n, (blocks, cols) in enumerate(column_pairs(mask_ref, r, c, 0, ss, b_s)):
        ph += dot_tall(cols, rows_at(r, hcol, blocks))
        far[:, n * BAND : (n + 1) * BAND] = far_rows(cols)
        hpp += hpp_term(mask_ref, r, hrow, pcol, blocks, cols)
    ph_ref[...] = ph
    hpp_ref[...] = hpp


def ph_kernel(mask_ref, hcol, qcol, so, b_o, part_ref, far, back_ref, tile_ref, ph2):
    r, c = lax.axis_index("row"), lax.axis_index("col")
    back_ref[...] = jnp.zeros_like(back_ref)
    tile_ref[...] = jnp.zeros_like(tile_ref)
    ph2[...] = jnp.zeros_like(ph2)

    @pl.when(is_middle(r))
    def _():
        ph = part_ref[...]
        terms = []
        for j in (0, 2):
            blocks = [jnp.bitwise_xor(c, 2 * (j + i)) for i in (0, 1)]
            terms.append((blocks, far[:, (j // 2) * BAND : (j // 2 + 1) * BAND]))
        for blocks, cols in column_pairs(mask_ref, r, c, 1, so, b_o):
            ph += dot_tall(cols, rows_at(r, hcol, blocks))
            terms.append((blocks, far_rows(cols)))
        for m in range(4):
            rows = ph[m * BAND : (m + 1) * BAND] * pattern_of(mask_ref, band_blocks(r, m), [c])
            ph2[m * BAND : (m + 1) * BAND, :] = beside(rows)
            if m == 0:
                tile_ref[...] = rows
            if m == 1:
                beyond = rows
        pph = jnp.zeros(tile_ref.shape, jnp.float32)
        php = jnp.zeros(tile_ref.shape, jnp.float32)
        for blocks, left in terms:
            pph += dot_parts(left, rows_at(r, ph2, blocks))
            php += dot_parts(left, rows_at(r, qcol, blocks))
        there = pattern_of(mask_ref, band_blocks(r, 1), [c])
        back_ref[0:BAND] = there * (3.0 * beyond - 2.0 * (pph + php))
        back_ref[BAND:] = there * php


def last_kernel(
    mask_ref, prow, hrow, pcol, so, b_o, ph2, hp_ref, ph_ref, hpp_ref, php_ref, grad_ref
):
    r, c = lax.axis_index("row"), lax.axis_index("col")
    second = hpp_ref[...] + dot_parts(prow[...], ph2[...])
    for blocks, cols in column_pairs(mask_ref, r, c, 1, so, b_o):
        second += hpp_term(mask_ref, r, hrow, pcol, blocks, cols)
    own = pattern_of(mask_ref, band_blocks(r, 0), [c])
    grad_ref[...] = 3.0 * (hp_ref[...] + ph_ref[...]) - 2.0 * (php_ref[...] + own * second)


def call(kernel, outs, scratch, flops, *args):
    smem, vmem = pl.BlockSpec(memory_space=pltpu.SMEM), pl.BlockSpec(memory_space=pltpu.VMEM)
    moved = sum(a.size * a.dtype.itemsize for a in (*args, *outs))
    return pl.pallas_call(
        kernel,
        out_shape=outs,
        in_specs=[smem] + [vmem] * (len(args) - 1),
        out_specs=tuple(vmem for _ in outs),
        scratch_shapes=scratch,
        cost_estimate=pl.CostEstimate(flops=flops, bytes_accessed=moved, transcendentals=0),
        compiler_params=pltpu.CompilerParams(vmem_limit_bytes=VMEM_LIMIT),
    )(*args)


def to_middle(x):
    routes = [
        [(0, 1), (3, 2), (1, 0), (2, 3)],
        [(0, 2), (3, 1), (1, 0), (2, 3)],
        [(1, 2), (2, 1), (0, 0), (3, 3)],
    ]
    return [lax.ppermute(x, "row", pairs) for pairs in routes]


def whole_body(density, hamiltonian, block_mask):
    f32, bf16 = jnp.float32, jnp.bfloat16
    rows, cols = density.shape
    order = rows * ROWS

    def shape(a, b, dtype=bf16):
        return jax.ShapeDtypeStruct((a, b), dtype)

    tile, strip = shape(rows, cols, f32), shape(order, cols, f32)
    rows2, cols2 = shape(2 * rows, order), shape(order, 2 * cols)
    weight = 6 * rows * order * order
    p0, h0 = density, hamiltonian
    hx, py = swap(h0, "col", 2), swap(p0, "col", 4)
    both = lax.optimization_barrier(jnp.concatenate([p0, h0], axis=0))
    p0, h0 = both[:rows], both[rows:]
    p1, p2, p3 = [swap(p0, "row", m) for m in (1, 2, 3)]
    hy = swap(jnp.concatenate([h0, hx], axis=0), "col", 4)
    px = swap(jnp.concatenate([p0, py], axis=0), "col", 2)
    p1, p2, p3, hy, px = lax.optimization_barrier((p1, p2, p3, hy, px))
    ss = jnp.stack([h0, hx, hy[:rows], hy[rows:], p0, px[:rows], py, px[rows:]])
    so = swap(ss, "col", 1)

    b = jnp.concatenate([p1, p2, p3], axis=0)
    half = b.shape[0] // 2
    upper, lower = b[:half], b[half:]
    ux, ly = swap(upper, "col", 2), swap(lower, "col", 4)

    hp, send, hrow, pcol = call(
        hp_kernel, (tile, shape(2 * rows, cols, f32), rows2, cols2), [], weight,
        block_mask, ss, so, p0, p1, p2, p3,
    )
    q1, q2, q3 = to_middle(send)
    uy = swap(jnp.concatenate([upper, ux], axis=0), "col", 4)
    lx = swap(jnp.concatenate([lower, ly], axis=0), "col", 2)
    (prow,) = call(rows_kernel, (rows2,), [], weight, block_mask, ss, so)
    php, qcol, hcol = call(
        php_kernel, (tile, cols2, cols2), [], AHEAD * weight, block_mask, prow, q3, q1, q2, send
    )
    uy, lx, php = lax.optimization_barrier((uy, lx, php))
    b_s = jnp.stack(
        [
            jnp.concatenate(pair, axis=0)
            for pair in ((upper, lower), (ux, lx[:half]), (uy[:half], ly), (uy[half:], lx[half:]))
        ]
    )
    b_o = swap(b_s, "col", 1)

    part, hpp, far = call(
        own_kernel, (strip, tile, shape(2 * rows, order // 2)), [], weight,
        block_mask, hrow, hcol, pcol, ss, b_s,
    )
    back, ph, ph2 = call(
        ph_kernel, (shape(2 * rows, cols, f32), tile, cols2), [], weight,
        block_mask, hcol, qcol, so, b_o, part, far,
    )
    got = lax.ppermute(back, "row", [(1, 0), (2, 3)])
    (grad,) = call(
        last_kernel, (tile,), [], weight,
        block_mask, prow, hrow, pcol, so, b_o, ph2, hp, ph, hpp, php,
    )
    return hp, php + got[rows:], grad + got[:rows]


def body(density, hamiltonian, block_mask, shape):
    tile_rows, tile_cols = density.shape
    if shape == (ROWS, COLS) and tile_rows == 2 * BLK and tile_cols == BLK:
        return whole_body(density, hamiltonian, block_mask)
    return strips_body(density, hamiltonian, block_mask)


def solution(mesh):
    placed = (P("row", "col"), P("row", "col"), P())
    return jax.shard_map(
        functools.partial(body, shape=(mesh.shape["row"], mesh.shape["col"])),
        mesh=mesh,
        in_specs=placed,
        out_specs=(P("row", "col"), P("row", "col"), P("row", "col")),
        check_vma=False,
    )
```

time: 75.7 us -> 57.5 us (0.76)
  the two profiles are of different devices: /device:TPU:8 before, /device:TPU:0 now
where the time goes in v2:
time: 57.5 us; the launch traced here: 57.3 us
  waiting for transfers between devices  24.9 us (43%)
  starting transfers between devices  17.4 us (30%)
  Pallas kernels  11.9 us (21%)
  other arithmetic  2.04 us (4%)
  between operations  0.89 us (2%)
    ppermute x13, starting transfers between devices, swap(): return lax.ppermute(x, axis, [(i, i ^ mask) for i in range(size)])  13.4 us
    pallas_call x6, Pallas kernels, call(): pl.pallas_call(kernel, out_shape=outs, in_specs=[smem] + [vmem] * (len(ar...  11.9 us
    ppermute x13, waiting for transfers between devices, swap(): return lax.ppermute(x, axis, [(i, i ^ mask) for i in range(size)])  10.2 us
    ppermute x3, waiting for transfers between devices, to_middle(): return [lax.ppermute(x, 'row', pairs) for pairs in routes]  7.92 us
    ppermute x1, waiting for transfers between devices, whole_body(): got = lax.ppermute(back, 'row', [(1, 0), (2, 3)])  6.8 us
    ppermute x3, starting transfers between devices, to_middle(): return [lax.ppermute(x, 'row', pairs) for pairs in routes]  2.69 us
    ppermute x1, starting transfers between devices, whole_body(): got = lax.ppermute(back, 'row', [(1, 0), (2, 3)])  1.29 us
  transfers between devices with their start and end apart: 17, of which 7 were waited for; matrix products, arithmetic and copies ran while one was open for 2% of the time, Pallas kernels for 20%

profile of v2, /device:TPU:0, one launch (start us, length us, event | category | flops | bytes accessed | tf_op | source)
XLA Modules:
  0.0 57.3 jit_solution(12594963098434579096)
XLA Ops:
  0.6 3.0 %collective-permute-start.5 = (f32[256,128]{1,0:T(8,128)}, f32[256,128]{1,0:T(8,128)S(1)}, u32[]{:S(2)}, u32[]{:S(2)}) collective-permute-start(f32[256,128]{1,0:T(8,128)} %param.3), channel_id=1, source_target_pairs={{0,4},{1,5},{2,6},{3,7},{4,0},{5,1},{6,2},{7,3},{8,12},{9,13},{10,... | collective-permute-start | bytes 393224 | tf_op jit(solution)/shard_map/ppermute | solution.py:59
  3.7 1.5 %collective-permute-start = (f32[256,128]{1,0:T(8,128)}, f32[256,128]{1,0:T(8,128)S(1)}, u32[]{:S(2)}, u32[]{:S(2)}) collective-permute-start(f32[256,128]{1,0:T(8,128)} %param.4), channel_id=1, source_target_pairs={{0,2},{1,3},{2,0},{3,1},{4,6},{5,7},{6,4},{7,5},{8,10},{9,11},{10,... | collective-permute-start | bytes 393224 | tf_op jit(solution)/shard_map/ppermute | solution.py:59
  5.2 1.0 %pad_maximum_fusion.5 = f32[512,128]{1,0:T(8,128)S(1)} fusion(f32[256,128]{1,0:T(8,128)} %param.4, f32[256,128]{1,0:T(8,128)} %param.3), kind=kLoop, calls=%fused_computation.9 | loop fusion | flops 65536 | bytes 524288 | tf_op jit(solution)/shard_map/concatenate | solution.py:296
  6.2 3.7 %collective-permute-start.3 = (f32[256,128]{1,0:T(8,128)S(1)}, f32[256,128]{1,0:T(8,128)S(1)}, u32[]{:S(2)}, u32[]{:S(2)}) collective-permute-start(f32[256,128]{1,0:T(8,128)S(1)} %get-tuple-element.52.p0), channel_id=1, source_target_pairs={{0,24},{8,16},{16,8},{24,0},{1,25},{9,17},{17,9},{25,1},{2,26},{10... | collective-permute-start | bytes 393224 | tf_op jit(solution)/shard_map/ppermute | solution.py:59
  9.8 0.0 collective-permute-start.2
  9.8 0.8 %collective-permute-start.1 = (f32[256,128]{1,0:T(8,128)S(1)}, f32[256,128]{1,0:T(8,128)S(1)}, u32[]{:S(2)}, u32[]{:S(2)}) collective-permute-start(f32[256,128]{1,0:T(8,128)S(1)} %get-tuple-element.52.p0), channel_id=1, source_target_pairs={{0,8},{8,0},{16,24},{24,16},{1,9},{9,1},{17,25},{25,17},{2,10},{10... | collective-permute-start | bytes 393224 | tf_op jit(solution)/shard_map/ppermute | solution.py:59
  10.6 0.0 collective-permute-done.5
  10.6 0.6 %collective-permute-start.6 = (f32[512,128]{1,0:T(8,128)S(1)}, f32[512,128]{1,0:T(8,128)S(1)}, u32[]{:S(2)}, u32[]{:S(2)}) collective-permute-start(f32[512,128]{1,0:T(8,128)S(1)} %pad_maximum_fusion.7), channel_id=1, source_target_pairs={{0,2},{1,3},{2,0},{3,1},{4,6},{5,7},{6,4},{7,5},{8,10},{9,11},{10,... | collective-permute-start | bytes 786440 | tf_op jit(solution)/shard_map/ppermute | solution.py:59
  11.2 0.0 collective-permute-done
  11.3 0.0 copy-start.1
  11.3 0.4 collective-permute-start.4
  11.7 2.7 %collective-permute-done.3.p3 = f32[256,128]{1,0:T(8,128)S(1)} collective-permute-done((f32[256,128]{1,0:T(8,128)S(1)}, f32[256,128]{1,0:T(8,128)S(1)}, u32[]{:S(2)}, u32[]{:S(2)}) %collective-permute-start.3) | collective-permute-done | bytes 131104 | tf_op jit(solution)/shard_map/ppermute | solution.py:59
  14.5 5.9 %collective-permute-done.2.p2 = f32[256,128]{1,0:T(8,128)S(1)} collective-permute-done((f32[256,128]{1,0:T(8,128)S(1)}, f32[256,128]{1,0:T(8,128)S(1)}, u32[]{:S(2)}, u32[]{:S(2)}) %collective-permute-start.2) | collective-permute-done | bytes 131104 | tf_op jit(solution)/shard_map/ppermute | solution.py:59
  20.4 0.0 collective-permute-done.1.p1
  20.4 0.0 collective-permute-done.6
  20.4 0.0 collective-permute-done.4
  20.5 0.1 collective-permute-start.7
  20.6 0.6 collective-permute-start.10
  21.2 0.5 collective-permute-start.8
  21.7 1.5 %collective-permute-done.7.so = f32[8,256,128]{2,1,0:T(8,128)S(1)} collective-permute-done((f32[8,256,128]{2,1,0:T(8,128)S(1)}, f32[8,256,128]{2,1,0:T(8,128)S(1)}, u32[]{:S(2)}, u32[]{:S(2)}) %collective-permute-start.7) | collective-permute-done | bytes 1048608 | tf_op jit(solution)/shard_map/ppermute | solution.py:59
  23.2 0.0 copy-done.1
  23.2 2.2 %shard_map.58 = (f32[256,128]{1,0:T(8,128)}, f32[512,128]{1,0:T(8,128)S(1)}, bf16[512,1024]{1,0:T(8,128)(2,1)S(1)}, bf16[1024,256]{1,0:T(8,128)(2,1)S(1)}) custom-call(s32[8,8]{1,0:T(8,128)S(1)} %copy-done.1, f32[8,256,128]{2,1,0:T(8,128)S(1)} %bitcast_dynamic-update-slice_fusion.ss, f32[8,256,128]{2,1,0:T(8,128)S(1)} %collective-permute-done.7.so, ...), custom_call_target="tpu_custom_call" | custom-call | flops 1610612736 | bytes 4587776 | tf_op jit(solution)/shard_map/pallas_call | solution.py:263
  25.4 0.2 collective-permute-start.14
  25.6 1.8 %collective-permute-start.13 = (f32[512,128]{1,0:T(8,128)S(1)}, f32[512,128]{1,0:T(8,128)S(1)}, u32[]{:S(2)}, u32[]{:S(2)}) collective-permute-start(f32[512,128]{1,0:T(8,128)S(1)} %get-tuple-element.30.q0), channel_id=1, source_target_pairs={{0,8},{24,16},{8,0},{16,24},{1,9},{25,17},{9,1},{17,25},{2,10},{26... | collective-permute-start | bytes 786440 | tf_op jit(solution)/shard_map/ppermute | solution.py:280
  27.4 0.7 %collective-permute-start.12 = (f32[512,128]{1,0:T(8,128)S(1)}, f32[512,128]{1,0:T(8,128)S(1)}, u32[]{:S(2)}, u32[]{:S(2)}) collective-permute-start(f32[512,128]{1,0:T(8,128)S(1)} %get-tuple-element.30.q0), channel_id=1, source_target_pairs={{8,16},{16,8},{0,0},{24,24},{9,17},{17,9},{1,1},{25,25},{10,18},{1... | collective-permute-start | bytes 786440 | tf_op jit(solution)/shard_map/ppermute | solution.py:280
  28.1 0.0 collective-permute-done.10
  28.1 0.1 collective-permute-done.8
  28.2 0.1 fusion.1
  28.3 0.6 %collective-permute-start.11 = (f32[768,128]{1,0:T(8,128)S(1)}, f32[768,128]{1,0:T(8,128)S(1)}, u32[]{:S(2)}, u32[]{:S(2)}) collective-permute-start(f32[768,128]{1,0:T(8,128)S(1)} %get-tuple-element.54), channel_id=1, source_target_pairs={{0,2},{1,3},{2,0},{3,1},{4,6},{5,7},{6,4},{7,5},{8,10},{9,11},{10,... | collective-permute-start | bytes 1179656 | tf_op jit(solution)/shard_map/ppermute | solution.py:59
  28.9 1.5 %collective-permute-start.9 = (f32[768,128]{1,0:T(8,128)S(1)}, f32[768,128]{1,0:T(8,128)S(1)}, u32[]{:S(2)}, u32[]{:S(2)}) collective-permute-start(f32[768,128]{1,0:T(8,128)S(1)} %get-tuple-element.55), channel_id=1, source_target_pairs={{0,4},{1,5},{2,6},{3,7},{4,0},{5,1},{6,2},{7,3},{8,12},{9,13},{10,... | collective-permute-start | bytes 1179656 | tf_op jit(solution)/shard_map/ppermute | solution.py:59
  30.4 1.0 %shard_map.59.prow = bf16[512,1024]{1,0:T(8,128)(2,1)S(1)} custom-call(s32[8,8]{1,0:T(8,128)S(1)} %copy-done.1, f32[8,256,128]{2,1,0:T(8,128)S(1)} %bitcast_dynamic-update-slice_fusion.ss, f32[8,256,128]{2,1,0:T(8,128)S(1)} %collective-permute-done.7.so), custom_call_target="tpu_custom_call" | custom-call | flops 1610612736 | bytes 3145984 | tf_op jit(solution)/shard_map/pallas_call | solution.py:263
  31.4 3.1 %collective-permute-done.14.q2 = f32[512,128]{1,0:T(8,128)S(1)} collective-permute-done((f32[512,128]{1,0:T(8,128)S(1)}, f32[512,128]{1,0:T(8,128)S(1)}, u32[]{:S(2)}, u32[]{:S(2)}) %collective-permute-start.14) | collective-permute-done | bytes 262176 | tf_op jit(solution)/shard_map/ppermute | solution.py:280
  34.5 4.8 %collective-permute-done.13.q1 = f32[512,128]{1,0:T(8,128)S(1)} collective-permute-done((f32[512,128]{1,0:T(8,128)S(1)}, f32[512,128]{1,0:T(8,128)S(1)}, u32[]{:S(2)}, u32[]{:S(2)}) %collective-permute-start.13) | collective-permute-done | bytes 262176 | tf_op jit(solution)/shard_map/ppermute | solution.py:280
  39.4 0.0 collective-permute-done.12.q3
  39.4 1.1 %shard_map.60 = (f32[256,128]{1,0:T(8,128)S(1)}, bf16[1024,256]{1,0:T(8,128)(2,1)S(1)}, bf16[1024,256]{1,0:T(8,128)(2,1)S(1)}) custom-call(s32[8,8]{1,0:T(8,128)S(1)} %copy-done.1, bf16[512,1024]{1,0:T(8,128)(2,1)S(1)} %shard_map.59.prow, f32[512,128]{1,0:T(8,128)S(1)} %collective-permute-done.12.q3, f32[512,128]{1,0:T(8,128)S(1)} %collective-permute-done.13.q1, ...), custom_call_target="tpu_custom_call" | custom-call | flops 12884901888 | bytes 3277056 | tf_op jit(solution)/shard_map/pallas_call | solution.py:263
  40.4 0.0 collective-permute-done.11
  40.4 0.0 collective-permute-done.9
  40.5 0.1 fusion.2
  40.6 0.1 pad_maximum_fusion.b_s
  40.8 0.1 collective-permute-start.15
  40.8 3.9 %shard_map.61 = (f32[1024,128]{1,0:T(8,128)S(1)}, f32[256,128]{1,0:T(8,128)S(1)}, bf16[512,512]{1,0:T(8,128)(2,1)S(1)}) custom-call(s32[8,8]{1,0:T(8,128)S(1)} %copy-done.1, bf16[512,1024]{1,0:T(8,128)(2,1)S(1)} %get-tuple-element.37.hrow, bf16[1024,256]{1,0:T(8,128)(2,1)S(1)} %get-tuple-element.33.hcol, bf16[1024,256]{1,0:T(8,128)(2,1)S(1)} %get-tuple-element.38.pcol, ...), custom_call_target="tpu_custom_call" | custom-call | flops 1610612736 | bytes 5898496 | tf_op jit(solution)/shard_map/pallas_call | solution.py:263
  44.7 0.0 collective-permute-done.15.b_o
  44.7 0.0 copy-start
  44.7 0.7 %shard_map.62 = (f32[512,128]{1,0:T(8,128)S(1)}, f32[256,128]{1,0:T(8,128)S(1)}, bf16[1024,256]{1,0:T(8,128)(2,1)S(1)}) custom-call(s32[8,8]{1,0:T(8,128)S(1)} %copy-done.1, bf16[1024,256]{1,0:T(8,128)(2,1)S(1)} %get-tuple-element.33.hcol, bf16[1024,256]{1,0:T(8,128)(2,1)S(1)} %get-tuple-element.34.qcol, f32[8,256,128]{2,1,0:T(8,128)S(1)} %collective-permute-done.7.so, ...), custom_call_target="tpu_custom_call" | custom-call | flops 1610612736 | bytes 5636352 | tf_op jit(solution)/shard_map/pallas_call | solution.py:263
  45.4 1.3 %collective-permute-start.16 = (f32[512,128]{1,0:T(8,128)S(1)}, f32[512,128]{1,0:T(8,128)S(1)}, u32[]{:S(2)}, u32[]{:S(2)}) collective-permute-start(f32[512,128]{1,0:T(8,128)S(1)} %get-tuple-element.41), channel_id=1, source_target_pairs={{8,0},{16,24},{9,1},{17,25},{10,2},{18,26},{11,3},{19,27},{12,4},{... | collective-permute-start | bytes 786440 | tf_op jit(solution)/shard_map/ppermute | solution.py:338
  46.7 3.1 %shard_map.63 = f32[256,128]{1,0:T(8,128)S(1)} custom-call(s32[8,8]{1,0:T(8,128)S(1)} %copy-done.1, bf16[512,1024]{1,0:T(8,128)(2,1)S(1)} %shard_map.59.prow, bf16[512,1024]{1,0:T(8,128)(2,1)S(1)} %get-tuple-element.37.hrow, bf16[1024,256]{1,0:T(8,128)(2,1)S(1)} %get-tuple-element.38.pcol, f32[8,256,128]{2,1,0:T(8,128)S(1)} %collective-permute-done.7.so, ...), custom_call_target="tpu_custom_call" | custom-call | flops 1610612736 | bytes 6422784 | tf_op jit(solution)/shard_map/pallas_call | solution.py:263
  49.8 6.8 %collective-permute-done.16 = f32[512,128]{1,0:T(8,128)S(1)} collective-permute-done((f32[512,128]{1,0:T(8,128)S(1)}, f32[512,128]{1,0:T(8,128)S(1)}, u32[]{:S(2)}, u32[]{:S(2)}) %collective-permute-start.16) | collective-permute-done | bytes 262176 | tf_op jit(solution)/shard_map/ppermute | solution.py:338
  56.6 0.7 %slice_add_fusion = (f32[256,128]{1,0:T(8,128)}, f32[256,128]{1,0:T(8,128)}) fusion(f32[256,128]{1,0:T(8,128)S(1)} %shard_map.63, f32[512,128]{1,0:T(8,128)S(1)} %collective-permute-done.16, f32[256,128]{1,0:T(8,128)S(1)} %get-tuple-element.32.php_ref), kind=kLoop, calls=%fused_computation.14 | loop fusion | flops 65536 | bytes 786432 | tf_op jit(solution)/shard_map/add | solution.py:343
  (16 shorter events, 0.3 us)
Async XLA Ops:
  0.6 10.0 %collective-permute-start.5 = (f32[256,128]{1,0:T(8,128)}, f32[256,128]{1,0:T(8,128)S(1)}, u32[]{:S(2)}, u32[]{:S(2)}) collective-permute-start(f32[256,128]{1,0:T(8,128)} %param.3), channel_id=1, source_target_pairs={{0,4},{1,5},{2,6},{3,7},{4,0},{5,1},{6,2},{7,3},{8,12},{9,13},{10,... | collective-permute-start | bytes 393224 | tf_op jit(solution)/shard_map/ppermute | solution.py:59
  3.7 7.6 %collective-permute-start = (f32[256,128]{1,0:T(8,128)}, f32[256,128]{1,0:T(8,128)S(1)}, u32[]{:S(2)}, u32[]{:S(2)}) collective-permute-start(f32[256,128]{1,0:T(8,128)} %param.4), channel_id=1, source_target_pairs={{0,2},{1,3},{2,0},{3,1},{4,6},{5,7},{6,4},{7,5},{8,10},{9,11},{10,... | collective-permute-start | bytes 393224 | tf_op jit(solution)/shard_map/ppermute | solution.py:59
  6.2 8.3 %collective-permute-start.3 = (f32[256,128]{1,0:T(8,128)S(1)}, f32[256,128]{1,0:T(8,128)S(1)}, u32[]{:S(2)}, u32[]{:S(2)}) collective-permute-start(f32[256,128]{1,0:T(8,128)S(1)} %get-tuple-element.52.p0), channel_id=1, source_target_pairs={{0,24},{8,16},{16,8},{24,0},{1,25},{9,17},{17,9},{25,1},{2,26},{10... | collective-permute-start | bytes 393224 | tf_op jit(solution)/shard_map/ppermute | solution.py:59
  9.8 10.5 %collective-permute-start.2 = (f32[256,128]{1,0:T(8,128)S(1)}, f32[256,128]{1,0:T(8,128)S(1)}, u32[]{:S(2)}, u32[]{:S(2)}) collective-permute-start(f32[256,128]{1,0:T(8,128)S(1)} %get-tuple-element.52.p0), channel_id=1, source_target_pairs={{0,16},{8,24},{16,0},{24,8},{1,17},{9,25},{17,1},{25,9},{2,18},{10... | collective-permute-start | bytes 393224 | tf_op jit(solution)/shard_map/ppermute | solution.py:59
  9.8 10.5 %collective-permute-start.1 = (f32[256,128]{1,0:T(8,128)S(1)}, f32[256,128]{1,0:T(8,128)S(1)}, u32[]{:S(2)}, u32[]{:S(2)}) collective-permute-start(f32[256,128]{1,0:T(8,128)S(1)} %get-tuple-element.52.p0), channel_id=1, source_target_pairs={{0,8},{8,0},{16,24},{24,16},{1,9},{9,1},{17,25},{25,17},{2,10},{10... | collective-permute-start | bytes 393224 | tf_op jit(solution)/shard_map/ppermute | solution.py:59
  10.6 9.7 %collective-permute-start.6 = (f32[512,128]{1,0:T(8,128)S(1)}, f32[512,128]{1,0:T(8,128)S(1)}, u32[]{:S(2)}, u32[]{:S(2)}) collective-permute-start(f32[512,128]{1,0:T(8,128)S(1)} %pad_maximum_fusion.7), channel_id=1, source_target_pairs={{0,2},{1,3},{2,0},{3,1},{4,6},{5,7},{6,4},{7,5},{8,10},{9,11},{10,... | collective-permute-start | bytes 786440 | tf_op jit(solution)/shard_map/ppermute | solution.py:59
  11.3 11.9 %copy-start.1 = (s32[8,8]{1,0:T(8,128)S(1)}, s32[8,8]{1,0:T(8,128)}, u32[]{:S(2)}) copy-start(s32[8,8]{1,0:T(8,128)} %mask_ref.11) | copy-start | bytes 772
  11.3 9.1 %collective-permute-start.4 = (f32[512,128]{1,0:T(8,128)S(1)}, f32[512,128]{1,0:T(8,128)S(1)}, u32[]{:S(2)}, u32[]{:S(2)}) collective-permute-start(f32[512,128]{1,0:T(8,128)S(1)} %pad_maximum_fusion.6), channel_id=1, source_target_pairs={{0,4},{1,5},{2,6},{3,7},{4,0},{5,1},{6,2},{7,3},{8,12},{9,13},{10,... | collective-permute-start | bytes 786440 | tf_op jit(solution)/shard_map/ppermute | solution.py:59
  20.5 2.7 %collective-permute-start.7 = (f32[8,256,128]{2,1,0:T(8,128)S(1)}, f32[8,256,128]{2,1,0:T(8,128)S(1)}, u32[]{:S(2)}, u32[]{:S(2)}) collective-permute-start(f32[8,256,128]{2,1,0:T(8,128)S(1)} %bitcast_dynamic-update-slice_fusion.ss), channel_id=1, source_target_pairs={{0,1},{1,0},{2,3},{3,2},{4,5},{5,4},{6,7},{7,6},{8,9},{9,8},{10,11... | collective-permute-start | bytes 3145736 | tf_op jit(solution)/shard_map/ppermute | solution.py:59
  20.6 7.5 %collective-permute-start.10 = (f32[384,128]{1,0:T(8,128)S(1)}, f32[384,128]{1,0:T(8,128)S(1)}, u32[]{:S(2)}, u32[]{:S(2)}) collective-permute-start(f32[384,128]{1,0:T(8,128)S(1)} %get-tuple-element.56), channel_id=1, source_target_pairs={{0,4},{1,5},{2,6},{3,7},{4,0},{5,1},{6,2},{7,3},{8,12},{9,13},{10,... | collective-permute-start | bytes 589832 | tf_op jit(solution)/shard_map/ppermute | solution.py:59
  21.2 7.0 %collective-permute-start.8 = (f32[384,128]{1,0:T(8,128)S(1)}, f32[384,128]{1,0:T(8,128)S(1)}, u32[]{:S(2)}, u32[]{:S(2)}) collective-permute-start(f32[384,128]{1,0:T(8,128)S(1)} %get-tuple-element.57), channel_id=1, source_target_pairs={{0,2},{1,3},{2,0},{3,1},{4,6},{5,7},{6,4},{7,5},{8,10},{9,11},{10,... | collective-permute-start | bytes 589832 | tf_op jit(solution)/shard_map/ppermute | solution.py:59
  25.4 9.2 %collective-permute-start.14 = (f32[512,128]{1,0:T(8,128)S(1)}, f32[512,128]{1,0:T(8,128)S(1)}, u32[]{:S(2)}, u32[]{:S(2)}) collective-permute-start(f32[512,128]{1,0:T(8,128)S(1)} %get-tuple-element.30.q0), channel_id=1, source_target_pairs={{0,16},{24,8},{8,0},{16,24},{1,17},{25,9},{9,1},{17,25},{2,18},{26... | collective-permute-start | bytes 786440 | tf_op jit(solution)/shard_map/ppermute | solution.py:280
  25.6 13.8 %collective-permute-start.13 = (f32[512,128]{1,0:T(8,128)S(1)}, f32[512,128]{1,0:T(8,128)S(1)}, u32[]{:S(2)}, u32[]{:S(2)}) collective-permute-start(f32[512,128]{1,0:T(8,128)S(1)} %get-tuple-element.30.q0), channel_id=1, source_target_pairs={{0,8},{24,16},{8,0},{16,24},{1,9},{25,17},{9,1},{17,25},{2,10},{26... | collective-permute-start | bytes 786440 | tf_op jit(solution)/shard_map/ppermute | solution.py:280
  27.4 11.9 %collective-permute-start.12 = (f32[512,128]{1,0:T(8,128)S(1)}, f32[512,128]{1,0:T(8,128)S(1)}, u32[]{:S(2)}, u32[]{:S(2)}) collective-permute-start(f32[512,128]{1,0:T(8,128)S(1)} %get-tuple-element.30.q0), channel_id=1, source_target_pairs={{8,16},{16,8},{0,0},{24,24},{9,17},{17,9},{1,1},{25,25},{10,18},{1... | collective-permute-start | bytes 786440 | tf_op jit(solution)/shard_map/ppermute | solution.py:280
  28.3 12.2 %collective-permute-start.11 = (f32[768,128]{1,0:T(8,128)S(1)}, f32[768,128]{1,0:T(8,128)S(1)}, u32[]{:S(2)}, u32[]{:S(2)}) collective-permute-start(f32[768,128]{1,0:T(8,128)S(1)} %get-tuple-element.54), channel_id=1, source_target_pairs={{0,2},{1,3},{2,0},{3,1},{4,6},{5,7},{6,4},{7,5},{8,10},{9,11},{10,... | collective-permute-start | bytes 1179656 | tf_op jit(solution)/shard_map/ppermute | solution.py:59
  28.9 11.6 %collective-permute-start.9 = (f32[768,128]{1,0:T(8,128)S(1)}, f32[768,128]{1,0:T(8,128)S(1)}, u32[]{:S(2)}, u32[]{:S(2)}) collective-permute-start(f32[768,128]{1,0:T(8,128)S(1)} %get-tuple-element.55), channel_id=1, source_target_pairs={{0,4},{1,5},{2,6},{3,7},{4,0},{5,1},{6,2},{7,3},{8,12},{9,13},{10,... | collective-permute-start | bytes 1179656 | tf_op jit(solution)/shard_map/ppermute | solution.py:59
  40.8 3.9 %collective-permute-start.15 = (f32[4,768,128]{2,1,0:T(8,128)S(1)}, f32[4,768,128]{2,1,0:T(8,128)S(1)}, u32[]{:S(2)}, u32[]{:S(2)}) collective-permute-start(f32[4,768,128]{2,1,0:T(8,128)S(1)} %pad_maximum_fusion.b_s), channel_id=1, source_target_pairs={{0,1},{1,0},{2,3},{3,2},{4,5},{5,4},{6,7},{7,6},{8,9},{9,8},{10,11... | collective-permute-start | bytes 4718600 | tf_op jit(solution)/shard_map/ppermute | solution.py:59
  44.7 2.0 %copy-start = (f32[256,128]{1,0:T(8,128)S(1)}, f32[256,128]{1,0:T(8,128)}, u32[]{:S(2)}) copy-start(f32[256,128]{1,0:T(8,128)} %get-tuple-element.21.hp_ref) | copy-start | bytes 393220
  45.4 11.2 %collective-permute-start.16 = (f32[512,128]{1,0:T(8,128)S(1)}, f32[512,128]{1,0:T(8,128)S(1)}, u32[]{:S(2)}, u32[]{:S(2)}) collective-permute-start(f32[512,128]{1,0:T(8,128)S(1)} %get-tuple-element.41), channel_id=1, source_target_pairs={{8,0},{16,24},{9,1},{17,25},{10,2},{18,26},{11,3},{19,27},{12,4},{... | collective-permute-start | bytes 786440 | tf_op jit(solution)/shard_map/ppermute | solution.py:338

commit v3 on v2

--- a/solution.py
+++ b/solution.py
@@ -141,19 +141,42 @@
         out[m * BAND : (m + 1) * BAND, :] = beside(kept)
 
 
-def hp_kernel(mask_ref, ss, so, p0, p1, p2, p3, hp_ref, send_ref, hrow, pcol):
-    r, c = lax.axis_index("row"), lax.axis_index("col")
+def left_pair(mask_ref, r, blocks, first, at):
+    parts = [
+        first[at + i] * pattern_of(mask_ref, band_blocks(r, 0), [blocks[i]]) for i in (0, 1)
+    ]
+    return stacked(jnp.concatenate(parts, axis=1))
+
+
+def pairs(c, flip):
+    for j in (0, 2):
+        yield j, [jnp.bitwise_xor(c, 2 * (j + i) + flip) for i in (0, 1)]
+
+
+def start_kernel(mask_ref, p0, p1, p2, p3, ss, part_ref, pcol):
+    r, c = lax.axis_index("row"), lax.axis_index("col")
+    fill_cols(mask_ref, r, c, (p0[...], p1[...], p2[...], p3[...]), pcol)
+    total = jnp.zeros(part_ref.shape, jnp.float32)
+    for j, blocks in pairs(c, 0):
+        total += dot_parts(left_pair(mask_ref, r, blocks, ss, j), rows_at(r, pcol, blocks))
+    part_ref[...] = total
+
+
+def hp_kernel(mask_ref, part_ref, pcol, ss, so, send_ref, mark_ref):
+    r, c = lax.axis_index("row"), lax.axis_index("col")
+    total = part_ref[...]
+    for j, blocks in pairs(c, 1):
+        total += dot_parts(left_pair(mask_ref, r, blocks, so, j), rows_at(r, pcol, blocks))
+    own = pattern_of(mask_ref, band_blocks(r, 0), [c])
+    send_ref[0:BAND] = total * own
+    send_ref[BAND:] = ss[0] * own
+    mark_ref[...] = jnp.zeros_like(mark_ref)
+
+
+def rows_kernel(mask_ref, ss, so, send_ref, mark_ref, hrow, prow, hp_ref):
+    r, c = lax.axis_index("row"), lax.axis_index("col")
+    hp_ref[...] = send_ref[0:BAND]
     fill_rows(mask_ref, r, c, ss, so, 0, hrow)
-    fill_cols(mask_ref, r, c, (p0[...], p1[...], p2[...], p3[...]), pcol)
-    own = pattern_of(mask_ref, band_blocks(r, 0), [c])
-    tile = dot_parts(hrow[...], pcol[...]) * own
-    hp_ref[...] = tile
-    send_ref[0:BAND] = tile
-    send_ref[BAND:] = ss[0] * own
-
-
-def rows_kernel(mask_ref, ss, so, prow):
-    r, c = lax.axis_index("row"), lax.axis_index("col")
     fill_rows(mask_ref, r, c, ss, so, 4, prow)
 
 
@@ -161,59 +184,78 @@
     return jnp.logical_or(r == 1, r == 2)
 
 
-def column_pairs(mask_ref, r, c, flip, first, rest):
-    for j in (0, 2):
-        blocks = [jnp.bitwise_xor(c, 2 * (j + i) + flip) for i in (0, 1)]
-        bands = []
-        for m in range(4):
-            parts = []
-            for i in (0, 1):
-                if m == 0:
-                    part = first[4 + j + i]
-                else:
-                    part = rest[j + i, (m - 1) * BAND : m * BAND]
-                parts.append(part * pattern_of(mask_ref, band_blocks(r, m), [blocks[i]]))
-            bands.append(jnp.concatenate(parts, axis=1))
-        yield blocks, split(jnp.concatenate(bands, axis=0))
+def tile_of(mask_ref, r, block, j, m, first, rest):
+    part = first[4 + j] if m == 0 else rest[j % 2, (m - 1) * BAND : m * BAND]
+    return part * pattern_of(mask_ref, band_blocks(r, m), [block])
+
+
+def meets(mask_ref, r, m, block):
+    return sum(mask_ref[i, block] for i in band_blocks(r, m)) != 0
+
+
+def block_of(c, j, flip):
+    return jnp.bitwise_xor(c, 2 * j + flip)
 
 
 def rows_at(r, ref, blocks):
     return jnp.concatenate([ref[pl.ds(place(r, b), BLK), :] for b in blocks], axis=0)
 
 
-def hpp_term(mask_ref, r, hrow, pcol, blocks, cols):
-    hp_rows = dot_wide(hrow[...], cols)
-    hp_rows = hp_rows * pattern_of(mask_ref, band_blocks(r, 0), blocks)
-    return dot_parts(stacked(hp_rows), rows_at(r, pcol, blocks))
-
-
-def far_rows(cols):
-    return jnp.concatenate([part[BAND : 2 * BAND] for part in cols], axis=0)
-
-
-def php_kernel(mask_ref, prow, q3, q1, q2, q0, php_ref, qcol, hcol):
+def php_kernel(mask_ref, prow, q3, q1, q2, q0, php_ref, hcol, across_ref, qcol):
     r, c = lax.axis_index("row"), lax.axis_index("col")
     for m, ref in enumerate((q0, q1, q2, q3)):
         qcol[m * BAND : (m + 1) * BAND, :] = beside(ref[0:BAND])
         fill = ref[BAND:] * pattern_of(mask_ref, band_blocks(r, m), [c])
         hcol[m * BAND : (m + 1) * BAND, :] = beside(fill)
     own = pattern_of(mask_ref, band_blocks(r, 0), [c])
-    php_ref[...] = dot_parts(prow[...], qcol[...]) * (own * is_middle(r).astype(jnp.float32))
-
-
-def own_kernel(mask_ref, hrow, hcol, pcol, ss, b_s, ph_ref, hpp_ref, far):
-    r, c = lax.axis_index("row"), lax.axis_index("col")
-    ph = jnp.zeros(ph_ref.shape, jnp.float32)
-    hpp = jnp.zeros(hpp_ref.shape, jnp.float32)
-    for n, (blocks, cols) in enumerate(column_pairs(mask_ref, r, c, 0, ss, b_s)):
-        ph += dot_tall(cols, rows_at(r, hcol, blocks))
-        far[:, n * BAND : (n + 1) * BAND] = far_rows(cols)
-        hpp += hpp_term(mask_ref, r, hrow, pcol, blocks, cols)
-    ph_ref[...] = ph
-    hpp_ref[...] = hpp
-
-
-def ph_kernel(mask_ref, hcol, qcol, so, b_o, part_ref, far, back_ref, tile_ref, ph2):
+    php_ref[...] = dot_parts(prow[...], qcol[...]) * own
+    across_ref[0:BAND] = q3[0:BAND]
+    across_ref[BAND:] = q2[0:BAND]
+
+
+def add_ph(mask_ref, r, c, flip, j, first, rest, hcol, ph_ref, far, slot):
+    block = block_of(c, j, flip)
+
+    @pl.when(mask_ref[block, c] != 0)
+    def _():
+        right = rows_at(r, hcol, [block])
+        for m in range(4):
+            at = pl.ds(m * BAND, BAND)
+            if m == 1:
+                left = stacked(tile_of(mask_ref, r, block, j, m, first, rest))
+                far[:, slot * BLK : (slot + 1) * BLK] = left
+                ph_ref[at, :] += dot_parts(left, right)
+                continue
+
+            @pl.when(jnp.logical_and(meets(mask_ref, r, m, block), meets(mask_ref, r, m, c)))
+            def _(m=m, at=at):
+                left = stacked(tile_of(mask_ref, r, block, j, m, first, rest))
+                ph_ref[at, :] += dot_parts(left, right)
+
+
+def own_kernel(mask_ref, hcol, ss, lo, hi, ph_ref, far):
+    r, c = lax.axis_index("row"), lax.axis_index("col")
+
+    @pl.when(is_middle(r))
+    def _():
+        ph_ref[...] = jnp.zeros_like(ph_ref)
+        for j in range(4):
+            add_ph(mask_ref, r, c, 0, j, ss, (lo, hi)[j // 2], hcol, ph_ref, far, j)
+
+
+def other_kernel(mask_ref, hcol, so, hi, part_ref, ph_ref, far):
+    r, c = lax.axis_index("row"), lax.axis_index("col")
+
+    @pl.when(is_middle(r))
+    def _():
+        ph_ref[...] = part_ref[...]
+        for j in (2, 3):
+            add_ph(mask_ref, r, c, 1, j, so, hi, hcol, ph_ref, far, j - 2)
+
+
+def ph_kernel(
+    mask_ref, hcol, so, lo, part_ref, far_own, far_hi, back_ref, tile_ref, ph2, ph_ref, far_lo
+):
     r, c = lax.axis_index("row"), lax.axis_index("col")
     back_ref[...] = jnp.zeros_like(back_ref)
     tile_ref[...] = jnp.zeros_like(tile_ref)
@@ -221,40 +263,70 @@
 
     @pl.when(is_middle(r))
     def _():
-        ph = part_ref[...]
-        terms = []
-        for j in (0, 2):
-            blocks = [jnp.bitwise_xor(c, 2 * (j + i)) for i in (0, 1)]
-            terms.append((blocks, far[:, (j // 2) * BAND : (j // 2 + 1) * BAND]))
-        for blocks, cols in column_pairs(mask_ref, r, c, 1, so, b_o):
-            ph += dot_tall(cols, rows_at(r, hcol, blocks))
-            terms.append((blocks, far_rows(cols)))
+        ph_ref[...] = part_ref[...]
+        for j in (0, 1):
+            add_ph(mask_ref, r, c, 1, j, so, lo, hcol, ph_ref, far_lo, j)
         for m in range(4):
-            rows = ph[m * BAND : (m + 1) * BAND] * pattern_of(mask_ref, band_blocks(r, m), [c])
-            ph2[m * BAND : (m + 1) * BAND, :] = beside(rows)
+            at = pl.ds(m * BAND, BAND)
+            rows = ph_ref[at, :] * pattern_of(mask_ref, band_blocks(r, m), [c])
+            ph2[at, :] = beside(rows)
             if m == 0:
                 tile_ref[...] = rows
             if m == 1:
-                beyond = rows
-        pph = jnp.zeros(tile_ref.shape, jnp.float32)
-        php = jnp.zeros(tile_ref.shape, jnp.float32)
-        for blocks, left in terms:
-            pph += dot_parts(left, rows_at(r, ph2, blocks))
-            php += dot_parts(left, rows_at(r, qcol, blocks))
+                back_ref[...] = 3.0 * rows
         there = pattern_of(mask_ref, band_blocks(r, 1), [c])
-        back_ref[0:BAND] = there * (3.0 * beyond - 2.0 * (pph + php))
-        back_ref[BAND:] = there * php
+        for flip, far, j, slot in (
+            *((0, far_own, j, j) for j in range(4)),
+            *((1, far_lo, j, j) for j in (0, 1)),
+            *((1, far_hi, j, j - 2) for j in (2, 3)),
+        ):
+            block = block_of(c, j, flip)
+
+            @pl.when(mask_ref[block, c] != 0)
+            def _(far=far, slot=slot, block=block):
+                left = far[:, slot * BLK : (slot + 1) * BLK]
+                back_ref[...] -= 2.0 * there * dot_parts(left, rows_at(r, ph2, [block]))
 
 
 def last_kernel(
-    mask_ref, prow, hrow, pcol, so, b_o, ph2, hp_ref, ph_ref, hpp_ref, php_ref, grad_ref
+    mask_ref, prow, hrow, pcol, ss, so, s_lo, s_hi, o_lo, o_hi, ph2, send_ref, q1, q23,
+    ph_ref, part_ref, php_ref, grad_ref, qcol, acc, row_acc,
 ):
     r, c = lax.axis_index("row"), lax.axis_index("col")
-    second = hpp_ref[...] + dot_parts(prow[...], ph2[...])
-    for blocks, cols in column_pairs(mask_ref, r, c, 1, so, b_o):
-        second += hpp_term(mask_ref, r, hrow, pcol, blocks, cols)
     own = pattern_of(mask_ref, band_blocks(r, 0), [c])
-    grad_ref[...] = 3.0 * (hp_ref[...] + ph_ref[...]) - 2.0 * (php_ref[...] + own * second)
+    hp = send_ref[0:BAND]
+
+    @pl.when(is_middle(r))
+    def _():
+        php_ref[...] = part_ref[...]
+        acc[...] = dot_parts(prow[...], ph2[...])
+
+    @pl.when(jnp.logical_not(is_middle(r)))
+    def _():
+        for m, part in enumerate((hp, q1[0:BAND], q23[0:BAND], q23[BAND:])):
+            qcol[m * BAND : (m + 1) * BAND, :] = beside(part)
+        php_ref[...] = dot_parts(prow[...], qcol[...]) * own
+        acc[...] = jnp.zeros_like(acc)
+
+    acc[...] += dot_parts(stacked(hp), rows_at(r, pcol, [c]))
+    for flip, first, rests in ((0, ss, (s_lo, s_hi)), (1, so, (o_lo, o_hi))):
+        for j in range(1 - flip, 4):
+            block = block_of(c, j, flip)
+
+            @pl.when(mask_ref[block, c] != 0)
+            def _(first=first, rest=rests[j // 2], j=j, block=block):
+                row_acc[...] = jnp.zeros_like(row_acc)
+                for m in range(4):
+
+                    @pl.when(meets(mask_ref, r, m, block))
+                    def _(m=m):
+                        right = beside(tile_of(mask_ref, r, block, j, m, first, rest))
+                        row_acc[...] += dot_parts(hrow[:, m * BAND : (m + 1) * BAND], right)
+
+                rows = row_acc[...] * pattern_of(mask_ref, band_blocks(r, 0), [block])
+                acc[...] += dot_parts(stacked(rows), rows_at(r, pcol, [block]))
+
+    grad_ref[...] = 3.0 * (hp + ph_ref[...]) - 2.0 * (php_ref[...] + own * acc[...])
 
 
 def call(kernel, outs, scratch, flops, *args):
@@ -293,9 +365,10 @@
     weight = 6 * rows * order * order
     p0, h0 = density, hamiltonian
     hx, py = swap(h0, "col", 2), swap(p0, "col", 4)
+    p3 = swap(p0, "row", 3)
     both = lax.optimization_barrier(jnp.concatenate([p0, h0], axis=0))
     p0, h0 = both[:rows], both[rows:]
-    p1, p2, p3 = [swap(p0, "row", m) for m in (1, 2, 3)]
+    p1, p2 = swap(p0, "row", 1), swap(p0, "row", 2)
     hy = swap(jnp.concatenate([h0, hx], axis=0), "col", 4)
     px = swap(jnp.concatenate([p0, py], axis=0), "col", 2)
     p1, p2, p3, hy, px = lax.optimization_barrier((p1, p2, p3, hy, px))
@@ -307,40 +380,48 @@
     upper, lower = b[:half], b[half:]
     ux, ly = swap(upper, "col", 2), swap(lower, "col", 4)
 
-    hp, send, hrow, pcol = call(
-        hp_kernel, (tile, shape(2 * rows, cols, f32), rows2, cols2), [], weight,
-        block_mask, ss, so, p0, p1, p2, p3,
-    )
+    part, pcol = call(start_kernel, (tile, cols2), [], weight, block_mask, p0, p1, p2, p3, ss)
+    send, mark = call(
+        hp_kernel, (shape(2 * rows, cols, f32), shape(8, cols, f32)), [], weight,
+        block_mask, part, pcol, ss, so,
+    )
+    ux, ly, mark = lax.optimization_barrier((ux, ly, mark))
     q1, q2, q3 = to_middle(send)
     uy = swap(jnp.concatenate([upper, ux], axis=0), "col", 4)
     lx = swap(jnp.concatenate([lower, ly], axis=0), "col", 2)
-    (prow,) = call(rows_kernel, (rows2,), [], weight, block_mask, ss, so)
-    php, qcol, hcol = call(
-        php_kernel, (tile, cols2, cols2), [], AHEAD * weight, block_mask, prow, q3, q1, q2, send
-    )
+    hrow, prow, hp = call(
+        rows_kernel, (rows2, rows2, tile), [], weight, block_mask, ss, so, send, mark
+    )
+    php, hcol, across = call(
+        php_kernel, (tile, cols2, shape(2 * rows, cols, f32)),
+        [pltpu.VMEM((order, 2 * cols), bf16)], AHEAD * weight,
+        block_mask, prow, q3, q1, q2, send,
+    )
+    q23 = swap(across, "row", 1)
     uy, lx, php = lax.optimization_barrier((uy, lx, php))
-    b_s = jnp.stack(
-        [
-            jnp.concatenate(pair, axis=0)
-            for pair in ((upper, lower), (ux, lx[:half]), (uy[:half], ly), (uy[half:], lx[half:]))
-        ]
-    )
-    b_o = swap(b_s, "col", 1)
-
-    part, hpp, far = call(
-        own_kernel, (strip, tile, shape(2 * rows, order // 2)), [], weight,
-        block_mask, hrow, hcol, pcol, ss, b_s,
+    s_lo = jnp.stack([b, jnp.concatenate([ux, lx[:half]], axis=0)])
+    s_hi = jnp.stack([jnp.concatenate(pair, axis=0) for pair in ((uy[:half], ly), (uy[half:], lx[half:]))])
+    o_lo, o_hi = swap(s_lo, "col", 1), swap(s_hi, "col", 1)
+
+    half_far, quarter_far = shape(2 * rows, order // 2), shape(2 * rows, order // 4)
+    strip_acc = pltpu.VMEM((order, cols), f32)
+    part, far_own = call(
+        own_kernel, (strip, half_far), [], AHEAD * weight, block_mask, hcol, ss, s_lo, s_hi
+    )
+    part, far_hi = call(
+        other_kernel, (strip, quarter_far), [], weight, block_mask, hcol, so, o_hi, part
     )
     back, ph, ph2 = call(
-        ph_kernel, (shape(2 * rows, cols, f32), tile, cols2), [], weight,
-        block_mask, hcol, qcol, so, b_o, part, far,
+        ph_kernel, (tile, tile, cols2), [strip_acc, pltpu.VMEM((2 * rows, order // 4), bf16)],
+        weight, block_mask, hcol, so, o_lo, part, far_own, far_hi,
     )
     got = lax.ppermute(back, "row", [(1, 0), (2, 3)])
-    (grad,) = call(
-        last_kernel, (tile,), [], weight,
-        block_mask, prow, hrow, pcol, so, b_o, ph2, hp, ph, hpp, php,
-    )
-    return hp, php + got[rows:], grad + got[:rows]
+    php, grad = call(
+        last_kernel, (tile, tile),
+        [pltpu.VMEM((order, 2 * cols), bf16)] + [pltpu.VMEM((rows, cols), f32)] * 2, weight,
+        block_mask, prow, hrow, pcol, ss, so, s_lo, s_hi, o_lo, o_hi, ph2, send, q1, q23, ph, php,
+    )
+    return hp, php, grad + got
 
 
 def body(density, hamiltonian, block_mask, shape):

time: 57.5 us -> 54.4 us (0.946)
  waiting for transfers between devices: 24.9 us -> 17.3 us
  starting transfers between devices: 17.4 us -> 21.4 us
  Pallas kernels: 11.9 us -> 13 us
    ppermute x1, waiting for transfers between devices: 6.8 us -> 0.74 us  [whole_body(): got = lax.ppermute(back, 'row', [(1, 0), (2, 3)])]
    ppermute x13 -> x15, starting transfers between devices: 13.4 us -> 17.4 us  [swap(): return lax.ppermute(x, axis, [(i, i ^ mask) for i in range(size)])]
    ppermute x3, waiting for transfers between devices: 7.92 us -> 5.53 us  [to_middle(): return [lax.ppermute(x, 'row', pairs) for pairs in routes]]
    pallas_call x6 -> x8, Pallas kernels: 11.9 us -> 13 us  [call(): pl.pallas_call(kernel, out_shape=outs, in_specs=[smem] + [vmem] * (len(ar...]
    ppermute x13 -> x15, waiting for transfers between devices: 10.2 us -> 11 us  [swap(): return lax.ppermute(x, axis, [(i, i ^ mask) for i in range(size)])]
  transfers between devices with their start and end apart: 17 -> 19, of which waited for: 7 -> 11; matrix products, arithmetic and copies ran while one was open for 2% -> 3% of each run, Pallas kernels for 20% -> 24%
where the time goes in v3:
time: 54.4 us; the launch traced here: 54.8 us
  starting transfers between devices  21.4 us (39%)
  waiting for transfers between devices  17.3 us (32%)
  Pallas kernels  13 us (24%)
  other arithmetic  2 us (4%)
  between operations  0.91 us (2%)
    ppermute x15, starting transfers between devices, swap(): return lax.ppermute(x, axis, [(i, i ^ mask) for i in range(size)])  17.4 us
    pallas_call x8, Pallas kernels, call(): pl.pallas_call(kernel, out_shape=outs, in_specs=[smem] + [vmem] * (len(ar...  13 us
    ppermute x15, waiting for transfers between devices, swap(): return lax.ppermute(x, axis, [(i, i ^ mask) for i in range(size)])  11 us
    ppermute x3, waiting for transfers between devices, to_middle(): return [lax.ppermute(x, 'row', pairs) for pairs in routes]  5.53 us
    ppermute x3, starting transfers between devices, to_middle(): return [lax.ppermute(x, 'row', pairs) for pairs in routes]  2.74 us
    ppermute x1, starting transfers between devices, whole_body(): got = lax.ppermute(back, 'row', [(1, 0), (2, 3)])  1.29 us
  transfers between devices with their start and end apart: 19, of which 11 were waited for; matrix products, arithmetic and copies ran while one was open for 3% of the time, Pallas kernels for 24%

profile of v3, /device:TPU:0, one launch (start us, length us, event | category | flops | bytes accessed | tf_op | source)
XLA Modules:
  0.0 54.8 jit_solution(8681581771020511223)
XLA Ops:
  0.6 3.0 %collective-permute-start.5 = (f32[256,128]{1,0:T(8,128)}, f32[256,128]{1,0:T(8,128)S(1)}, u32[]{:S(2)}, u32[]{:S(2)}) collective-permute-start(f32[256,128]{1,0:T(8,128)} %param.3), channel_id=1, source_target_pairs={{0,4},{1,5},{2,6},{3,7},{4,0},{5,1},{6,2},{7,3},{8,12},{9,13},{10,... | collective-permute-start | bytes 393224 | tf_op jit(solution)/shard_map/ppermute | solution.py:59
  3.7 3.6 %collective-permute-start.3 = (f32[256,128]{1,0:T(8,128)}, f32[256,128]{1,0:T(8,128)S(1)}, u32[]{:S(2)}, u32[]{:S(2)}) collective-permute-start(f32[256,128]{1,0:T(8,128)} %param.3), channel_id=1, source_target_pairs={{0,24},{8,16},{16,8},{24,0},{1,25},{9,17},{17,9},{25,1},{2,26},{10... | collective-permute-start | bytes 393224 | tf_op jit(solution)/shard_map/ppermute | solution.py:59
  7.3 1.5 %collective-permute-start = (f32[256,128]{1,0:T(8,128)}, f32[256,128]{1,0:T(8,128)S(1)}, u32[]{:S(2)}, u32[]{:S(2)}) collective-permute-start(f32[256,128]{1,0:T(8,128)} %param.4), channel_id=1, source_target_pairs={{0,2},{1,3},{2,0},{3,1},{4,6},{5,7},{6,4},{7,5},{8,10},{9,11},{10,... | collective-permute-start | bytes 393224 | tf_op jit(solution)/shard_map/ppermute | solution.py:59
  8.8 1.0 %pad_maximum_fusion.5 = f32[512,128]{1,0:T(8,128)S(1)} fusion(f32[256,128]{1,0:T(8,128)} %param.4, f32[256,128]{1,0:T(8,128)} %param.3), kind=kLoop, calls=%fused_computation.9 | loop fusion | flops 65536 | bytes 524288 | tf_op jit(solution)/shard_map/concatenate | solution.py:369
  9.8 0.1 collective-permute-start.2
  9.9 0.8 %collective-permute-start.1 = (f32[256,128]{1,0:T(8,128)S(1)}, f32[256,128]{1,0:T(8,128)S(1)}, u32[]{:S(2)}, u32[]{:S(2)}) collective-permute-start(f32[256,128]{1,0:T(8,128)S(1)} %get-tuple-element.68.p0), channel_id=1, source_target_pairs={{0,8},{8,0},{16,24},{24,16},{1,9},{9,1},{17,25},{25,17},{2,10},{10... | collective-permute-start | bytes 393224 | tf_op jit(solution)/shard_map/ppermute | solution.py:59
  10.6 0.0 collective-permute-done.5
  10.6 0.6 %collective-permute-start.6 = (f32[512,128]{1,0:T(8,128)S(1)}, f32[512,128]{1,0:T(8,128)S(1)}, u32[]{:S(2)}, u32[]{:S(2)}) collective-permute-start(f32[512,128]{1,0:T(8,128)S(1)} %pad_maximum_fusion.7), channel_id=1, source_target_pairs={{0,2},{1,3},{2,0},{3,1},{4,6},{5,7},{6,4},{7,5},{8,10},{9,11},{10,... | collective-permute-start | bytes 786440 | tf_op jit(solution)/shard_map/ppermute | solution.py:59
  11.2 1.9 %collective-permute-done = f32[256,128]{1,0:T(8,128)S(1)} collective-permute-done((f32[256,128]{1,0:T(8,128)}, f32[256,128]{1,0:T(8,128)S(1)}, u32[]{:S(2)}, u32[]{:S(2)}) %collective-permute-start) | collective-permute-done | bytes 131104 | tf_op jit(solution)/shard_map/ppermute | solution.py:59
  13.1 0.6 %collective-permute-start.4 = (f32[512,128]{1,0:T(8,128)S(1)}, f32[512,128]{1,0:T(8,128)S(1)}, u32[]{:S(2)}, u32[]{:S(2)}) collective-permute-start(f32[512,128]{1,0:T(8,128)S(1)} %pad_maximum_fusion.6), channel_id=1, source_target_pairs={{0,4},{1,5},{2,6},{3,7},{4,0},{5,1},{6,2},{7,3},{8,12},{9,13},{10,... | collective-permute-start | bytes 786440 | tf_op jit(solution)/shard_map/ppermute | solution.py:59
  13.7 4.5 %collective-permute-done.2.p2 = f32[256,128]{1,0:T(8,128)S(1)} collective-permute-done((f32[256,128]{1,0:T(8,128)S(1)}, f32[256,128]{1,0:T(8,128)S(1)}, u32[]{:S(2)}, u32[]{:S(2)}) %collective-permute-start.2) | collective-permute-done | bytes 131104 | tf_op jit(solution)/shard_map/ppermute | solution.py:59
  18.3 0.0 collective-permute-done.1.p1
  18.3 0.0 collective-permute-done.6
  18.3 1.3 %collective-permute-done.4 = f32[512,128]{1,0:T(8,128)S(1)} collective-permute-done((f32[512,128]{1,0:T(8,128)S(1)}, f32[512,128]{1,0:T(8,128)S(1)}, u32[]{:S(2)}, u32[]{:S(2)}) %collective-permute-start.4) | collective-permute-done | bytes 262176 | tf_op jit(solution)/shard_map/ppermute | solution.py:59
  19.7 0.0 copy-start
  19.7 0.1 collective-permute-start.7
  19.8 0.6 %collective-permute-start.9 = (f32[384,128]{1,0:T(8,128)S(1)}, f32[384,128]{1,0:T(8,128)S(1)}, u32[]{:S(2)}, u32[]{:S(2)}) collective-permute-start(f32[384,128]{1,0:T(8,128)S(1)} %get-tuple-element.69), channel_id=1, source_target_pairs={{0,4},{1,5},{2,6},{3,7},{4,0},{5,1},{6,2},{7,3},{8,12},{9,13},{10,... | collective-permute-start | bytes 589832 | tf_op jit(solution)/shard_map/ppermute | solution.py:59
  20.4 2.2 %collective-permute-start.8 = (f32[384,128]{1,0:T(8,128)S(1)}, f32[384,128]{1,0:T(8,128)S(1)}, u32[]{:S(2)}, u32[]{:S(2)}) collective-permute-start(f32[384,128]{1,0:T(8,128)S(1)} %get-tuple-element.70), channel_id=1, source_target_pairs={{0,2},{1,3},{2,0},{3,1},{4,6},{5,7},{6,4},{7,5},{8,10},{9,11},{10,... | collective-permute-start | bytes 589832 | tf_op jit(solution)/shard_map/ppermute | solution.py:59
  22.6 1.0 %shard_map.58 = (f32[256,128]{1,0:T(8,128)S(1)}, bf16[1024,256]{1,0:T(8,128)(2,1)S(1)}) custom-call(s32[8,8]{1,0:T(8,128)S(1)} %copy-done, f32[256,128]{1,0:T(8,128)S(1)} %get-tuple-element.68.p0, f32[256,128]{1,0:T(8,128)S(1)} %collective-permute-done.1.p1, f32[256,128]{1,0:T(8,128)S(1)} %collective-permute-done.2.p2, ...), custom_call_target="tpu_custom_call" | custom-call | flops 1610612736 | bytes 2228480 | tf_op jit(solution)/shard_map/pallas_call | solution.py:335
  23.7 0.9 %shard_map.59 = (f32[512,128]{1,0:T(8,128)S(1)}, f32[8,128]{1,0:T(8,128)S(1)}) custom-call(s32[8,8]{1,0:T(8,128)S(1)} %copy-done, f32[256,128]{1,0:T(8,128)S(1)} %get-tuple-element.38.part_ref, bf16[1024,256]{1,0:T(8,128)(2,1)S(1)} %get-tuple-element.39.pcol, f32[8,256,128]{2,1,0:T(8,128)S(1)} %bitcast_dynamic-update-slice_fusion.ss, ...), custom_call_target="tpu_custom_call" | custom-call | flops 1610612736 | bytes 3019008 | tf_op jit(solution)/shard_map/pallas_call | solution.py:335
  24.6 0.1 collective-permute-start.14
  24.7 2.0 %collective-permute-start.13 = (f32[512,128]{1,0:T(8,128)S(1)}, f32[512,128]{1,0:T(8,128)S(1)}, u32[]{:S(2)}, u32[]{:S(2)}) collective-permute-start(f32[512,128]{1,0:T(8,128)S(1)} %get-tuple-element.40.send_ref.q0), channel_id=1, source_target_pairs={{0,8},{24,16},{8,0},{16,24},{1,9},{25,17},{9,1},{17,25},{2,10},{26... | collective-permute-start | bytes 786440 | tf_op jit(solution)/shard_map/ppermute | solution.py:352
  26.7 0.7 %collective-permute-start.12 = (f32[512,128]{1,0:T(8,128)S(1)}, f32[512,128]{1,0:T(8,128)S(1)}, u32[]{:S(2)}, u32[]{:S(2)}) collective-permute-start(f32[512,128]{1,0:T(8,128)S(1)} %get-tuple-element.40.send_ref.q0), channel_id=1, source_target_pairs={{8,16},{16,8},{0,0},{24,24},{9,17},{17,9},{1,1},{25,25},{10,18},{1... | collective-permute-start | bytes 786440 | tf_op jit(solution)/shard_map/ppermute | solution.py:352
  27.4 0.5 collective-permute-done.8
  27.9 1.8 %collective-permute-start.11 = (f32[768,128]{1,0:T(8,128)S(1)}, f32[768,128]{1,0:T(8,128)S(1)}, u32[]{:S(2)}, u32[]{:S(2)}) collective-permute-start(f32[768,128]{1,0:T(8,128)S(1)} %pad_maximum_fusion.3), channel_id=1, source_target_pairs={{0,2},{1,3},{2,0},{3,1},{4,6},{5,7},{6,4},{7,5},{8,10},{9,11},{10,... | collective-permute-start | bytes 1179656 | tf_op jit(solution)/shard_map/ppermute | solution.py:59
  29.7 1.6 %collective-permute-start.10 = (f32[768,128]{1,0:T(8,128)S(1)}, f32[768,128]{1,0:T(8,128)S(1)}, u32[]{:S(2)}, u32[]{:S(2)}) collective-permute-start(f32[768,128]{1,0:T(8,128)S(1)} %pad_maximum_fusion.4), channel_id=1, source_target_pairs={{0,4},{1,5},{2,6},{3,7},{4,0},{5,1},{6,2},{7,3},{8,12},{9,13},{10,... | collective-permute-start | bytes 1179656 | tf_op jit(solution)/shard_map/ppermute | solution.py:59
  31.3 1.6 %shard_map.60 = (bf16[512,1024]{1,0:T(8,128)(2,1)S(1)}, bf16[512,1024]{1,0:T(8,128)(2,1)S(1)}, f32[256,128]{1,0:T(8,128)}) custom-call(s32[8,8]{1,0:T(8,128)S(1)} %copy-done, f32[8,256,128]{2,1,0:T(8,128)S(1)} %bitcast_dynamic-update-slice_fusion.ss, f32[8,256,128]{2,1,0:T(8,128)S(1)} %collective-permute-done.7.so, ...), custom_call_target="tpu_custom_call" | custom-call | flops 1610612736 | bytes 4591872 | tf_op jit(solution)/shard_map/pallas_call | solution.py:335
  32.9 1.0 %collective-permute-done.14.q2 = f32[512,128]{1,0:T(8,128)S(1)} collective-permute-done((f32[512,128]{1,0:T(8,128)S(1)}, f32[512,128]{1,0:T(8,128)S(1)}, u32[]{:S(2)}, u32[]{:S(2)}) %collective-permute-start.14) | collective-permute-done | bytes 262176 | tf_op jit(solution)/shard_map/ppermute | solution.py:352
  33.9 4.6 %collective-permute-done.13.q1 = f32[512,128]{1,0:T(8,128)S(1)} collective-permute-done((f32[512,128]{1,0:T(8,128)S(1)}, f32[512,128]{1,0:T(8,128)S(1)}, u32[]{:S(2)}, u32[]{:S(2)}) %collective-permute-start.13) | collective-permute-done | bytes 262176 | tf_op jit(solution)/shard_map/ppermute | solution.py:352
  38.4 0.0 collective-permute-done.12.q3
  38.4 1.1 %shard_map.61 = (f32[256,128]{1,0:T(8,128)S(1)}, bf16[1024,256]{1,0:T(8,128)(2,1)S(1)}, f32[512,128]{1,0:T(8,128)S(1)}) custom-call(s32[8,8]{1,0:T(8,128)S(1)} %copy-done, bf16[512,1024]{1,0:T(8,128)(2,1)S(1)} %get-tuple-element.44.prow, f32[512,128]{1,0:T(8,128)S(1)} %collective-permute-done.12.q3, f32[512,128]{1,0:T(8,128)S(1)} %collective-permute-done.13.q1, ...), custom_call_target="tpu_custom_call" | custom-call | flops 12884901888 | bytes 3014912 | tf_op jit(solution)/shard_map/pallas_call | solution.py:335
  39.5 0.4 collective-permute-start.17
  39.9 0.1 collective-permute-done.10
  40.0 0.1 fusion.1
  40.2 0.1 pad_maximum_fusion.1.hi.s_hi
  40.3 0.1 collective-permute-start.16
  40.3 0.1 pad_maximum_fusion.lo.s_lo
  40.4 0.6 %collective-permute-start.15 = (f32[2,768,128]{2,1,0:T(8,128)S(1)}, f32[2,768,128]{2,1,0:T(8,128)S(1)}, u32[]{:S(2)}, u32[]{:S(2)}) collective-permute-start(f32[2,768,128]{2,1,0:T(8,128)S(1)} %pad_maximum_fusion.lo.s_lo), channel_id=1, source_target_pairs={{0,1},{1,0},{2,3},{3,2},{4,5},{5,4},{6,7},{7,6},{8,9},{9,8},{10,11... | collective-permute-start | bytes 2359304 | tf_op jit(solution)/shard_map/ppermute | solution.py:59
  41.0 0.6 %shard_map.62 = (f32[1024,128]{1,0:T(8,128)S(1)}, bf16[512,512]{1,0:T(8,128)(2,1)S(1)}) custom-call(s32[8,8]{1,0:T(8,128)S(1)} %copy-done, bf16[1024,256]{1,0:T(8,128)(2,1)S(1)} %get-tuple-element.51.hcol, f32[8,256,128]{2,1,0:T(8,128)S(1)} %bitcast_dynamic-update-slice_fusion.ss, f32[2,768,128]{2,1,0:T(8,128)S(1)} %pad_maximum_fusion.lo.s_lo, ...), custom_call_target="tpu_custom_call" | custom-call | flops 12884901888 | bytes 4194560 | tf_op jit(solution)/shard_map/pallas_call | solution.py:335
  41.6 1.0 %collective-permute-done.16.hi.o_hi = f32[2,768,128]{2,1,0:T(8,128)S(1)} collective-permute-done((f32[2,768,128]{2,1,0:T(8,128)S(1)}, f32[2,768,128]{2,1,0:T(8,128)S(1)}, u32[]{:S(2)}, u32[]{:S(2)}) %collective-permute-start.16) | collective-permute-done | bytes 786464 | tf_op jit(solution)/shard_map/ppermute | solution.py:59
  42.6 0.6 %shard_map.63 = (f32[1024,128]{1,0:T(8,128)S(1)}, bf16[512,256]{1,0:T(8,128)(2,1)S(1)}) custom-call(s32[8,8]{1,0:T(8,128)S(1)} %copy-done, bf16[1024,256]{1,0:T(8,128)(2,1)S(1)} %get-tuple-element.51.hcol, f32[8,256,128]{2,1,0:T(8,128)S(1)} %collective-permute-done.7.so, f32[2,768,128]{2,1,0:T(8,128)S(1)} %collective-permute-done.16.hi.o_hi, ...), custom_call_target="tpu_custom_call" | custom-call | flops 1610612736 | bytes 3670272 | tf_op jit(solution)/shard_map/pallas_call | solution.py:335
  43.2 0.5 collective-permute-done.15.lo.o_lo
  43.7 0.7 %shard_map.64 = (f32[256,128]{1,0:T(8,128)S(1)}, f32[256,128]{1,0:T(8,128)S(1)}, bf16[1024,256]{1,0:T(8,128)(2,1)S(1)}) custom-call(s32[8,8]{1,0:T(8,128)S(1)} %copy-done, bf16[1024,256]{1,0:T(8,128)(2,1)S(1)} %get-tuple-element.51.hcol, f32[8,256,128]{2,1,0:T(8,128)S(1)} %collective-permute-done.7.so, f32[2,768,128]{2,1,0:T(8,128)S(1)} %collective-permute-done.15.lo.o_lo, ...), custom_call_target="tpu_custom_call" | custom-call | flops 1610612736 | bytes 4456704 | tf_op jit(solution)/shard_map/pallas_call | solution.py:335
  44.4 1.3 %collective-permute-start.18 = (f32[256,128]{1,0:T(8,128)S(1)}, f32[256,128]{1,0:T(8,128)S(1)}, u32[]{:S(2)}, u32[]{:S(2)}) collective-permute-start(f32[256,128]{1,0:T(8,128)S(1)} %get-tuple-element.62), channel_id=1, source_target_pairs={{8,0},{16,24},{9,1},{17,25},{10,2},{18,26},{11,3},{19,27},{12,4},{... | collective-permute-start | bytes 393224 | tf_op jit(solution)/shard_map/ppermute | solution.py:418
  45.7 1.2 %collective-permute-done.17.q23 = f32[512,128]{1,0:T(8,128)S(1)} collective-permute-done((f32[512,128]{1,0:T(8,128)S(1)}, f32[512,128]{1,0:T(8,128)S(1)}, u32[]{:S(2)}, u32[]{:S(2)}) %collective-permute-start.17) | collective-permute-done | bytes 262176 | tf_op jit(solution)/shard_map/ppermute | solution.py:59
  46.9 6.5 %shard_map.65 = (f32[256,128]{1,0:T(8,128)}, f32[256,128]{1,0:T(8,128)S(1)}) custom-call(s32[8,8]{1,0:T(8,128)S(1)} %copy-done, bf16[512,1024]{1,0:T(8,128)(2,1)S(1)} %get-tuple-element.44.prow, bf16[512,1024]{1,0:T(8,128)(2,1)S(1)} %get-tuple-element.45.hrow, bf16[1024,256]{1,0:T(8,128)(2,1)S(1)} %get-tuple-element.39.pcol, ...), custom_call_target="tpu_custom_call" | custom-call | flops 1610612736 | bytes 9699584 | tf_op jit(solution)/shard_map/pallas_call | solution.py:335
  53.4 0.7 %collective-permute-done.18 = f32[256,128]{1,0:T(8,128)S(1)} collective-permute-done((f32[256,128]{1,0:T(8,128)S(1)}, f32[256,128]{1,0:T(8,128)S(1)}, u32[]{:S(2)}, u32[]{:S(2)}) %collective-permute-start.18) | collective-permute-done | bytes 131104 | tf_op jit(solution)/shard_map/ppermute | solution.py:418
  54.1 0.7 %add.3 = f32[256,128]{1,0:T(8,128)} add(f32[256,128]{1,0:T(8,128)S(1)} %get-tuple-element.61, f32[256,128]{1,0:T(8,128)S(1)} %collective-permute-done.18) | non-fusion elementwise | flops 32768 | bytes 393216 | tf_op jit(solution)/shard_map/add | solution.py:424
  (23 shorter events, 0.4 us)
Async XLA Ops:
  0.6 10.0 %collective-permute-start.5 = (f32[256,128]{1,0:T(8,128)}, f32[256,128]{1,0:T(8,128)S(1)}, u32[]{:S(2)}, u32[]{:S(2)}) collective-permute-start(f32[256,128]{1,0:T(8,128)} %param.3), channel_id=1, source_target_pairs={{0,4},{1,5},{2,6},{3,7},{4,0},{5,1},{6,2},{7,3},{8,12},{9,13},{10,... | collective-permute-start | bytes 393224 | tf_op jit(solution)/shard_map/ppermute | solution.py:59
  3.7 10.1 %collective-permute-start.3 = (f32[256,128]{1,0:T(8,128)}, f32[256,128]{1,0:T(8,128)S(1)}, u32[]{:S(2)}, u32[]{:S(2)}) collective-permute-start(f32[256,128]{1,0:T(8,128)} %param.3), channel_id=1, source_target_pairs={{0,24},{8,16},{16,8},{24,0},{1,25},{9,17},{17,9},{25,1},{2,26},{10... | collective-permute-start | bytes 393224 | tf_op jit(solution)/shard_map/ppermute | solution.py:59
  7.3 5.8 %collective-permute-start = (f32[256,128]{1,0:T(8,128)}, f32[256,128]{1,0:T(8,128)S(1)}, u32[]{:S(2)}, u32[]{:S(2)}) collective-permute-start(f32[256,128]{1,0:T(8,128)} %param.4), channel_id=1, source_target_pairs={{0,2},{1,3},{2,0},{3,1},{4,6},{5,7},{6,4},{7,5},{8,10},{9,11},{10,... | collective-permute-start | bytes 393224 | tf_op jit(solution)/shard_map/ppermute | solution.py:59
  9.8 8.5 %collective-permute-start.2 = (f32[256,128]{1,0:T(8,128)S(1)}, f32[256,128]{1,0:T(8,128)S(1)}, u32[]{:S(2)}, u32[]{:S(2)}) collective-permute-start(f32[256,128]{1,0:T(8,128)S(1)} %get-tuple-element.68.p0), channel_id=1, source_target_pairs={{0,16},{8,24},{16,0},{24,8},{1,17},{9,25},{17,1},{25,9},{2,18},{10... | collective-permute-start | bytes 393224 | tf_op jit(solution)/shard_map/ppermute | solution.py:59
  9.9 8.4 %collective-permute-start.1 = (f32[256,128]{1,0:T(8,128)S(1)}, f32[256,128]{1,0:T(8,128)S(1)}, u32[]{:S(2)}, u32[]{:S(2)}) collective-permute-start(f32[256,128]{1,0:T(8,128)S(1)} %get-tuple-element.68.p0), channel_id=1, source_target_pairs={{0,8},{8,0},{16,24},{24,16},{1,9},{9,1},{17,25},{25,17},{2,10},{10... | collective-permute-start | bytes 393224 | tf_op jit(solution)/shard_map/ppermute | solution.py:59
  10.6 7.6 %collective-permute-start.6 = (f32[512,128]{1,0:T(8,128)S(1)}, f32[512,128]{1,0:T(8,128)S(1)}, u32[]{:S(2)}, u32[]{:S(2)}) collective-permute-start(f32[512,128]{1,0:T(8,128)S(1)} %pad_maximum_fusion.7), channel_id=1, source_target_pairs={{0,2},{1,3},{2,0},{3,1},{4,6},{5,7},{6,4},{7,5},{8,10},{9,11},{10,... | collective-permute-start | bytes 786440 | tf_op jit(solution)/shard_map/ppermute | solution.py:59
  13.1 6.4 %collective-permute-start.4 = (f32[512,128]{1,0:T(8,128)S(1)}, f32[512,128]{1,0:T(8,128)S(1)}, u32[]{:S(2)}, u32[]{:S(2)}) collective-permute-start(f32[512,128]{1,0:T(8,128)S(1)} %pad_maximum_fusion.6), channel_id=1, source_target_pairs={{0,4},{1,5},{2,6},{3,7},{4,0},{5,1},{6,2},{7,3},{8,12},{9,13},{10,... | collective-permute-start | bytes 786440 | tf_op jit(solution)/shard_map/ppermute | solution.py:59
  19.7 2.9 %copy-start = (s32[8,8]{1,0:T(8,128)S(1)}, s32[8,8]{1,0:T(8,128)}, u32[]{:S(2)}) copy-start(s32[8,8]{1,0:T(8,128)} %mask_ref.15) | copy-start | bytes 772
  19.7 4.0 %collective-permute-start.7 = (f32[8,256,128]{2,1,0:T(8,128)S(1)}, f32[8,256,128]{2,1,0:T(8,128)S(1)}, u32[]{:S(2)}, u32[]{:S(2)}) collective-permute-start(f32[8,256,128]{2,1,0:T(8,128)S(1)} %bitcast_dynamic-update-slice_fusion.ss), channel_id=1, source_target_pairs={{0,1},{1,0},{2,3},{3,2},{4,5},{5,4},{6,7},{7,6},{8,9},{9,8},{10,11... | collective-permute-start | bytes 3145736 | tf_op jit(solution)/shard_map/ppermute | solution.py:59
  19.8 7.6 %collective-permute-start.9 = (f32[384,128]{1,0:T(8,128)S(1)}, f32[384,128]{1,0:T(8,128)S(1)}, u32[]{:S(2)}, u32[]{:S(2)}) collective-permute-start(f32[384,128]{1,0:T(8,128)S(1)} %get-tuple-element.69), channel_id=1, source_target_pairs={{0,4},{1,5},{2,6},{3,7},{4,0},{5,1},{6,2},{7,3},{8,12},{9,13},{10,... | collective-permute-start | bytes 589832 | tf_op jit(solution)/shard_map/ppermute | solution.py:59
  20.4 7.5 %collective-permute-start.8 = (f32[384,128]{1,0:T(8,128)S(1)}, f32[384,128]{1,0:T(8,128)S(1)}, u32[]{:S(2)}, u32[]{:S(2)}) collective-permute-start(f32[384,128]{1,0:T(8,128)S(1)} %get-tuple-element.70), channel_id=1, source_target_pairs={{0,2},{1,3},{2,0},{3,1},{4,6},{5,7},{6,4},{7,5},{8,10},{9,11},{10,... | collective-permute-start | bytes 589832 | tf_op jit(solution)/shard_map/ppermute | solution.py:59
  24.6 9.2 %collective-permute-start.14 = (f32[512,128]{1,0:T(8,128)S(1)}, f32[512,128]{1,0:T(8,128)S(1)}, u32[]{:S(2)}, u32[]{:S(2)}) collective-permute-start(f32[512,128]{1,0:T(8,128)S(1)} %get-tuple-element.40.send_ref.q0), channel_id=1, source_target_pairs={{0,16},{24,8},{8,0},{16,24},{1,17},{25,9},{9,1},{17,25},{2,18},{26... | collective-permute-start | bytes 786440 | tf_op jit(solution)/shard_map/ppermute | solution.py:352
  24.7 13.7 %collective-permute-start.13 = (f32[512,128]{1,0:T(8,128)S(1)}, f32[512,128]{1,0:T(8,128)S(1)}, u32[]{:S(2)}, u32[]{:S(2)}) collective-permute-start(f32[512,128]{1,0:T(8,128)S(1)} %get-tuple-element.40.send_ref.q0), channel_id=1, source_target_pairs={{0,8},{24,16},{8,0},{16,24},{1,9},{25,17},{9,1},{17,25},{2,10},{26... | collective-permute-start | bytes 786440 | tf_op jit(solution)/shard_map/ppermute | solution.py:352
  26.7 11.7 %collective-permute-start.12 = (f32[512,128]{1,0:T(8,128)S(1)}, f32[512,128]{1,0:T(8,128)S(1)}, u32[]{:S(2)}, u32[]{:S(2)}) collective-permute-start(f32[512,128]{1,0:T(8,128)S(1)} %get-tuple-element.40.send_ref.q0), channel_id=1, source_target_pairs={{8,16},{16,8},{0,0},{24,24},{9,17},{17,9},{1,1},{25,25},{10,18},{1... | collective-permute-start | bytes 786440 | tf_op jit(solution)/shard_map/ppermute | solution.py:352
  27.9 12.0 %collective-permute-start.11 = (f32[768,128]{1,0:T(8,128)S(1)}, f32[768,128]{1,0:T(8,128)S(1)}, u32[]{:S(2)}, u32[]{:S(2)}) collective-permute-start(f32[768,128]{1,0:T(8,128)S(1)} %pad_maximum_fusion.3), channel_id=1, source_target_pairs={{0,2},{1,3},{2,0},{3,1},{4,6},{5,7},{6,4},{7,5},{8,10},{9,11},{10,... | collective-permute-start | bytes 1179656 | tf_op jit(solution)/shard_map/ppermute | solution.py:59
  29.7 10.3 %collective-permute-start.10 = (f32[768,128]{1,0:T(8,128)S(1)}, f32[768,128]{1,0:T(8,128)S(1)}, u32[]{:S(2)}, u32[]{:S(2)}) collective-permute-start(f32[768,128]{1,0:T(8,128)S(1)} %pad_maximum_fusion.4), channel_id=1, source_target_pairs={{0,4},{1,5},{2,6},{3,7},{4,0},{5,1},{6,2},{7,3},{8,12},{9,13},{10,... | collective-permute-start | bytes 1179656 | tf_op jit(solution)/shard_map/ppermute | solution.py:59
  39.5 7.3 %collective-permute-start.17 = (f32[512,128]{1,0:T(8,128)S(1)}, f32[512,128]{1,0:T(8,128)S(1)}, u32[]{:S(2)}, u32[]{:S(2)}) collective-permute-start(f32[512,128]{1,0:T(8,128)S(1)} %get-tuple-element.57), channel_id=1, source_target_pairs={{0,8},{8,0},{16,24},{24,16},{1,9},{9,1},{17,25},{25,17},{2,10},{10... | collective-permute-start | bytes 786440 | tf_op jit(solution)/shard_map/ppermute | solution.py:59
  40.3 2.4 %collective-permute-start.16 = (f32[2,768,128]{2,1,0:T(8,128)S(1)}, f32[2,768,128]{2,1,0:T(8,128)S(1)}, u32[]{:S(2)}, u32[]{:S(2)}) collective-permute-start(f32[2,768,128]{2,1,0:T(8,128)S(1)} %pad_maximum_fusion.1.hi.s_hi), channel_id=1, source_target_pairs={{0,1},{1,0},{2,3},{3,2},{4,5},{5,4},{6,7},{7,6},{8,9},{9,8},{10,11... | collective-permute-start | bytes 2359304 | tf_op jit(solution)/shard_map/ppermute | solution.py:59
  40.4 3.3 %collective-permute-start.15 = (f32[2,768,128]{2,1,0:T(8,128)S(1)}, f32[2,768,128]{2,1,0:T(8,128)S(1)}, u32[]{:S(2)}, u32[]{:S(2)}) collective-permute-start(f32[2,768,128]{2,1,0:T(8,128)S(1)} %pad_maximum_fusion.lo.s_lo), channel_id=1, source_target_pairs={{0,1},{1,0},{2,3},{3,2},{4,5},{5,4},{6,7},{7,6},{8,9},{9,8},{10,11... | collective-permute-start | bytes 2359304 | tf_op jit(solution)/shard_map/ppermute | solution.py:59
  44.4 9.7 %collective-permute-start.18 = (f32[256,128]{1,0:T(8,128)S(1)}, f32[256,128]{1,0:T(8,128)S(1)}, u32[]{:S(2)}, u32[]{:S(2)}) collective-permute-start(f32[256,128]{1,0:T(8,128)S(1)} %get-tuple-element.62), channel_id=1, source_target_pairs={{8,0},{16,24},{9,1},{17,25},{10,2},{18,26},{11,3},{19,27},{12,4},{... | collective-permute-start | bytes 393224 | tf_op jit(solution)/shard_map/ppermute | solution.py:418

commit v4 on v3

--- a/solution.py
+++ b/solution.py
@@ -184,63 +184,65 @@
     return jnp.logical_or(r == 1, r == 2)
 
 
-def tile_of(mask_ref, r, block, j, m, first, rest):
-    part = first[4 + j] if m == 0 else rest[j % 2, (m - 1) * BAND : m * BAND]
-    return part * pattern_of(mask_ref, band_blocks(r, m), [block])
-
-
-def meets(mask_ref, r, m, block):
-    return sum(mask_ref[i, block] for i in band_blocks(r, m)) != 0
-
-
-def block_of(c, j, flip):
-    return jnp.bitwise_xor(c, 2 * j + flip)
+def column_pair(mask_ref, r, blocks, j, first, rest):
+    bands = []
+    for m in range(4):
+        parts = []
+        for i in (0, 1):
+            part = first[4 + j + i] if m == 0 else rest[i, (m - 1) * BAND : m * BAND]
+            parts.append(part * pattern_of(mask_ref, band_blocks(r, m), [blocks[i]]))
+        bands.append(jnp.concatenate(parts, axis=1))
+    return split(jnp.concatenate(bands, axis=0))
 
 
 def rows_at(r, ref, blocks):
     return jnp.concatenate([ref[pl.ds(place(r, b), BLK), :] for b in blocks], axis=0)
 
 
-def php_kernel(mask_ref, prow, q3, q1, q2, q0, php_ref, hcol, across_ref, qcol):
-    r, c = lax.axis_index("row"), lax.axis_index("col")
-    for m, ref in enumerate((q0, q1, q2, q3)):
-        qcol[m * BAND : (m + 1) * BAND, :] = beside(ref[0:BAND])
-        fill = ref[BAND:] * pattern_of(mask_ref, band_blocks(r, m), [c])
-        hcol[m * BAND : (m + 1) * BAND, :] = beside(fill)
-    own = pattern_of(mask_ref, band_blocks(r, 0), [c])
-    php_ref[...] = dot_parts(prow[...], qcol[...]) * own
+def far_rows(cols):
+    return jnp.concatenate([part[BAND : 2 * BAND] for part in cols], axis=0)
+
+
+def h_kernel(mask_ref, q3, q1, q2, q0, hcol, across_ref):
+    r, c = lax.axis_index("row"), lax.axis_index("col")
+    fill_cols(mask_ref, r, c, [ref[BAND:] for ref in (q0, q1, q2, q3)], hcol)
     across_ref[0:BAND] = q3[0:BAND]
     across_ref[BAND:] = q2[0:BAND]
 
 
-def add_ph(mask_ref, r, c, flip, j, first, rest, hcol, ph_ref, far, slot):
-    block = block_of(c, j, flip)
-
-    @pl.when(mask_ref[block, c] != 0)
-    def _():
-        right = rows_at(r, hcol, [block])
-        for m in range(4):
-            at = pl.ds(m * BAND, BAND)
-            if m == 1:
-                left = stacked(tile_of(mask_ref, r, block, j, m, first, rest))
-                far[:, slot * BLK : (slot + 1) * BLK] = left
-                ph_ref[at, :] += dot_parts(left, right)
-                continue
-
-            @pl.when(jnp.logical_and(meets(mask_ref, r, m, block), meets(mask_ref, r, m, c)))
-            def _(m=m, at=at):
-                left = stacked(tile_of(mask_ref, r, block, j, m, first, rest))
-                ph_ref[at, :] += dot_parts(left, right)
-
-
-def own_kernel(mask_ref, hcol, ss, lo, hi, ph_ref, far):
+def any_live(mask_ref, blocks, c):
+    return sum(mask_ref[b, c] for b in blocks) != 0
+
+
+def add_ph(mask_ref, r, c, pair, first, rest, hcol, ph_ref, far):
+    j, blocks = pair
+
+    @pl.when(any_live(mask_ref, blocks, c))
+    def _():
+        cols = column_pair(mask_ref, r, blocks, j, first, rest)
+        ph_ref[...] += dot_tall(cols, rows_at(r, hcol, blocks))
+        far[...] = far_rows(cols)
+
+
+def php_of(mask_ref, r, c, parts, prow, qcol):
+    for m, part in enumerate(parts):
+        qcol[m * BAND : (m + 1) * BAND, :] = beside(part)
+    own = pattern_of(mask_ref, band_blocks(r, 0), [c])
+    return dot_parts(prow[...], qcol[...]) * own
+
+
+def own_kernel(
+    mask_ref, hcol, ss, lo, hi, prow, q0, q1, q2, q3, ph_ref, far_lo, far_hi, php_ref, qcol
+):
     r, c = lax.axis_index("row"), lax.axis_index("col")
 
     @pl.when(is_middle(r))
     def _():
+        parts = [ref[0:BAND] for ref in (q0, q1, q2, q3)]
+        php_ref[...] = php_of(mask_ref, r, c, parts, prow, qcol)
         ph_ref[...] = jnp.zeros_like(ph_ref)
-        for j in range(4):
-            add_ph(mask_ref, r, c, 0, j, ss, (lo, hi)[j // 2], hcol, ph_ref, far, j)
+        for pair, rest, far in zip(pairs(c, 0), (lo, hi), (far_lo, far_hi)):
+            add_ph(mask_ref, r, c, pair, ss, rest, hcol, ph_ref, far)
 
 
 def other_kernel(mask_ref, hcol, so, hi, part_ref, ph_ref, far):
@@ -249,12 +251,13 @@
     @pl.when(is_middle(r))
     def _():
         ph_ref[...] = part_ref[...]
-        for j in (2, 3):
-            add_ph(mask_ref, r, c, 1, j, so, hi, hcol, ph_ref, far, j - 2)
+        _, pair = pairs(c, 1)
+        add_ph(mask_ref, r, c, pair, so, hi, hcol, ph_ref, far)
 
 
 def ph_kernel(
-    mask_ref, hcol, so, lo, part_ref, far_own, far_hi, back_ref, tile_ref, ph2, ph_ref, far_lo
+    mask_ref, hcol, so, lo, part_ref, own_lo, own_hi, other_hi, back_ref, tile_ref, ph2,
+    ph_ref, other_lo,
 ):
     r, c = lax.axis_index("row"), lax.axis_index("col")
     back_ref[...] = jnp.zeros_like(back_ref)
@@ -264,8 +267,7 @@
     @pl.when(is_middle(r))
     def _():
         ph_ref[...] = part_ref[...]
-        for j in (0, 1):
-            add_ph(mask_ref, r, c, 1, j, so, lo, hcol, ph_ref, far_lo, j)
+        add_ph(mask_ref, r, c, next(pairs(c, 1)), so, lo, hcol, ph_ref, other_lo)
         for m in range(4):
             at = pl.ds(m * BAND, BAND)
             rows = ph_ref[at, :] * pattern_of(mask_ref, band_blocks(r, m), [c])
@@ -275,22 +277,27 @@
             if m == 1:
                 back_ref[...] = 3.0 * rows
         there = pattern_of(mask_ref, band_blocks(r, 1), [c])
-        for flip, far, j, slot in (
-            *((0, far_own, j, j) for j in range(4)),
-            *((1, far_lo, j, j) for j in (0, 1)),
-            *((1, far_hi, j, j - 2) for j in (2, 3)),
-        ):
-            block = block_of(c, j, flip)
-
-            @pl.when(mask_ref[block, c] != 0)
-            def _(far=far, slot=slot, block=block):
-                left = far[:, slot * BLK : (slot + 1) * BLK]
-                back_ref[...] -= 2.0 * there * dot_parts(left, rows_at(r, ph2, [block]))
+        fars = ((0, (own_lo, own_hi)), (1, (other_lo, other_hi)))
+        for flip, parts in fars:
+            for (_, blocks), far in zip(pairs(c, flip), parts):
+
+                @pl.when(any_live(mask_ref, blocks, c))
+                def _(blocks=blocks, far=far):
+                    term = dot_parts(far[...], rows_at(r, ph2, blocks))
+                    back_ref[...] -= 2.0 * there * term
+
+
+def column(mask_ref, r, block, j, first, rest):
+    bands = []
+    for m in range(4):
+        part = first[4 + j] if m == 0 else rest[j % 2, (m - 1) * BAND : m * BAND]
+        bands.append(part * pattern_of(mask_ref, band_blocks(r, m), [block]))
+    return beside(jnp.concatenate(bands, axis=0))
 
 
 def last_kernel(
     mask_ref, prow, hrow, pcol, ss, so, s_lo, s_hi, o_lo, o_hi, ph2, send_ref, q1, q23,
-    ph_ref, part_ref, php_ref, grad_ref, qcol, acc, row_acc,
+    ph_ref, part_ref, php_ref, grad_ref, qcol, acc,
 ):
     r, c = lax.axis_index("row"), lax.axis_index("col")
     own = pattern_of(mask_ref, band_blocks(r, 0), [c])
@@ -303,27 +310,20 @@
 
     @pl.when(jnp.logical_not(is_middle(r)))
     def _():
-        for m, part in enumerate((hp, q1[0:BAND], q23[0:BAND], q23[BAND:])):
-            qcol[m * BAND : (m + 1) * BAND, :] = beside(part)
-        php_ref[...] = dot_parts(prow[...], qcol[...]) * own
+        parts = (hp, q1[0:BAND], q23[0:BAND], q23[BAND:])
+        php_ref[...] = php_of(mask_ref, r, c, parts, prow, qcol)
         acc[...] = jnp.zeros_like(acc)
 
     acc[...] += dot_parts(stacked(hp), rows_at(r, pcol, [c]))
     for flip, first, rests in ((0, ss, (s_lo, s_hi)), (1, so, (o_lo, o_hi))):
         for j in range(1 - flip, 4):
-            block = block_of(c, j, flip)
+            block = jnp.bitwise_xor(c, 2 * j + flip)
 
             @pl.when(mask_ref[block, c] != 0)
             def _(first=first, rest=rests[j // 2], j=j, block=block):
-                row_acc[...] = jnp.zeros_like(row_acc)
-                for m in range(4):
-
-                    @pl.when(meets(mask_ref, r, m, block))
-                    def _(m=m):
-                        right = beside(tile_of(mask_ref, r, block, j, m, first, rest))
-                        row_acc[...] += dot_parts(hrow[:, m * BAND : (m + 1) * BAND], right)
-
-                rows = row_acc[...] * pattern_of(mask_ref, band_blocks(r, 0), [block])
+                cols = column(mask_ref, r, block, j, first, rest)
+                rows = dot_parts(hrow[...], cols)
+                rows = rows * pattern_of(mask_ref, band_blocks(r, 0), [block])
                 acc[...] += dot_parts(stacked(rows), rows_at(r, pcol, [block]))
 
     grad_ref[...] = 3.0 * (hp + ph_ref[...]) - 2.0 * (php_ref[...] + own * acc[...])
@@ -392,33 +392,33 @@
     hrow, prow, hp = call(
         rows_kernel, (rows2, rows2, tile), [], weight, block_mask, ss, so, send, mark
     )
-    php, hcol, across = call(
-        php_kernel, (tile, cols2, shape(2 * rows, cols, f32)),
-        [pltpu.VMEM((order, 2 * cols), bf16)], AHEAD * weight,
-        block_mask, prow, q3, q1, q2, send,
+    hcol, across = call(
+        h_kernel, (cols2, shape(2 * rows, cols, f32)), [], AHEAD * weight,
+        block_mask, q3, q1, q2, send,
     )
     q23 = swap(across, "row", 1)
-    uy, lx, php = lax.optimization_barrier((uy, lx, php))
+    uy, lx, hcol = lax.optimization_barrier((uy, lx, hcol))
     s_lo = jnp.stack([b, jnp.concatenate([ux, lx[:half]], axis=0)])
     s_hi = jnp.stack([jnp.concatenate(pair, axis=0) for pair in ((uy[:half], ly), (uy[half:], lx[half:]))])
     o_lo, o_hi = swap(s_lo, "col", 1), swap(s_hi, "col", 1)
 
-    half_far, quarter_far = shape(2 * rows, order // 2), shape(2 * rows, order // 4)
-    strip_acc = pltpu.VMEM((order, cols), f32)
-    part, far_own = call(
-        own_kernel, (strip, half_far), [], AHEAD * weight, block_mask, hcol, ss, s_lo, s_hi
-    )
-    part, far_hi = call(
-        other_kernel, (strip, quarter_far), [], weight, block_mask, hcol, so, o_hi, part
+    far = shape(2 * rows, order // 4)
+    part, own_lo, own_hi, php = call(
+        own_kernel, (strip, far, far, tile), [pltpu.VMEM((order, 2 * cols), bf16)],
+        AHEAD * weight, block_mask, hcol, ss, s_lo, s_hi, prow, send, q1, q2, q3,
+    )
+    part, other_hi = call(
+        other_kernel, (strip, far), [], weight, block_mask, hcol, so, o_hi, part
     )
     back, ph, ph2 = call(
-        ph_kernel, (tile, tile, cols2), [strip_acc, pltpu.VMEM((2 * rows, order // 4), bf16)],
-        weight, block_mask, hcol, so, o_lo, part, far_own, far_hi,
-    )
-    got = lax.ppermute(back, "row", [(1, 0), (2, 3)])
+        ph_kernel, (tile, tile, cols2),
+        [pltpu.VMEM((order, cols), f32), pltpu.VMEM((2 * rows, order // 4), bf16)], weight,
+        block_mask, hcol, so, o_lo, part, own_lo, own_hi, other_hi,
+    )
+    got = swap(back, "row", 1)
     php, grad = call(
         last_kernel, (tile, tile),
-        [pltpu.VMEM((order, 2 * cols), bf16)] + [pltpu.VMEM((rows, cols), f32)] * 2, weight,
+        [pltpu.VMEM((order, 2 * cols), bf16), pltpu.VMEM((rows, cols), f32)], weight,
         block_mask, prow, hrow, pcol, ss, so, s_lo, s_hi, o_lo, o_hi, ph2, send, q1, q23, ph, php,
     )
     return hp, php, grad + got

time: 54.4 us -> 51.3 us (0.943); the launches traced: 54.8 us -> 50.7 us
  Pallas kernels: 13 us -> 8.81 us
  starting transfers between devices: 21.4 us -> 22 us
    pallas_call x8, Pallas kernels: 13 us -> 8.81 us  [call(): pl.pallas_call(kernel, out_shape=outs, in_specs=[smem] + [vmem] * (len(ar...]
    ppermute x15 -> x16, starting transfers between devices: 17.4 us -> 19.3 us  [swap(): return lax.ppermute(x, axis, [(i, i ^ mask) for i in range(size)])]
    ppermute x1 -> x0, starting transfers between devices: 1.29 us -> none  [whole_body(): got = lax.ppermute(back, 'row', [(1, 0), (2, 3)])]
    ppermute x1 -> x0, waiting for transfers between devices: 0.74 us -> none  [whole_body(): got = lax.ppermute(back, 'row', [(1, 0), (2, 3)])]
    ppermute x15 -> x16, waiting for transfers between devices: 11 us -> 11.2 us  [swap(): return lax.ppermute(x, axis, [(i, i ^ mask) for i in range(size)])]
  transfers between devices with their start and end apart: 19 -> 19, of which waited for: 11 -> 11; matrix products, arithmetic and copies ran while one was open for 3% -> 3% of each run, Pallas kernels for 24% -> 17%
where the time goes in v4:
time: 51.3 us; the launch traced here: 50.7 us
  starting transfers between devices  22 us (43%)
  waiting for transfers between devices  16.8 us (33%)
  Pallas kernels  8.81 us (17%)
  other arithmetic  1.99 us (4%)
  between operations  0.9 us (2%)
    ppermute x16, starting transfers between devices, swap(): return lax.ppermute(x, axis, [(i, i ^ mask) for i in range(size)])  19.3 us
    ppermute x16, waiting for transfers between devices, swap(): return lax.ppermute(x, axis, [(i, i ^ mask) for i in range(size)])  11.2 us
    pallas_call x8, Pallas kernels, call(): pl.pallas_call(kernel, out_shape=outs, in_specs=[smem] + [vmem] * (len(ar...  8.81 us
    ppermute x3, waiting for transfers between devices, to_middle(): return [lax.ppermute(x, 'row', pairs) for pairs in routes]  5.53 us
    ppermute x3, starting transfers between devices, to_middle(): return [lax.ppermute(x, 'row', pairs) for pairs in routes]  2.74 us
  transfers between devices with their start and end apart: 19, of which 11 were waited for; matrix products, arithmetic and copies ran while one was open for 3% of the time, Pallas kernels for 17%

profile of v4, /device:TPU:0, one launch (start us, length us, event | category | flops | bytes accessed | tf_op | source)
XLA Modules:
  0.0 50.7 jit_solution(3254530518243972477)
XLA Ops:
  0.6 3.0 %collective-permute-start.5 = (f32[256,128]{1,0:T(8,128)}, f32[256,128]{1,0:T(8,128)S(1)}, u32[]{:S(2)}, u32[]{:S(2)}) collective-permute-start(f32[256,128]{1,0:T(8,128)} %param.3), channel_id=1, source_target_pairs={{0,4},{1,5},{2,6},{3,7},{4,0},{5,1},{6,2},{7,3},{8,12},{9,13},{10,... | collective-permute-start | bytes 393224 | tf_op jit(solution)/shard_map/ppermute | solution.py:59
  3.7 3.6 %collective-permute-start.3 = (f32[256,128]{1,0:T(8,128)}, f32[256,128]{1,0:T(8,128)S(1)}, u32[]{:S(2)}, u32[]{:S(2)}) collective-permute-start(f32[256,128]{1,0:T(8,128)} %param.3), channel_id=1, source_target_pairs={{0,24},{8,16},{16,8},{24,0},{1,25},{9,17},{17,9},{25,1},{2,26},{10... | collective-permute-start | bytes 393224 | tf_op jit(solution)/shard_map/ppermute | solution.py:59
  7.3 1.5 %collective-permute-start = (f32[256,128]{1,0:T(8,128)}, f32[256,128]{1,0:T(8,128)S(1)}, u32[]{:S(2)}, u32[]{:S(2)}) collective-permute-start(f32[256,128]{1,0:T(8,128)} %param.4), channel_id=1, source_target_pairs={{0,2},{1,3},{2,0},{3,1},{4,6},{5,7},{6,4},{7,5},{8,10},{9,11},{10,... | collective-permute-start | bytes 393224 | tf_op jit(solution)/shard_map/ppermute | solution.py:59
  8.8 1.0 %pad_maximum_fusion.5 = f32[512,128]{1,0:T(8,128)S(1)} fusion(f32[256,128]{1,0:T(8,128)} %param.4, f32[256,128]{1,0:T(8,128)} %param.3), kind=kLoop, calls=%fused_computation.9 | loop fusion | flops 65536 | bytes 524288 | tf_op jit(solution)/shard_map/concatenate | solution.py:369
  9.8 0.1 collective-permute-start.2
  9.9 0.8 %collective-permute-start.1 = (f32[256,128]{1,0:T(8,128)S(1)}, f32[256,128]{1,0:T(8,128)S(1)}, u32[]{:S(2)}, u32[]{:S(2)}) collective-permute-start(f32[256,128]{1,0:T(8,128)S(1)} %get-tuple-element.70.p0), channel_id=1, source_target_pairs={{0,8},{8,0},{16,24},{24,16},{1,9},{9,1},{17,25},{25,17},{2,10},{10... | collective-permute-start | bytes 393224 | tf_op jit(solution)/shard_map/ppermute | solution.py:59
  10.6 0.0 collective-permute-done.5
  10.6 0.6 %collective-permute-start.6 = (f32[512,128]{1,0:T(8,128)S(1)}, f32[512,128]{1,0:T(8,128)S(1)}, u32[]{:S(2)}, u32[]{:S(2)}) collective-permute-start(f32[512,128]{1,0:T(8,128)S(1)} %pad_maximum_fusion.7), channel_id=1, source_target_pairs={{0,2},{1,3},{2,0},{3,1},{4,6},{5,7},{6,4},{7,5},{8,10},{9,11},{10,... | collective-permute-start | bytes 786440 | tf_op jit(solution)/shard_map/ppermute | solution.py:59
  11.2 1.9 %collective-permute-done = f32[256,128]{1,0:T(8,128)S(1)} collective-permute-done((f32[256,128]{1,0:T(8,128)}, f32[256,128]{1,0:T(8,128)S(1)}, u32[]{:S(2)}, u32[]{:S(2)}) %collective-permute-start) | collective-permute-done | bytes 131104 | tf_op jit(solution)/shard_map/ppermute | solution.py:59
  13.1 0.6 %collective-permute-start.4 = (f32[512,128]{1,0:T(8,128)S(1)}, f32[512,128]{1,0:T(8,128)S(1)}, u32[]{:S(2)}, u32[]{:S(2)}) collective-permute-start(f32[512,128]{1,0:T(8,128)S(1)} %pad_maximum_fusion.6), channel_id=1, source_target_pairs={{0,4},{1,5},{2,6},{3,7},{4,0},{5,1},{6,2},{7,3},{8,12},{9,13},{10,... | collective-permute-start | bytes 786440 | tf_op jit(solution)/shard_map/ppermute | solution.py:59
  13.7 0.0 collective-permute-done.3.p3
  13.7 4.5 %collective-permute-done.2.p2 = f32[256,128]{1,0:T(8,128)S(1)} collective-permute-done((f32[256,128]{1,0:T(8,128)S(1)}, f32[256,128]{1,0:T(8,128)S(1)}, u32[]{:S(2)}, u32[]{:S(2)}) %collective-permute-start.2) | collective-permute-done | bytes 131104 | tf_op jit(solution)/shard_map/ppermute | solution.py:59
  18.3 1.3 %collective-permute-done.4 = f32[512,128]{1,0:T(8,128)S(1)} collective-permute-done((f32[512,128]{1,0:T(8,128)S(1)}, f32[512,128]{1,0:T(8,128)S(1)}, u32[]{:S(2)}, u32[]{:S(2)}) %collective-permute-start.4) | collective-permute-done | bytes 262176 | tf_op jit(solution)/shard_map/ppermute | solution.py:59
  19.7 0.0 copy-start
  19.7 0.1 collective-permute-start.7
  19.8 0.6 %collective-permute-start.9 = (f32[384,128]{1,0:T(8,128)S(1)}, f32[384,128]{1,0:T(8,128)S(1)}, u32[]{:S(2)}, u32[]{:S(2)}) collective-permute-start(f32[384,128]{1,0:T(8,128)S(1)} %get-tuple-element.71), channel_id=1, source_target_pairs={{0,4},{1,5},{2,6},{3,7},{4,0},{5,1},{6,2},{7,3},{8,12},{9,13},{10,... | collective-permute-start | bytes 589832 | tf_op jit(solution)/shard_map/ppermute | solution.py:59
  20.4 2.2 %collective-permute-start.8 = (f32[384,128]{1,0:T(8,128)S(1)}, f32[384,128]{1,0:T(8,128)S(1)}, u32[]{:S(2)}, u32[]{:S(2)}) collective-permute-start(f32[384,128]{1,0:T(8,128)S(1)} %get-tuple-element.72), channel_id=1, source_target_pairs={{0,2},{1,3},{2,0},{3,1},{4,6},{5,7},{6,4},{7,5},{8,10},{9,11},{10,... | collective-permute-start | bytes 589832 | tf_op jit(solution)/shard_map/ppermute | solution.py:59
  22.6 1.0 %shard_map.58 = (f32[256,128]{1,0:T(8,128)S(1)}, bf16[1024,256]{1,0:T(8,128)(2,1)S(1)}) custom-call(s32[8,8]{1,0:T(8,128)S(1)} %copy-done, f32[256,128]{1,0:T(8,128)S(1)} %get-tuple-element.70.p0, f32[256,128]{1,0:T(8,128)S(1)} %collective-permute-done.1.p1, f32[256,128]{1,0:T(8,128)S(1)} %collective-permute-done.2.p2, ...), custom_call_target="tpu_custom_call" | custom-call | flops 1610612736 | bytes 2228480 | tf_op jit(solution)/shard_map/pallas_call | solution.py:335
  23.7 0.0 collective-permute-done.7.so
  23.7 0.9 %shard_map.59 = (f32[512,128]{1,0:T(8,128)S(1)}, f32[8,128]{1,0:T(8,128)S(1)}) custom-call(s32[8,8]{1,0:T(8,128)S(1)} %copy-done, f32[256,128]{1,0:T(8,128)S(1)} %get-tuple-element.39.part_ref, bf16[1024,256]{1,0:T(8,128)(2,1)S(1)} %get-tuple-element.40.pcol, f32[8,256,128]{2,1,0:T(8,128)S(1)} %bitcast_dynamic-update-slice_fusion.ss, ...), custom_call_target="tpu_custom_call" | custom-call | flops 1610612736 | bytes 3019008 | tf_op jit(solution)/shard_map/pallas_call | solution.py:335
  24.6 0.1 collective-permute-start.14
  24.7 2.0 %collective-permute-start.13 = (f32[512,128]{1,0:T(8,128)S(1)}, f32[512,128]{1,0:T(8,128)S(1)}, u32[]{:S(2)}, u32[]{:S(2)}) collective-permute-start(f32[512,128]{1,0:T(8,128)S(1)} %get-tuple-element.41.send_ref.q0), channel_id=1, source_target_pairs={{0,8},{24,16},{8,0},{16,24},{1,9},{25,17},{9,1},{17,25},{2,10},{26... | collective-permute-start | bytes 786440 | tf_op jit(solution)/shard_map/ppermute | solution.py:352
  26.7 0.7 %collective-permute-start.12 = (f32[512,128]{1,0:T(8,128)S(1)}, f32[512,128]{1,0:T(8,128)S(1)}, u32[]{:S(2)}, u32[]{:S(2)}) collective-permute-start(f32[512,128]{1,0:T(8,128)S(1)} %get-tuple-element.41.send_ref.q0), channel_id=1, source_target_pairs={{8,16},{16,8},{0,0},{24,24},{9,17},{17,9},{1,1},{25,25},{10,18},{1... | collective-permute-start | bytes 786440 | tf_op jit(solution)/shard_map/ppermute | solution.py:352
  27.4 0.0 collective-permute-done.9
  27.4 0.5 collective-permute-done.8
  27.9 1.8 %collective-permute-start.11 = (f32[768,128]{1,0:T(8,128)S(1)}, f32[768,128]{1,0:T(8,128)S(1)}, u32[]{:S(2)}, u32[]{:S(2)}) collective-permute-start(f32[768,128]{1,0:T(8,128)S(1)} %pad_maximum_fusion.3), channel_id=1, source_target_pairs={{0,2},{1,3},{2,0},{3,1},{4,6},{5,7},{6,4},{7,5},{8,10},{9,11},{10,... | collective-permute-start | bytes 1179656 | tf_op jit(solution)/shard_map/ppermute | solution.py:59
  29.7 1.6 %collective-permute-start.10 = (f32[768,128]{1,0:T(8,128)S(1)}, f32[768,128]{1,0:T(8,128)S(1)}, u32[]{:S(2)}, u32[]{:S(2)}) collective-permute-start(f32[768,128]{1,0:T(8,128)S(1)} %pad_maximum_fusion.4), channel_id=1, source_target_pairs={{0,4},{1,5},{2,6},{3,7},{4,0},{5,1},{6,2},{7,3},{8,12},{9,13},{10,... | collective-permute-start | bytes 1179656 | tf_op jit(solution)/shard_map/ppermute | solution.py:59
  31.3 1.6 %shard_map.60 = (bf16[512,1024]{1,0:T(8,128)(2,1)S(1)}, bf16[512,1024]{1,0:T(8,128)(2,1)S(1)}, f32[256,128]{1,0:T(8,128)}) custom-call(s32[8,8]{1,0:T(8,128)S(1)} %copy-done, f32[8,256,128]{2,1,0:T(8,128)S(1)} %bitcast_dynamic-update-slice_fusion.ss, f32[8,256,128]{2,1,0:T(8,128)S(1)} %collective-permute-done.7.so, ...), custom_call_target="tpu_custom_call" | custom-call | flops 1610612736 | bytes 4591872 | tf_op jit(solution)/shard_map/pallas_call | solution.py:335
  32.9 1.0 %collective-permute-done.14.q2 = f32[512,128]{1,0:T(8,128)S(1)} collective-permute-done((f32[512,128]{1,0:T(8,128)S(1)}, f32[512,128]{1,0:T(8,128)S(1)}, u32[]{:S(2)}, u32[]{:S(2)}) %collective-permute-start.14) | collective-permute-done | bytes 262176 | tf_op jit(solution)/shard_map/ppermute | solution.py:352
  33.9 4.6 %collective-permute-done.13.q1 = f32[512,128]{1,0:T(8,128)S(1)} collective-permute-done((f32[512,128]{1,0:T(8,128)S(1)}, f32[512,128]{1,0:T(8,128)S(1)}, u32[]{:S(2)}, u32[]{:S(2)}) %collective-permute-start.13) | collective-permute-done | bytes 262176 | tf_op jit(solution)/shard_map/ppermute | solution.py:352
  38.4 0.7 %shard_map.61 = (bf16[1024,256]{1,0:T(8,128)(2,1)S(1)}, f32[512,128]{1,0:T(8,128)S(1)}) custom-call(s32[8,8]{1,0:T(8,128)S(1)} %copy-done, f32[512,128]{1,0:T(8,128)S(1)} %collective-permute-done.12.q3, f32[512,128]{1,0:T(8,128)S(1)} %collective-permute-done.13.q1, f32[512,128]{1,0:T(8,128)S(1)} %collective-permute-done.14.q2, ...), custom_call_target="tpu_custom_call" | custom-call | flops 12884901888 | bytes 1835264 | tf_op jit(solution)/shard_map/pallas_call | solution.py:335
  39.1 0.4 collective-permute-start.17
  39.5 0.5 collective-permute-done.10
  40.0 0.1 fusion.1
  40.2 0.1 pad_maximum_fusion.1.hi.s_hi
  40.3 0.1 collective-permute-start.16
  40.3 0.1 pad_maximum_fusion.lo.s_lo
  40.4 0.6 %collective-permute-start.15 = (f32[2,768,128]{2,1,0:T(8,128)S(1)}, f32[2,768,128]{2,1,0:T(8,128)S(1)}, u32[]{:S(2)}, u32[]{:S(2)}) collective-permute-start(f32[2,768,128]{2,1,0:T(8,128)S(1)} %pad_maximum_fusion.lo.s_lo), channel_id=1, source_target_pairs={{0,1},{1,0},{2,3},{3,2},{4,5},{5,4},{6,7},{7,6},{8,9},{9,8},{10,11... | collective-permute-start | bytes 2359304 | tf_op jit(solution)/shard_map/ppermute | solution.py:59
  41.0 0.6 %shard_map.62 = (f32[1024,128]{1,0:T(8,128)S(1)}, bf16[512,256]{1,0:T(8,128)(2,1)S(1)}, bf16[512,256]{1,0:T(8,128)(2,1)S(1)}, f32[256,128]{1,0:T(8,128)S(1)}) custom-call(s32[8,8]{1,0:T(8,128)S(1)} %copy-done, bf16[1024,256]{1,0:T(8,128)(2,1)S(1)} %get-tuple-element.52.hcol, f32[8,256,128]{2,1,0:T(8,128)S(1)} %bitcast_dynamic-update-slice_fusion.ss, ...), custom_call_target="tpu_custom_call" | custom-call | flops 12884901888 | bytes 6422784 | tf_op jit(solution)/shard_map/pallas_call | solution.py:335
  41.6 1.0 %collective-permute-done.16.hi.o_hi = f32[2,768,128]{2,1,0:T(8,128)S(1)} collective-permute-done((f32[2,768,128]{2,1,0:T(8,128)S(1)}, f32[2,768,128]{2,1,0:T(8,128)S(1)}, u32[]{:S(2)}, u32[]{:S(2)}) %collective-permute-start.16) | collective-permute-done | bytes 786464 | tf_op jit(solution)/shard_map/ppermute | solution.py:59
  42.6 0.6 %shard_map.63 = (f32[1024,128]{1,0:T(8,128)S(1)}, bf16[512,256]{1,0:T(8,128)(2,1)S(1)}) custom-call(s32[8,8]{1,0:T(8,128)S(1)} %copy-done, bf16[1024,256]{1,0:T(8,128)(2,1)S(1)} %get-tuple-element.52.hcol, f32[8,256,128]{2,1,0:T(8,128)S(1)} %collective-permute-done.7.so, f32[2,768,128]{2,1,0:T(8,128)S(1)} %collective-permute-done.16.hi.o_hi, ...), custom_call_target="tpu_custom_call" | custom-call | flops 1610612736 | bytes 3670272 | tf_op jit(solution)/shard_map/pallas_call | solution.py:335
  43.2 0.5 collective-permute-done.15.lo.o_lo
  43.7 0.7 %shard_map.64 = (f32[256,128]{1,0:T(8,128)S(1)}, f32[256,128]{1,0:T(8,128)S(1)}, bf16[1024,256]{1,0:T(8,128)(2,1)S(1)}) custom-call(s32[8,8]{1,0:T(8,128)S(1)} %copy-done, bf16[1024,256]{1,0:T(8,128)(2,1)S(1)} %get-tuple-element.52.hcol, f32[8,256,128]{2,1,0:T(8,128)S(1)} %collective-permute-done.7.so, f32[2,768,128]{2,1,0:T(8,128)S(1)} %collective-permute-done.15.lo.o_lo, ...), custom_call_target="tpu_custom_call" | custom-call | flops 1610612736 | bytes 4456704 | tf_op jit(solution)/shard_map/pallas_call | solution.py:335
  44.4 1.9 %collective-permute-start.18 = (f32[256,128]{1,0:T(8,128)S(1)}, f32[256,128]{1,0:T(8,128)S(1)}, u32[]{:S(2)}, u32[]{:S(2)}) collective-permute-start(f32[256,128]{1,0:T(8,128)S(1)} %get-tuple-element.64), channel_id=1, source_target_pairs={{0,8},{8,0},{16,24},{24,16},{1,9},{9,1},{17,25},{25,17},{2,10},{10... | collective-permute-start | bytes 393224 | tf_op jit(solution)/shard_map/ppermute | solution.py:59
  46.3 0.2 collective-permute-done.17.q23
  46.5 2.7 %shard_map.65 = (f32[256,128]{1,0:T(8,128)}, f32[256,128]{1,0:T(8,128)S(1)}) custom-call(s32[8,8]{1,0:T(8,128)S(1)} %copy-done, bf16[512,1024]{1,0:T(8,128)(2,1)S(1)} %get-tuple-element.45.prow, bf16[512,1024]{1,0:T(8,128)(2,1)S(1)} %get-tuple-element.46.hrow, bf16[1024,256]{1,0:T(8,128)(2,1)S(1)} %get-tuple-element.40.pcol, ...), custom_call_target="tpu_custom_call" | custom-call | flops 1610612736 | bytes 9699584 | tf_op jit(solution)/shard_map/pallas_call | solution.py:335
  49.2 0.8 %collective-permute-done.18 = f32[256,128]{1,0:T(8,128)S(1)} collective-permute-done((f32[256,128]{1,0:T(8,128)S(1)}, f32[256,128]{1,0:T(8,128)S(1)}, u32[]{:S(2)}, u32[]{:S(2)}) %collective-permute-start.18) | collective-permute-done | bytes 131104 | tf_op jit(solution)/shard_map/ppermute | solution.py:59
  50.0 0.7 %add.3 = f32[256,128]{1,0:T(8,128)} add(f32[256,128]{1,0:T(8,128)S(1)} %get-tuple-element.63, f32[256,128]{1,0:T(8,128)S(1)} %collective-permute-done.18) | non-fusion elementwise | flops 32768 | bytes 393216 | tf_op jit(solution)/shard_map/add | solution.py:424
  (23 shorter events, 0.3 us)
Async XLA Ops:
  0.6 10.0 %collective-permute-start.5 = (f32[256,128]{1,0:T(8,128)}, f32[256,128]{1,0:T(8,128)S(1)}, u32[]{:S(2)}, u32[]{:S(2)}) collective-permute-start(f32[256,128]{1,0:T(8,128)} %param.3), channel_id=1, source_target_pairs={{0,4},{1,5},{2,6},{3,7},{4,0},{5,1},{6,2},{7,3},{8,12},{9,13},{10,... | collective-permute-start | bytes 393224 | tf_op jit(solution)/shard_map/ppermute | solution.py:59
  3.7 10.1 %collective-permute-start.3 = (f32[256,128]{1,0:T(8,128)}, f32[256,128]{1,0:T(8,128)S(1)}, u32[]{:S(2)}, u32[]{:S(2)}) collective-permute-start(f32[256,128]{1,0:T(8,128)} %param.3), channel_id=1, source_target_pairs={{0,24},{8,16},{16,8},{24,0},{1,25},{9,17},{17,9},{25,1},{2,26},{10... | collective-permute-start | bytes 393224 | tf_op jit(solution)/shard_map/ppermute | solution.py:59
  7.3 5.8 %collective-permute-start = (f32[256,128]{1,0:T(8,128)}, f32[256,128]{1,0:T(8,128)S(1)}, u32[]{:S(2)}, u32[]{:S(2)}) collective-permute-start(f32[256,128]{1,0:T(8,128)} %param.4), channel_id=1, source_target_pairs={{0,2},{1,3},{2,0},{3,1},{4,6},{5,7},{6,4},{7,5},{8,10},{9,11},{10,... | collective-permute-start | bytes 393224 | tf_op jit(solution)/shard_map/ppermute | solution.py:59
  9.8 8.5 %collective-permute-start.2 = (f32[256,128]{1,0:T(8,128)S(1)}, f32[256,128]{1,0:T(8,128)S(1)}, u32[]{:S(2)}, u32[]{:S(2)}) collective-permute-start(f32[256,128]{1,0:T(8,128)S(1)} %get-tuple-element.70.p0), channel_id=1, source_target_pairs={{0,16},{8,24},{16,0},{24,8},{1,17},{9,25},{17,1},{25,9},{2,18},{10... | collective-permute-start | bytes 393224 | tf_op jit(solution)/shard_map/ppermute | solution.py:59
  9.9 8.4 %collective-permute-start.1 = (f32[256,128]{1,0:T(8,128)S(1)}, f32[256,128]{1,0:T(8,128)S(1)}, u32[]{:S(2)}, u32[]{:S(2)}) collective-permute-start(f32[256,128]{1,0:T(8,128)S(1)} %get-tuple-element.70.p0), channel_id=1, source_target_pairs={{0,8},{8,0},{16,24},{24,16},{1,9},{9,1},{17,25},{25,17},{2,10},{10... | collective-permute-start | bytes 393224 | tf_op jit(solution)/shard_map/ppermute | solution.py:59
  10.6 7.6 %collective-permute-start.6 = (f32[512,128]{1,0:T(8,128)S(1)}, f32[512,128]{1,0:T(8,128)S(1)}, u32[]{:S(2)}, u32[]{:S(2)}) collective-permute-start(f32[512,128]{1,0:T(8,128)S(1)} %pad_maximum_fusion.7), channel_id=1, source_target_pairs={{0,2},{1,3},{2,0},{3,1},{4,6},{5,7},{6,4},{7,5},{8,10},{9,11},{10,... | collective-permute-start | bytes 786440 | tf_op jit(solution)/shard_map/ppermute | solution.py:59
  13.1 6.4 %collective-permute-start.4 = (f32[512,128]{1,0:T(8,128)S(1)}, f32[512,128]{1,0:T(8,128)S(1)}, u32[]{:S(2)}, u32[]{:S(2)}) collective-permute-start(f32[512,128]{1,0:T(8,128)S(1)} %pad_maximum_fusion.6), channel_id=1, source_target_pairs={{0,4},{1,5},{2,6},{3,7},{4,0},{5,1},{6,2},{7,3},{8,12},{9,13},{10,... | collective-permute-start | bytes 786440 | tf_op jit(solution)/shard_map/ppermute | solution.py:59
  19.7 2.9 %copy-start = (s32[8,8]{1,0:T(8,128)S(1)}, s32[8,8]{1,0:T(8,128)}, u32[]{:S(2)}) copy-start(s32[8,8]{1,0:T(8,128)} %mask_ref.15) | copy-start | bytes 772
  19.7 4.0 %collective-permute-start.7 = (f32[8,256,128]{2,1,0:T(8,128)S(1)}, f32[8,256,128]{2,1,0:T(8,128)S(1)}, u32[]{:S(2)}, u32[]{:S(2)}) collective-permute-start(f32[8,256,128]{2,1,0:T(8,128)S(1)} %bitcast_dynamic-update-slice_fusion.ss), channel_id=1, source_target_pairs={{0,1},{1,0},{2,3},{3,2},{4,5},{5,4},{6,7},{7,6},{8,9},{9,8},{10,11... | collective-permute-start | bytes 3145736 | tf_op jit(solution)/shard_map/ppermute | solution.py:59
  19.8 7.6 %collective-permute-start.9 = (f32[384,128]{1,0:T(8,128)S(1)}, f32[384,128]{1,0:T(8,128)S(1)}, u32[]{:S(2)}, u32[]{:S(2)}) collective-permute-start(f32[384,128]{1,0:T(8,128)S(1)} %get-tuple-element.71), channel_id=1, source_target_pairs={{0,4},{1,5},{2,6},{3,7},{4,0},{5,1},{6,2},{7,3},{8,12},{9,13},{10,... | collective-permute-start | bytes 589832 | tf_op jit(solution)/shard_map/ppermute | solution.py:59
  20.4 7.5 %collective-permute-start.8 = (f32[384,128]{1,0:T(8,128)S(1)}, f32[384,128]{1,0:T(8,128)S(1)}, u32[]{:S(2)}, u32[]{:S(2)}) collective-permute-start(f32[384,128]{1,0:T(8,128)S(1)} %get-tuple-element.72), channel_id=1, source_target_pairs={{0,2},{1,3},{2,0},{3,1},{4,6},{5,7},{6,4},{7,5},{8,10},{9,11},{10,... | collective-permute-start | bytes 589832 | tf_op jit(solution)/shard_map/ppermute | solution.py:59
  24.6 9.2 %collective-permute-start.14 = (f32[512,128]{1,0:T(8,128)S(1)}, f32[512,128]{1,0:T(8,128)S(1)}, u32[]{:S(2)}, u32[]{:S(2)}) collective-permute-start(f32[512,128]{1,0:T(8,128)S(1)} %get-tuple-element.41.send_ref.q0), channel_id=1, source_target_pairs={{0,16},{24,8},{8,0},{16,24},{1,17},{25,9},{9,1},{17,25},{2,18},{26... | collective-permute-start | bytes 786440 | tf_op jit(solution)/shard_map/ppermute | solution.py:352
  24.7 13.7 %collective-permute-start.13 = (f32[512,128]{1,0:T(8,128)S(1)}, f32[512,128]{1,0:T(8,128)S(1)}, u32[]{:S(2)}, u32[]{:S(2)}) collective-permute-start(f32[512,128]{1,0:T(8,128)S(1)} %get-tuple-element.41.send_ref.q0), channel_id=1, source_target_pairs={{0,8},{24,16},{8,0},{16,24},{1,9},{25,17},{9,1},{17,25},{2,10},{26... | collective-permute-start | bytes 786440 | tf_op jit(solution)/shard_map/ppermute | solution.py:352
  26.7 11.7 %collective-permute-start.12 = (f32[512,128]{1,0:T(8,128)S(1)}, f32[512,128]{1,0:T(8,128)S(1)}, u32[]{:S(2)}, u32[]{:S(2)}) collective-permute-start(f32[512,128]{1,0:T(8,128)S(1)} %get-tuple-element.41.send_ref.q0), channel_id=1, source_target_pairs={{8,16},{16,8},{0,0},{24,24},{9,17},{17,9},{1,1},{25,25},{10,18},{1... | collective-permute-start | bytes 786440 | tf_op jit(solution)/shard_map/ppermute | solution.py:352
  27.9 11.6 %collective-permute-start.11 = (f32[768,128]{1,0:T(8,128)S(1)}, f32[768,128]{1,0:T(8,128)S(1)}, u32[]{:S(2)}, u32[]{:S(2)}) collective-permute-start(f32[768,128]{1,0:T(8,128)S(1)} %pad_maximum_fusion.3), channel_id=1, source_target_pairs={{0,2},{1,3},{2,0},{3,1},{4,6},{5,7},{6,4},{7,5},{8,10},{9,11},{10,... | collective-permute-start | bytes 1179656 | tf_op jit(solution)/shard_map/ppermute | solution.py:59
  29.7 10.3 %collective-permute-start.10 = (f32[768,128]{1,0:T(8,128)S(1)}, f32[768,128]{1,0:T(8,128)S(1)}, u32[]{:S(2)}, u32[]{:S(2)}) collective-permute-start(f32[768,128]{1,0:T(8,128)S(1)} %pad_maximum_fusion.4), channel_id=1, source_target_pairs={{0,4},{1,5},{2,6},{3,7},{4,0},{5,1},{6,2},{7,3},{8,12},{9,13},{10,... | collective-permute-start | bytes 1179656 | tf_op jit(solution)/shard_map/ppermute | solution.py:59
  39.1 7.3 %collective-permute-start.17 = (f32[512,128]{1,0:T(8,128)S(1)}, f32[512,128]{1,0:T(8,128)S(1)}, u32[]{:S(2)}, u32[]{:S(2)}) collective-permute-start(f32[512,128]{1,0:T(8,128)S(1)} %get-tuple-element.59), channel_id=1, source_target_pairs={{0,8},{8,0},{16,24},{24,16},{1,9},{9,1},{17,25},{25,17},{2,10},{10... | collective-permute-start | bytes 786440 | tf_op jit(solution)/shard_map/ppermute | solution.py:59
  40.3 2.4 %collective-permute-start.16 = (f32[2,768,128]{2,1,0:T(8,128)S(1)}, f32[2,768,128]{2,1,0:T(8,128)S(1)}, u32[]{:S(2)}, u32[]{:S(2)}) collective-permute-start(f32[2,768,128]{2,1,0:T(8,128)S(1)} %pad_maximum_fusion.1.hi.s_hi), channel_id=1, source_target_pairs={{0,1},{1,0},{2,3},{3,2},{4,5},{5,4},{6,7},{7,6},{8,9},{9,8},{10,11... | collective-permute-start | bytes 2359304 | tf_op jit(solution)/shard_map/ppermute | solution.py:59
  40.4 3.3 %collective-permute-start.15 = (f32[2,768,128]{2,1,0:T(8,128)S(1)}, f32[2,768,128]{2,1,0:T(8,128)S(1)}, u32[]{:S(2)}, u32[]{:S(2)}) collective-permute-start(f32[2,768,128]{2,1,0:T(8,128)S(1)} %pad_maximum_fusion.lo.s_lo), channel_id=1, source_target_pairs={{0,1},{1,0},{2,3},{3,2},{4,5},{5,4},{6,7},{7,6},{8,9},{9,8},{10,11... | collective-permute-start | bytes 2359304 | tf_op jit(solution)/shard_map/ppermute | solution.py:59
  44.4 5.6 %collective-permute-start.18 = (f32[256,128]{1,0:T(8,128)S(1)}, f32[256,128]{1,0:T(8,128)S(1)}, u32[]{:S(2)}, u32[]{:S(2)}) collective-permute-start(f32[256,128]{1,0:T(8,128)S(1)} %get-tuple-element.64), channel_id=1, source_target_pairs={{0,8},{8,0},{16,24},{24,16},{1,9},{9,1},{17,25},{25,17},{2,10},{10... | collective-permute-start | bytes 393224 | tf_op jit(solution)/shard_map/ppermute | solution.py:59

commit v5 on v4

--- a/solution.py
+++ b/solution.py
@@ -153,7 +153,7 @@
         yield j, [jnp.bitwise_xor(c, 2 * (j + i) + flip) for i in (0, 1)]
 
 
-def start_kernel(mask_ref, p0, p1, p2, p3, ss, part_ref, pcol):
+def start_kernel(mask_ref, p0, p1, p3, p2, ss, part_ref, pcol):
     r, c = lax.axis_index("row"), lax.axis_index("col")
     fill_cols(mask_ref, r, c, (p0[...], p1[...], p2[...], p3[...]), pcol)
     total = jnp.zeros(part_ref.shape, jnp.float32)
@@ -203,7 +203,7 @@
     return jnp.concatenate([part[BAND : 2 * BAND] for part in cols], axis=0)
 
 
-def h_kernel(mask_ref, q3, q1, q2, q0, hcol, across_ref):
+def h_kernel(mask_ref, q0, q1, q3, q2, hcol, across_ref):
     r, c = lax.axis_index("row"), lax.axis_index("col")
     fill_cols(mask_ref, r, c, [ref[BAND:] for ref in (q0, q1, q2, q3)], hcol)
     across_ref[0:BAND] = q3[0:BAND]
@@ -224,22 +224,11 @@
         far[...] = far_rows(cols)
 
 
-def php_of(mask_ref, r, c, parts, prow, qcol):
-    for m, part in enumerate(parts):
-        qcol[m * BAND : (m + 1) * BAND, :] = beside(part)
-    own = pattern_of(mask_ref, band_blocks(r, 0), [c])
-    return dot_parts(prow[...], qcol[...]) * own
-
-
-def own_kernel(
-    mask_ref, hcol, ss, lo, hi, prow, q0, q1, q2, q3, ph_ref, far_lo, far_hi, php_ref, qcol
-):
+def own_kernel(mask_ref, hcol, ss, lo, hi, ph_ref, far_lo, far_hi):
     r, c = lax.axis_index("row"), lax.axis_index("col")
 
     @pl.when(is_middle(r))
     def _():
-        parts = [ref[0:BAND] for ref in (q0, q1, q2, q3)]
-        php_ref[...] = php_of(mask_ref, r, c, parts, prow, qcol)
         ph_ref[...] = jnp.zeros_like(ph_ref)
         for pair, rest, far in zip(pairs(c, 0), (lo, hi), (far_lo, far_hi)):
             add_ph(mask_ref, r, c, pair, ss, rest, hcol, ph_ref, far)
@@ -296,24 +285,30 @@
 
 
 def last_kernel(
-    mask_ref, prow, hrow, pcol, ss, so, s_lo, s_hi, o_lo, o_hi, ph2, send_ref, q1, q23,
-    ph_ref, part_ref, php_ref, grad_ref, qcol, acc,
+    mask_ref, prow, hrow, pcol, ss, so, s_lo, s_hi, o_lo, o_hi, ph2, send_ref, q1, q2, q3, q23,
+    ph_ref, php_ref, grad_ref, qcol, acc,
 ):
     r, c = lax.axis_index("row"), lax.axis_index("col")
     own = pattern_of(mask_ref, band_blocks(r, 0), [c])
     hp = send_ref[0:BAND]
 
+    for m, part in enumerate((hp, q1[0:BAND])):
+        qcol[m * BAND : (m + 1) * BAND, :] = beside(part)
+
     @pl.when(is_middle(r))
     def _():
-        php_ref[...] = part_ref[...]
+        for m, part in ((2, q2[0:BAND]), (3, q3[0:BAND])):
+            qcol[m * BAND : (m + 1) * BAND, :] = beside(part)
         acc[...] = dot_parts(prow[...], ph2[...])
 
     @pl.when(jnp.logical_not(is_middle(r)))
     def _():
-        parts = (hp, q1[0:BAND], q23[0:BAND], q23[BAND:])
-        php_ref[...] = php_of(mask_ref, r, c, parts, prow, qcol)
+        for m, part in ((2, q23[0:BAND]), (3, q23[BAND:])):
+            qcol[m * BAND : (m + 1) * BAND, :] = beside(part)
         acc[...] = jnp.zeros_like(acc)
 
+    php = dot_parts(prow[...], qcol[...]) * own
+    php_ref[...] = php
     acc[...] += dot_parts(stacked(hp), rows_at(r, pcol, [c]))
     for flip, first, rests in ((0, ss, (s_lo, s_hi)), (1, so, (o_lo, o_hi))):
         for j in range(1 - flip, 4):
@@ -326,7 +321,7 @@
                 rows = rows * pattern_of(mask_ref, band_blocks(r, 0), [block])
                 acc[...] += dot_parts(stacked(rows), rows_at(r, pcol, [block]))
 
-    grad_ref[...] = 3.0 * (hp + ph_ref[...]) - 2.0 * (php_ref[...] + own * acc[...])
+    grad_ref[...] = 3.0 * (hp + ph_ref[...]) - 2.0 * (php + own * acc[...])
 
 
 def call(kernel, outs, scratch, flops, *args):
@@ -368,10 +363,11 @@
     p3 = swap(p0, "row", 3)
     both = lax.optimization_barrier(jnp.concatenate([p0, h0], axis=0))
     p0, h0 = both[:rows], both[rows:]
-    p1, p2 = swap(p0, "row", 1), swap(p0, "row", 2)
+    p1 = swap(p0, "row", 1)
+    p2 = swap(p0, "row", 2)
     hy = swap(jnp.concatenate([h0, hx], axis=0), "col", 4)
     px = swap(jnp.concatenate([p0, py], axis=0), "col", 2)
-    p1, p2, p3, hy, px = lax.optimization_barrier((p1, p2, p3, hy, px))
+    px, p1, hy, p2, p3 = lax.optimization_barrier((px, p1, hy, p2, p3))
     ss = jnp.stack([h0, hx, hy[:rows], hy[rows:], p0, px[:rows], py, px[rows:]])
     so = swap(ss, "col", 1)
 
@@ -380,12 +376,12 @@
     upper, lower = b[:half], b[half:]
     ux, ly = swap(upper, "col", 2), swap(lower, "col", 4)
 
-    part, pcol = call(start_kernel, (tile, cols2), [], weight, block_mask, p0, p1, p2, p3, ss)
+    part, pcol = call(start_kernel, (tile, cols2), [], weight, block_mask, p0, p1, p3, p2, ss)
     send, mark = call(
         hp_kernel, (shape(2 * rows, cols, f32), shape(8, cols, f32)), [], weight,
         block_mask, part, pcol, ss, so,
     )
-    ux, ly, mark = lax.optimization_barrier((ux, ly, mark))
+    ly, ux, mark = lax.optimization_barrier((ly, ux, mark))
     q1, q2, q3 = to_middle(send)
     uy = swap(jnp.concatenate([upper, ux], axis=0), "col", 4)
     lx = swap(jnp.concatenate([lower, ly], axis=0), "col", 2)
@@ -394,18 +390,17 @@
     )
     hcol, across = call(
         h_kernel, (cols2, shape(2 * rows, cols, f32)), [], AHEAD * weight,
-        block_mask, q3, q1, q2, send,
+        block_mask, send, q1, q3, q2,
     )
     q23 = swap(across, "row", 1)
-    uy, lx, hcol = lax.optimization_barrier((uy, lx, hcol))
+    lx, uy, hcol = lax.optimization_barrier((lx, uy, hcol))
     s_lo = jnp.stack([b, jnp.concatenate([ux, lx[:half]], axis=0)])
     s_hi = jnp.stack([jnp.concatenate(pair, axis=0) for pair in ((uy[:half], ly), (uy[half:], lx[half:]))])
     o_lo, o_hi = swap(s_lo, "col", 1), swap(s_hi, "col", 1)
 
     far = shape(2 * rows, order // 4)
-    part, own_lo, own_hi, php = call(
-        own_kernel, (strip, far, far, tile), [pltpu.VMEM((order, 2 * cols), bf16)],
-        AHEAD * weight, block_mask, hcol, ss, s_lo, s_hi, prow, send, q1, q2, q3,
+    part, own_lo, own_hi = call(
+        own_kernel, (strip, far, far), [], AHEAD * weight, block_mask, hcol, ss, s_lo, s_hi
     )
     part, other_hi = call(
         other_kernel, (strip, far), [], weight, block_mask, hcol, so, o_hi, part
@@ -419,7 +414,8 @@
     php, grad = call(
         last_kernel, (tile, tile),
         [pltpu.VMEM((order, 2 * cols), bf16), pltpu.VMEM((rows, cols), f32)], weight,
-        block_mask, prow, hrow, pcol, ss, so, s_lo, s_hi, o_lo, o_hi, ph2, send, q1, q23, ph, php,
+        block_mask, prow, hrow, pcol, ss, so, s_lo, s_hi, o_lo, o_hi, ph2, send, q1, q2, q3, q23,
+        ph,
     )
     return hp, php, grad + got
 

time: 51.3 us -> 50.8 us (level)
  starting transfers between devices: 22 us -> 24.3 us
  waiting for transfers between devices: 16.8 us -> 14.6 us
    ppermute x3, starting transfers between devices: 2.74 us -> 5.19 us  [to_middle(): return [lax.ppermute(x, 'row', pairs) for pairs in routes]]
    ppermute x16, waiting for transfers between devices: 11.2 us -> 9.81 us  [swap(): return lax.ppermute(x, axis, [(i, i ^ mask) for i in range(size)])]
    ppermute x3, waiting for transfers between devices: 5.53 us -> 4.79 us  [to_middle(): return [lax.ppermute(x, 'row', pairs) for pairs in routes]]
  transfers between devices with their start and end apart: 19 -> 19, of which waited for: 11 -> 12; matrix products, arithmetic and copies ran while one was open for 3% -> 3% of each run, Pallas kernels for 17% -> 17%
where the time goes in v5:
time: 50.8 us; the launch traced here: 50.6 us
  starting transfers between devices  24.3 us (48%)
  waiting for transfers between devices  14.6 us (29%)
  Pallas kernels  8.72 us (17%)
  other arithmetic  1.99 us (4%)
  between operations  0.89 us (2%)
    ppermute x16, starting transfers between devices, swap(): return lax.ppermute(x, axis, [(i, i ^ mask) for i in range(size)])  19.1 us
    ppermute x16, waiting for transfers between devices, swap(): return lax.ppermute(x, axis, [(i, i ^ mask) for i in range(size)])  9.81 us
    pallas_call x8, Pallas kernels, call(): pl.pallas_call(kernel, out_shape=outs, in_specs=[smem] + [vmem] * (len(ar...  8.72 us
    ppermute x3, starting transfers between devices, to_middle(): return [lax.ppermute(x, 'row', pairs) for pairs in routes]  5.19 us
    ppermute x3, waiting for transfers between devices, to_middle(): return [lax.ppermute(x, 'row', pairs) for pairs in routes]  4.79 us
  transfers between devices with their start and end apart: 19, of which 12 were waited for; matrix products, arithmetic and copies ran while one was open for 3% of the time, Pallas kernels for 17%

profile of v5, /device:TPU:0, one launch (start us, length us, event | category | flops | bytes accessed | tf_op | source)
XLA Modules:
  0.0 50.6 jit_solution(15606499158487374281)
XLA Ops:
  0.6 5.1 %collective-permute-start.6 = (f32[256,128]{1,0:T(8,128)}, f32[256,128]{1,0:T(8,128)S(1)}, u32[]{:S(2)}, u32[]{:S(2)}) collective-permute-start(f32[256,128]{1,0:T(8,128)} %param.3), channel_id=1, source_target_pairs={{0,24},{8,16},{16,8},{24,0},{1,25},{9,17},{17,9},{25,1},{2,26},{10... | collective-permute-start | bytes 393224 | tf_op jit(solution)/shard_map/ppermute | solution.py:59
  5.7 1.5 %collective-permute-start.1 = (f32[256,128]{1,0:T(8,128)}, f32[256,128]{1,0:T(8,128)S(1)}, u32[]{:S(2)}, u32[]{:S(2)}) collective-permute-start(f32[256,128]{1,0:T(8,128)} %param.3), channel_id=1, source_target_pairs={{0,4},{1,5},{2,6},{3,7},{4,0},{5,1},{6,2},{7,3},{8,12},{9,13},{10,... | collective-permute-start | bytes 393224 | tf_op jit(solution)/shard_map/ppermute | solution.py:59
  7.3 1.5 %collective-permute-start = (f32[256,128]{1,0:T(8,128)}, f32[256,128]{1,0:T(8,128)S(1)}, u32[]{:S(2)}, u32[]{:S(2)}) collective-permute-start(f32[256,128]{1,0:T(8,128)} %param.4), channel_id=1, source_target_pairs={{0,2},{1,3},{2,0},{3,1},{4,6},{5,7},{6,4},{7,5},{8,10},{9,11},{10,... | collective-permute-start | bytes 393224 | tf_op jit(solution)/shard_map/ppermute | solution.py:59
  8.8 1.0 %pad_maximum_fusion.5 = f32[512,128]{1,0:T(8,128)S(1)} fusion(f32[256,128]{1,0:T(8,128)} %param.4, f32[256,128]{1,0:T(8,128)} %param.3), kind=kLoop, calls=%fused_computation.9 | loop fusion | flops 65536 | bytes 524288 | tf_op jit(solution)/shard_map/concatenate | solution.py:364
  9.8 0.1 collective-permute-start.5
  9.9 0.8 %collective-permute-start.3 = (f32[256,128]{1,0:T(8,128)S(1)}, f32[256,128]{1,0:T(8,128)S(1)}, u32[]{:S(2)}, u32[]{:S(2)}) collective-permute-start(f32[256,128]{1,0:T(8,128)S(1)} %get-tuple-element.68.p0), channel_id=1, source_target_pairs={{0,8},{8,0},{16,24},{24,16},{1,9},{9,1},{17,25},{25,17},{2,10},{10... | collective-permute-start | bytes 393224 | tf_op jit(solution)/shard_map/ppermute | solution.py:59
  10.6 0.3 collective-permute-done.1
  10.9 1.6 %collective-permute-start.2 = (f32[512,128]{1,0:T(8,128)S(1)}, f32[512,128]{1,0:T(8,128)S(1)}, u32[]{:S(2)}, u32[]{:S(2)}) collective-permute-start(f32[512,128]{1,0:T(8,128)S(1)} %pad_maximum_fusion.6), channel_id=1, source_target_pairs={{0,2},{1,3},{2,0},{3,1},{4,6},{5,7},{6,4},{7,5},{8,10},{9,11},{10,... | collective-permute-start | bytes 786440 | tf_op jit(solution)/shard_map/ppermute | solution.py:59
  12.5 0.1 collective-permute-done
  12.6 1.5 %collective-permute-start.4 = (f32[512,128]{1,0:T(8,128)S(1)}, f32[512,128]{1,0:T(8,128)S(1)}, u32[]{:S(2)}, u32[]{:S(2)}) collective-permute-start(f32[512,128]{1,0:T(8,128)S(1)} %pad_maximum_fusion.7), channel_id=1, source_target_pairs={{0,4},{1,5},{2,6},{3,7},{4,0},{5,1},{6,2},{7,3},{8,12},{9,13},{10,... | collective-permute-start | bytes 786440 | tf_op jit(solution)/shard_map/ppermute | solution.py:59
  14.2 2.9 %collective-permute-done.5.p2 = f32[256,128]{1,0:T(8,128)S(1)} collective-permute-done((f32[256,128]{1,0:T(8,128)S(1)}, f32[256,128]{1,0:T(8,128)S(1)}, u32[]{:S(2)}, u32[]{:S(2)}) %collective-permute-start.5) | collective-permute-done | bytes 131104 | tf_op jit(solution)/shard_map/ppermute | solution.py:59
  17.1 0.0 collective-permute-done.3.p1
  17.1 0.9 %collective-permute-done.2 = f32[512,128]{1,0:T(8,128)S(1)} collective-permute-done((f32[512,128]{1,0:T(8,128)S(1)}, f32[512,128]{1,0:T(8,128)S(1)}, u32[]{:S(2)}, u32[]{:S(2)}) %collective-permute-start.2) | collective-permute-done | bytes 262176 | tf_op jit(solution)/shard_map/ppermute | solution.py:59
  18.1 1.2 %collective-permute-done.4 = f32[512,128]{1,0:T(8,128)S(1)} collective-permute-done((f32[512,128]{1,0:T(8,128)S(1)}, f32[512,128]{1,0:T(8,128)S(1)}, u32[]{:S(2)}, u32[]{:S(2)}) %collective-permute-start.4) | collective-permute-done | bytes 262176 | tf_op jit(solution)/shard_map/ppermute | solution.py:59
  19.3 0.0 copy-start
  19.3 0.1 collective-permute-start.7
  19.5 1.5 %collective-permute-start.9 = (f32[384,128]{1,0:T(8,128)S(1)}, f32[384,128]{1,0:T(8,128)S(1)}, u32[]{:S(2)}, u32[]{:S(2)}) collective-permute-start(f32[384,128]{1,0:T(8,128)S(1)} %get-tuple-element.69), channel_id=1, source_target_pairs={{0,2},{1,3},{2,0},{3,1},{4,6},{5,7},{6,4},{7,5},{8,10},{9,11},{10,... | collective-permute-start | bytes 589832 | tf_op jit(solution)/shard_map/ppermute | solution.py:59
  21.0 0.6 %collective-permute-start.8 = (f32[384,128]{1,0:T(8,128)S(1)}, f32[384,128]{1,0:T(8,128)S(1)}, u32[]{:S(2)}, u32[]{:S(2)}) collective-permute-start(f32[384,128]{1,0:T(8,128)S(1)} %get-tuple-element.70), channel_id=1, source_target_pairs={{0,4},{1,5},{2,6},{3,7},{4,0},{5,1},{6,2},{7,3},{8,12},{9,13},{10,... | collective-permute-start | bytes 589832 | tf_op jit(solution)/shard_map/ppermute | solution.py:59
  21.6 1.0 %shard_map.58 = (f32[256,128]{1,0:T(8,128)S(1)}, bf16[1024,256]{1,0:T(8,128)(2,1)S(1)}) custom-call(s32[8,8]{1,0:T(8,128)S(1)} %copy-done, f32[256,128]{1,0:T(8,128)S(1)} %get-tuple-element.68.p0, f32[256,128]{1,0:T(8,128)S(1)} %collective-permute-done.3.p1, f32[256,128]{1,0:T(8,128)S(1)} %collective-permute-done.6.p3, ...), custom_call_target="tpu_custom_call" | custom-call | flops 1610612736 | bytes 2228480 | tf_op jit(solution)/shard_map/pallas_call | solution.py:330
  22.6 0.0 collective-permute-done.7.so
  22.6 0.9 %shard_map.59 = (f32[512,128]{1,0:T(8,128)S(1)}, f32[8,128]{1,0:T(8,128)S(1)}) custom-call(s32[8,8]{1,0:T(8,128)S(1)} %copy-done, f32[256,128]{1,0:T(8,128)S(1)} %get-tuple-element.38.part_ref, bf16[1024,256]{1,0:T(8,128)(2,1)S(1)} %get-tuple-element.39.pcol, f32[8,256,128]{2,1,0:T(8,128)S(1)} %bitcast_dynamic-update-slice_fusion.ss, ...), custom_call_target="tpu_custom_call" | custom-call | flops 1610612736 | bytes 3019008 | tf_op jit(solution)/shard_map/pallas_call | solution.py:330
  23.6 0.9 %collective-permute-start.14 = (f32[512,128]{1,0:T(8,128)S(1)}, f32[512,128]{1,0:T(8,128)S(1)}, u32[]{:S(2)}, u32[]{:S(2)}) collective-permute-start(f32[512,128]{1,0:T(8,128)S(1)} %get-tuple-element.40.send_ref.q0), channel_id=1, source_target_pairs={{0,16},{24,8},{8,0},{16,24},{1,17},{25,9},{9,1},{17,25},{2,18},{26... | collective-permute-start | bytes 786440 | tf_op jit(solution)/shard_map/ppermute | solution.py:347
  24.5 0.7 %collective-permute-start.13 = (f32[512,128]{1,0:T(8,128)S(1)}, f32[512,128]{1,0:T(8,128)S(1)}, u32[]{:S(2)}, u32[]{:S(2)}) collective-permute-start(f32[512,128]{1,0:T(8,128)S(1)} %get-tuple-element.40.send_ref.q0), channel_id=1, source_target_pairs={{8,16},{16,8},{0,0},{24,24},{9,17},{17,9},{1,1},{25,25},{10,18},{1... | collective-permute-start | bytes 786440 | tf_op jit(solution)/shard_map/ppermute | solution.py:347
  25.2 3.6 %collective-permute-start.12 = (f32[512,128]{1,0:T(8,128)S(1)}, f32[512,128]{1,0:T(8,128)S(1)}, u32[]{:S(2)}, u32[]{:S(2)}) collective-permute-start(f32[512,128]{1,0:T(8,128)S(1)} %get-tuple-element.40.send_ref.q0), channel_id=1, source_target_pairs={{0,8},{24,16},{8,0},{16,24},{1,9},{25,17},{9,1},{17,25},{2,10},{26... | collective-permute-start | bytes 786440 | tf_op jit(solution)/shard_map/ppermute | solution.py:347
  28.8 0.0 collective-permute-done.9
  28.8 1.0 %collective-permute-start.10 = (f32[768,128]{1,0:T(8,128)S(1)}, f32[768,128]{1,0:T(8,128)S(1)}, u32[]{:S(2)}, u32[]{:S(2)}) collective-permute-start(f32[768,128]{1,0:T(8,128)S(1)} %pad_maximum_fusion.3), channel_id=1, source_target_pairs={{0,2},{1,3},{2,0},{3,1},{4,6},{5,7},{6,4},{7,5},{8,10},{9,11},{10,... | collective-permute-start | bytes 1179656 | tf_op jit(solution)/shard_map/ppermute | solution.py:59
  29.9 1.2 %collective-permute-start.11 = (f32[768,128]{1,0:T(8,128)S(1)}, f32[768,128]{1,0:T(8,128)S(1)}, u32[]{:S(2)}, u32[]{:S(2)}) collective-permute-start(f32[768,128]{1,0:T(8,128)S(1)} %pad_maximum_fusion.4), channel_id=1, source_target_pairs={{0,4},{1,5},{2,6},{3,7},{4,0},{5,1},{6,2},{7,3},{8,12},{9,13},{10,... | collective-permute-start | bytes 1179656 | tf_op jit(solution)/shard_map/ppermute | solution.py:59
  31.0 1.6 %shard_map.60 = (bf16[512,1024]{1,0:T(8,128)(2,1)S(1)}, bf16[512,1024]{1,0:T(8,128)(2,1)S(1)}, f32[256,128]{1,0:T(8,128)}) custom-call(s32[8,8]{1,0:T(8,128)S(1)} %copy-done, f32[8,256,128]{2,1,0:T(8,128)S(1)} %bitcast_dynamic-update-slice_fusion.ss, f32[8,256,128]{2,1,0:T(8,128)S(1)} %collective-permute-done.7.so, ...), custom_call_target="tpu_custom_call" | custom-call | flops 1610612736 | bytes 4591872 | tf_op jit(solution)/shard_map/pallas_call | solution.py:330
  32.6 0.2 collective-permute-done.14.q2
  32.8 4.6 %collective-permute-done.12.q1 = f32[512,128]{1,0:T(8,128)S(1)} collective-permute-done((f32[512,128]{1,0:T(8,128)S(1)}, f32[512,128]{1,0:T(8,128)S(1)}, u32[]{:S(2)}, u32[]{:S(2)}) %collective-permute-start.12) | collective-permute-done | bytes 262176 | tf_op jit(solution)/shard_map/ppermute | solution.py:347
  37.4 0.7 %shard_map.61 = (bf16[1024,256]{1,0:T(8,128)(2,1)S(1)}, f32[512,128]{1,0:T(8,128)S(1)}) custom-call(s32[8,8]{1,0:T(8,128)S(1)} %copy-done, f32[512,128]{1,0:T(8,128)S(1)} %get-tuple-element.40.send_ref.q0, f32[512,128]{1,0:T(8,128)S(1)} %collective-permute-done.12.q1, f32[512,128]{1,0:T(8,128)S(1)} %collective-permute-done.13.q3, ...), custom_call_target="tpu_custom_call" | custom-call | flops 12884901888 | bytes 1835264 | tf_op jit(solution)/shard_map/pallas_call | solution.py:330
  38.1 1.0 %collective-permute-start.17 = (f32[512,128]{1,0:T(8,128)S(1)}, f32[512,128]{1,0:T(8,128)S(1)}, u32[]{:S(2)}, u32[]{:S(2)}) collective-permute-start(f32[512,128]{1,0:T(8,128)S(1)} %get-tuple-element.58), channel_id=1, source_target_pairs={{0,8},{8,0},{16,24},{24,16},{1,9},{9,1},{17,25},{25,17},{2,10},{10... | collective-permute-start | bytes 786440 | tf_op jit(solution)/shard_map/ppermute | solution.py:59
  39.1 0.9 %collective-permute-done.11 = f32[768,128]{1,0:T(8,128)S(1)} collective-permute-done((f32[768,128]{1,0:T(8,128)S(1)}, f32[768,128]{1,0:T(8,128)S(1)}, u32[]{:S(2)}, u32[]{:S(2)}) %collective-permute-start.11) | collective-permute-done | bytes 393248 | tf_op jit(solution)/shard_map/ppermute | solution.py:59
  40.0 0.1 fusion.1
  40.1 0.1 pad_maximum_fusion.1.hi.s_hi
  40.2 0.1 collective-permute-start.16
  40.3 0.1 pad_maximum_fusion.lo.s_lo
  40.3 0.6 %collective-permute-start.15 = (f32[2,768,128]{2,1,0:T(8,128)S(1)}, f32[2,768,128]{2,1,0:T(8,128)S(1)}, u32[]{:S(2)}, u32[]{:S(2)}) collective-permute-start(f32[2,768,128]{2,1,0:T(8,128)S(1)} %pad_maximum_fusion.lo.s_lo), channel_id=1, source_target_pairs={{0,1},{1,0},{2,3},{3,2},{4,5},{5,4},{6,7},{7,6},{8,9},{9,8},{10,11... | collective-permute-start | bytes 2359304 | tf_op jit(solution)/shard_map/ppermute | solution.py:59
  40.9 0.6 %shard_map.62 = (f32[1024,128]{1,0:T(8,128)S(1)}, bf16[512,256]{1,0:T(8,128)(2,1)S(1)}, bf16[512,256]{1,0:T(8,128)(2,1)S(1)}) custom-call(s32[8,8]{1,0:T(8,128)S(1)} %copy-done, bf16[1024,256]{1,0:T(8,128)(2,1)S(1)} %get-tuple-element.51.hcol, f32[8,256,128]{2,1,0:T(8,128)S(1)} %bitcast_dynamic-update-slice_fusion.ss, ...), custom_call_target="tpu_custom_call" | custom-call | flops 12884901888 | bytes 4194560 | tf_op jit(solution)/shard_map/pallas_call | solution.py:330
  41.5 1.0 %collective-permute-done.16.hi.o_hi = f32[2,768,128]{2,1,0:T(8,128)S(1)} collective-permute-done((f32[2,768,128]{2,1,0:T(8,128)S(1)}, f32[2,768,128]{2,1,0:T(8,128)S(1)}, u32[]{:S(2)}, u32[]{:S(2)}) %collective-permute-start.16) | collective-permute-done | bytes 786464 | tf_op jit(solution)/shard_map/ppermute | solution.py:59
  42.6 0.6 %shard_map.63 = (f32[1024,128]{1,0:T(8,128)S(1)}, bf16[512,256]{1,0:T(8,128)(2,1)S(1)}) custom-call(s32[8,8]{1,0:T(8,128)S(1)} %copy-done, bf16[1024,256]{1,0:T(8,128)(2,1)S(1)} %get-tuple-element.51.hcol, f32[8,256,128]{2,1,0:T(8,128)S(1)} %collective-permute-done.7.so, f32[2,768,128]{2,1,0:T(8,128)S(1)} %collective-permute-done.16.hi.o_hi, ...), custom_call_target="tpu_custom_call" | custom-call | flops 1610612736 | bytes 3670272 | tf_op jit(solution)/shard_map/pallas_call | solution.py:330
  43.2 0.5 collective-permute-done.15.lo.o_lo
  43.7 0.7 %shard_map.64 = (f32[256,128]{1,0:T(8,128)S(1)}, f32[256,128]{1,0:T(8,128)S(1)}, bf16[1024,256]{1,0:T(8,128)(2,1)S(1)}) custom-call(s32[8,8]{1,0:T(8,128)S(1)} %copy-done, bf16[1024,256]{1,0:T(8,128)(2,1)S(1)} %get-tuple-element.51.hcol, f32[8,256,128]{2,1,0:T(8,128)S(1)} %collective-permute-done.7.so, f32[2,768,128]{2,1,0:T(8,128)S(1)} %collective-permute-done.15.lo.o_lo, ...), custom_call_target="tpu_custom_call" | custom-call | flops 1610612736 | bytes 4456704 | tf_op jit(solution)/shard_map/pallas_call | solution.py:330
  44.3 1.0 %collective-permute-start.18 = (f32[256,128]{1,0:T(8,128)S(1)}, f32[256,128]{1,0:T(8,128)S(1)}, u32[]{:S(2)}, u32[]{:S(2)}) collective-permute-start(f32[256,128]{1,0:T(8,128)S(1)} %get-tuple-element.62), channel_id=1, source_target_pairs={{0,8},{8,0},{16,24},{24,16},{1,9},{9,1},{17,25},{25,17},{2,10},{10... | collective-permute-start | bytes 393224 | tf_op jit(solution)/shard_map/ppermute | solution.py:59
  45.3 0.3 collective-permute-done.17.q23
  45.6 2.6 %shard_map.65 = (f32[256,128]{1,0:T(8,128)}, f32[256,128]{1,0:T(8,128)S(1)}) custom-call(s32[8,8]{1,0:T(8,128)S(1)} %copy-done, bf16[512,1024]{1,0:T(8,128)(2,1)S(1)} %get-tuple-element.44.prow, bf16[512,1024]{1,0:T(8,128)(2,1)S(1)} %get-tuple-element.45.hrow, bf16[1024,256]{1,0:T(8,128)(2,1)S(1)} %get-tuple-element.39.pcol, ...), custom_call_target="tpu_custom_call" | custom-call | flops 1610612736 | bytes 10092800 | tf_op jit(solution)/shard_map/pallas_call | solution.py:330
  48.2 1.7 %collective-permute-done.18 = f32[256,128]{1,0:T(8,128)S(1)} collective-permute-done((f32[256,128]{1,0:T(8,128)S(1)}, f32[256,128]{1,0:T(8,128)S(1)}, u32[]{:S(2)}, u32[]{:S(2)}) %collective-permute-start.18) | collective-permute-done | bytes 131104 | tf_op jit(solution)/shard_map/ppermute | solution.py:59
  49.9 0.7 %add.3 = f32[256,128]{1,0:T(8,128)} add(f32[256,128]{1,0:T(8,128)S(1)} %get-tuple-element.61, f32[256,128]{1,0:T(8,128)S(1)} %collective-permute-done.18) | non-fusion elementwise | flops 32768 | bytes 393216 | tf_op jit(solution)/shard_map/add | solution.py:420
  (23 shorter events, 0.4 us)
Async XLA Ops:
  0.6 13.5 %collective-permute-start.6 = (f32[256,128]{1,0:T(8,128)}, f32[256,128]{1,0:T(8,128)S(1)}, u32[]{:S(2)}, u32[]{:S(2)}) collective-permute-start(f32[256,128]{1,0:T(8,128)} %param.3), channel_id=1, source_target_pairs={{0,24},{8,16},{16,8},{24,0},{1,25},{9,17},{17,9},{25,1},{2,26},{10... | collective-permute-start | bytes 393224 | tf_op jit(solution)/shard_map/ppermute | solution.py:59
  5.7 5.2 %collective-permute-start.1 = (f32[256,128]{1,0:T(8,128)}, f32[256,128]{1,0:T(8,128)S(1)}, u32[]{:S(2)}, u32[]{:S(2)}) collective-permute-start(f32[256,128]{1,0:T(8,128)} %param.3), channel_id=1, source_target_pairs={{0,4},{1,5},{2,6},{3,7},{4,0},{5,1},{6,2},{7,3},{8,12},{9,13},{10,... | collective-permute-start | bytes 393224 | tf_op jit(solution)/shard_map/ppermute | solution.py:59
  7.3 5.3 %collective-permute-start = (f32[256,128]{1,0:T(8,128)}, f32[256,128]{1,0:T(8,128)S(1)}, u32[]{:S(2)}, u32[]{:S(2)}) collective-permute-start(f32[256,128]{1,0:T(8,128)} %param.4), channel_id=1, source_target_pairs={{0,2},{1,3},{2,0},{3,1},{4,6},{5,7},{6,4},{7,5},{8,10},{9,11},{10,... | collective-permute-start | bytes 393224 | tf_op jit(solution)/shard_map/ppermute | solution.py:59
  9.8 7.3 %collective-permute-start.5 = (f32[256,128]{1,0:T(8,128)S(1)}, f32[256,128]{1,0:T(8,128)S(1)}, u32[]{:S(2)}, u32[]{:S(2)}) collective-permute-start(f32[256,128]{1,0:T(8,128)S(1)} %get-tuple-element.68.p0), channel_id=1, source_target_pairs={{0,16},{8,24},{16,0},{24,8},{1,17},{9,25},{17,1},{25,9},{2,18},{10... | collective-permute-start | bytes 393224 | tf_op jit(solution)/shard_map/ppermute | solution.py:59
  9.9 7.3 %collective-permute-start.3 = (f32[256,128]{1,0:T(8,128)S(1)}, f32[256,128]{1,0:T(8,128)S(1)}, u32[]{:S(2)}, u32[]{:S(2)}) collective-permute-start(f32[256,128]{1,0:T(8,128)S(1)} %get-tuple-element.68.p0), channel_id=1, source_target_pairs={{0,8},{8,0},{16,24},{24,16},{1,9},{9,1},{17,25},{25,17},{2,10},{10... | collective-permute-start | bytes 393224 | tf_op jit(solution)/shard_map/ppermute | solution.py:59
  10.9 7.1 %collective-permute-start.2 = (f32[512,128]{1,0:T(8,128)S(1)}, f32[512,128]{1,0:T(8,128)S(1)}, u32[]{:S(2)}, u32[]{:S(2)}) collective-permute-start(f32[512,128]{1,0:T(8,128)S(1)} %pad_maximum_fusion.6), channel_id=1, source_target_pairs={{0,2},{1,3},{2,0},{3,1},{4,6},{5,7},{6,4},{7,5},{8,10},{9,11},{10,... | collective-permute-start | bytes 786440 | tf_op jit(solution)/shard_map/ppermute | solution.py:59
  12.6 6.6 %collective-permute-start.4 = (f32[512,128]{1,0:T(8,128)S(1)}, f32[512,128]{1,0:T(8,128)S(1)}, u32[]{:S(2)}, u32[]{:S(2)}) collective-permute-start(f32[512,128]{1,0:T(8,128)S(1)} %pad_maximum_fusion.7), channel_id=1, source_target_pairs={{0,4},{1,5},{2,6},{3,7},{4,0},{5,1},{6,2},{7,3},{8,12},{9,13},{10,... | collective-permute-start | bytes 786440 | tf_op jit(solution)/shard_map/ppermute | solution.py:59
  19.3 2.2 %copy-start = (s32[8,8]{1,0:T(8,128)S(1)}, s32[8,8]{1,0:T(8,128)}, u32[]{:S(2)}) copy-start(s32[8,8]{1,0:T(8,128)} %mask_ref.15) | copy-start | bytes 772
  19.3 3.3 %collective-permute-start.7 = (f32[8,256,128]{2,1,0:T(8,128)S(1)}, f32[8,256,128]{2,1,0:T(8,128)S(1)}, u32[]{:S(2)}, u32[]{:S(2)}) collective-permute-start(f32[8,256,128]{2,1,0:T(8,128)S(1)} %bitcast_dynamic-update-slice_fusion.ss), channel_id=1, source_target_pairs={{0,1},{1,0},{2,3},{3,2},{4,5},{5,4},{6,7},{7,6},{8,9},{9,8},{10,11... | collective-permute-start | bytes 3145736 | tf_op jit(solution)/shard_map/ppermute | solution.py:59
  19.5 9.3 %collective-permute-start.9 = (f32[384,128]{1,0:T(8,128)S(1)}, f32[384,128]{1,0:T(8,128)S(1)}, u32[]{:S(2)}, u32[]{:S(2)}) collective-permute-start(f32[384,128]{1,0:T(8,128)S(1)} %get-tuple-element.69), channel_id=1, source_target_pairs={{0,2},{1,3},{2,0},{3,1},{4,6},{5,7},{6,4},{7,5},{8,10},{9,11},{10,... | collective-permute-start | bytes 589832 | tf_op jit(solution)/shard_map/ppermute | solution.py:59
  21.0 7.8 %collective-permute-start.8 = (f32[384,128]{1,0:T(8,128)S(1)}, f32[384,128]{1,0:T(8,128)S(1)}, u32[]{:S(2)}, u32[]{:S(2)}) collective-permute-start(f32[384,128]{1,0:T(8,128)S(1)} %get-tuple-element.70), channel_id=1, source_target_pairs={{0,4},{1,5},{2,6},{3,7},{4,0},{5,1},{6,2},{7,3},{8,12},{9,13},{10,... | collective-permute-start | bytes 589832 | tf_op jit(solution)/shard_map/ppermute | solution.py:59
  23.6 9.2 %collective-permute-start.14 = (f32[512,128]{1,0:T(8,128)S(1)}, f32[512,128]{1,0:T(8,128)S(1)}, u32[]{:S(2)}, u32[]{:S(2)}) collective-permute-start(f32[512,128]{1,0:T(8,128)S(1)} %get-tuple-element.40.send_ref.q0), channel_id=1, source_target_pairs={{0,16},{24,8},{8,0},{16,24},{1,17},{25,9},{9,1},{17,25},{2,18},{26... | collective-permute-start | bytes 786440 | tf_op jit(solution)/shard_map/ppermute | solution.py:347
  24.5 8.3 %collective-permute-start.13 = (f32[512,128]{1,0:T(8,128)S(1)}, f32[512,128]{1,0:T(8,128)S(1)}, u32[]{:S(2)}, u32[]{:S(2)}) collective-permute-start(f32[512,128]{1,0:T(8,128)S(1)} %get-tuple-element.40.send_ref.q0), channel_id=1, source_target_pairs={{8,16},{16,8},{0,0},{24,24},{9,17},{17,9},{1,1},{25,25},{10,18},{1... | collective-permute-start | bytes 786440 | tf_op jit(solution)/shard_map/ppermute | solution.py:347
  25.2 12.2 %collective-permute-start.12 = (f32[512,128]{1,0:T(8,128)S(1)}, f32[512,128]{1,0:T(8,128)S(1)}, u32[]{:S(2)}, u32[]{:S(2)}) collective-permute-start(f32[512,128]{1,0:T(8,128)S(1)} %get-tuple-element.40.send_ref.q0), channel_id=1, source_target_pairs={{0,8},{24,16},{8,0},{16,24},{1,9},{25,17},{9,1},{17,25},{2,10},{26... | collective-permute-start | bytes 786440 | tf_op jit(solution)/shard_map/ppermute | solution.py:347
  28.8 10.3 %collective-permute-start.10 = (f32[768,128]{1,0:T(8,128)S(1)}, f32[768,128]{1,0:T(8,128)S(1)}, u32[]{:S(2)}, u32[]{:S(2)}) collective-permute-start(f32[768,128]{1,0:T(8,128)S(1)} %pad_maximum_fusion.3), channel_id=1, source_target_pairs={{0,2},{1,3},{2,0},{3,1},{4,6},{5,7},{6,4},{7,5},{8,10},{9,11},{10,... | collective-permute-start | bytes 1179656 | tf_op jit(solution)/shard_map/ppermute | solution.py:59
  29.9 10.1 %collective-permute-start.11 = (f32[768,128]{1,0:T(8,128)S(1)}, f32[768,128]{1,0:T(8,128)S(1)}, u32[]{:S(2)}, u32[]{:S(2)}) collective-permute-start(f32[768,128]{1,0:T(8,128)S(1)} %pad_maximum_fusion.4), channel_id=1, source_target_pairs={{0,4},{1,5},{2,6},{3,7},{4,0},{5,1},{6,2},{7,3},{8,12},{9,13},{10,... | collective-permute-start | bytes 1179656 | tf_op jit(solution)/shard_map/ppermute | solution.py:59
  38.1 7.5 %collective-permute-start.17 = (f32[512,128]{1,0:T(8,128)S(1)}, f32[512,128]{1,0:T(8,128)S(1)}, u32[]{:S(2)}, u32[]{:S(2)}) collective-permute-start(f32[512,128]{1,0:T(8,128)S(1)} %get-tuple-element.58), channel_id=1, source_target_pairs={{0,8},{8,0},{16,24},{24,16},{1,9},{9,1},{17,25},{25,17},{2,10},{10... | collective-permute-start | bytes 786440 | tf_op jit(solution)/shard_map/ppermute | solution.py:59
  40.2 2.4 %collective-permute-start.16 = (f32[2,768,128]{2,1,0:T(8,128)S(1)}, f32[2,768,128]{2,1,0:T(8,128)S(1)}, u32[]{:S(2)}, u32[]{:S(2)}) collective-permute-start(f32[2,768,128]{2,1,0:T(8,128)S(1)} %pad_maximum_fusion.1.hi.s_hi), channel_id=1, source_target_pairs={{0,1},{1,0},{2,3},{3,2},{4,5},{5,4},{6,7},{7,6},{8,9},{9,8},{10,11... | collective-permute-start | bytes 2359304 | tf_op jit(solution)/shard_map/ppermute | solution.py:59
  40.3 3.3 %collective-permute-start.15 = (f32[2,768,128]{2,1,0:T(8,128)S(1)}, f32[2,768,128]{2,1,0:T(8,128)S(1)}, u32[]{:S(2)}, u32[]{:S(2)}) collective-permute-start(f32[2,768,128]{2,1,0:T(8,128)S(1)} %pad_maximum_fusion.lo.s_lo), channel_id=1, source_target_pairs={{0,1},{1,0},{2,3},{3,2},{4,5},{5,4},{6,7},{7,6},{8,9},{9,8},{10,11... | collective-permute-start | bytes 2359304 | tf_op jit(solution)/shard_map/ppermute | solution.py:59
  44.3 5.6 %collective-permute-start.18 = (f32[256,128]{1,0:T(8,128)S(1)}, f32[256,128]{1,0:T(8,128)S(1)}, u32[]{:S(2)}, u32[]{:S(2)}) collective-permute-start(f32[256,128]{1,0:T(8,128)S(1)} %get-tuple-element.62), channel_id=1, source_target_pairs={{0,8},{8,0},{16,24},{24,16},{1,9},{9,1},{17,25},{25,17},{2,10},{10... | collective-permute-start | bytes 393224 | tf_op jit(solution)/shard_map/ppermute | solution.py:59

commit v6 on v5

--- a/solution.py
+++ b/solution.py
@@ -314,7 +314,9 @@
         for j in range(1 - flip, 4):
             block = jnp.bitwise_xor(c, 2 * j + flip)
 
-            @pl.when(mask_ref[block, c] != 0)
+            met = any_live(mask_ref, band_blocks(r, 0), block)
+
+            @pl.when(jnp.logical_and(mask_ref[block, c] != 0, met))
             def _(first=first, rest=rests[j // 2], j=j, block=block):
                 cols = column(mask_ref, r, block, j, first, rest)
                 rows = dot_parts(hrow[...], cols)

time: 50.8 us -> 50.8 us (level)
  waiting for transfers between devices: 14.6 us -> 13.2 us
  Pallas kernels: 8.72 us -> 9.44 us
  starting transfers between devices: 24.3 us -> 24.9 us
    ppermute x16, waiting for transfers between devices: 9.81 us -> 8.4 us  [swap(): return lax.ppermute(x, axis, [(i, i ^ mask) for i in range(size)])]
    pallas_call x8, Pallas kernels: 8.72 us -> 9.44 us  [call(): pl.pallas_call(kernel, out_shape=outs, in_specs=[smem] + [vmem] * (len(ar...]
    ppermute x16, starting transfers between devices: 19.1 us -> 19.7 us  [swap(): return lax.ppermute(x, axis, [(i, i ^ mask) for i in range(size)])]
  transfers between devices with their start and end apart: 19 -> 19, of which waited for: 12 -> 11; matrix products, arithmetic and copies ran while one was open for 3% -> 3% of each run, Pallas kernels for 17% -> 19%
where the time goes in v6:
time: 50.8 us; the launch traced here: 50.6 us
  starting transfers between devices  24.9 us (49%)
  waiting for transfers between devices  13.2 us (26%)
  Pallas kernels  9.44 us (19%)
  other arithmetic  1.99 us (4%)
  between operations  0.89 us (2%)
    ppermute x16, starting transfers between devices, swap(): return lax.ppermute(x, axis, [(i, i ^ mask) for i in range(size)])  19.7 us
    pallas_call x8, Pallas kernels, call(): pl.pallas_call(kernel, out_shape=outs, in_specs=[smem] + [vmem] * (len(ar...  9.44 us
    ppermute x16, waiting for transfers between devices, swap(): return lax.ppermute(x, axis, [(i, i ^ mask) for i in range(size)])  8.4 us
    ppermute x3, starting transfers between devices, to_middle(): return [lax.ppermute(x, 'row', pairs) for pairs in routes]  5.19 us
    ppermute x3, waiting for transfers between devices, to_middle(): return [lax.ppermute(x, 'row', pairs) for pairs in routes]  4.79 us
  transfers between devices with their start and end apart: 19, of which 11 were waited for; matrix products, arithmetic and copies ran while one was open for 3% of the time, Pallas kernels for 19%

profile of v6, /device:TPU:0, one launch (start us, length us, event | category | flops | bytes accessed | tf_op | source)
XLA Modules:
  0.0 50.6 jit_solution(3052602030226406071)
XLA Ops:
  0.6 5.1 %collective-permute-start.6 = (f32[256,128]{1,0:T(8,128)}, f32[256,128]{1,0:T(8,128)S(1)}, u32[]{:S(2)}, u32[]{:S(2)}) collective-permute-start(f32[256,128]{1,0:T(8,128)} %param.3), channel_id=1, source_target_pairs={{0,24},{8,16},{16,8},{24,0},{1,25},{9,17},{17,9},{25,1},{2,26},{10... | collective-permute-start | bytes 393224 | tf_op jit(solution)/shard_map/ppermute | solution.py:59
  5.7 1.5 %collective-permute-start.1 = (f32[256,128]{1,0:T(8,128)}, f32[256,128]{1,0:T(8,128)S(1)}, u32[]{:S(2)}, u32[]{:S(2)}) collective-permute-start(f32[256,128]{1,0:T(8,128)} %param.3), channel_id=1, source_target_pairs={{0,4},{1,5},{2,6},{3,7},{4,0},{5,1},{6,2},{7,3},{8,12},{9,13},{10,... | collective-permute-start | bytes 393224 | tf_op jit(solution)/shard_map/ppermute | solution.py:59
  7.3 1.5 %collective-permute-start = (f32[256,128]{1,0:T(8,128)}, f32[256,128]{1,0:T(8,128)S(1)}, u32[]{:S(2)}, u32[]{:S(2)}) collective-permute-start(f32[256,128]{1,0:T(8,128)} %param.4), channel_id=1, source_target_pairs={{0,2},{1,3},{2,0},{3,1},{4,6},{5,7},{6,4},{7,5},{8,10},{9,11},{10,... | collective-permute-start | bytes 393224 | tf_op jit(solution)/shard_map/ppermute | solution.py:59
  8.8 1.0 %pad_maximum_fusion.5 = f32[512,128]{1,0:T(8,128)S(1)} fusion(f32[256,128]{1,0:T(8,128)} %param.4, f32[256,128]{1,0:T(8,128)} %param.3), kind=kLoop, calls=%fused_computation.9 | loop fusion | flops 65536 | bytes 524288 | tf_op jit(solution)/shard_map/concatenate | solution.py:366
  9.8 0.1 collective-permute-start.5
  9.9 0.8 %collective-permute-start.3 = (f32[256,128]{1,0:T(8,128)S(1)}, f32[256,128]{1,0:T(8,128)S(1)}, u32[]{:S(2)}, u32[]{:S(2)}) collective-permute-start(f32[256,128]{1,0:T(8,128)S(1)} %get-tuple-element.68.p0), channel_id=1, source_target_pairs={{0,8},{8,0},{16,24},{24,16},{1,9},{9,1},{17,25},{25,17},{2,10},{10... | collective-permute-start | bytes 393224 | tf_op jit(solution)/shard_map/ppermute | solution.py:59
  10.6 0.3 collective-permute-done.1
  10.9 1.6 %collective-permute-start.2 = (f32[512,128]{1,0:T(8,128)S(1)}, f32[512,128]{1,0:T(8,128)S(1)}, u32[]{:S(2)}, u32[]{:S(2)}) collective-permute-start(f32[512,128]{1,0:T(8,128)S(1)} %pad_maximum_fusion.6), channel_id=1, source_target_pairs={{0,2},{1,3},{2,0},{3,1},{4,6},{5,7},{6,4},{7,5},{8,10},{9,11},{10,... | collective-permute-start | bytes 786440 | tf_op jit(solution)/shard_map/ppermute | solution.py:59
  12.5 0.1 collective-permute-done
  12.6 1.5 %collective-permute-start.4 = (f32[512,128]{1,0:T(8,128)S(1)}, f32[512,128]{1,0:T(8,128)S(1)}, u32[]{:S(2)}, u32[]{:S(2)}) collective-permute-start(f32[512,128]{1,0:T(8,128)S(1)} %pad_maximum_fusion.7), channel_id=1, source_target_pairs={{0,4},{1,5},{2,6},{3,7},{4,0},{5,1},{6,2},{7,3},{8,12},{9,13},{10,... | collective-permute-start | bytes 786440 | tf_op jit(solution)/shard_map/ppermute | solution.py:59
  14.1 0.0 collective-permute-done.6.p3
  14.2 2.9 %collective-permute-done.5.p2 = f32[256,128]{1,0:T(8,128)S(1)} collective-permute-done((f32[256,128]{1,0:T(8,128)S(1)}, f32[256,128]{1,0:T(8,128)S(1)}, u32[]{:S(2)}, u32[]{:S(2)}) %collective-permute-start.5) | collective-permute-done | bytes 131104 | tf_op jit(solution)/shard_map/ppermute | solution.py:59
  17.1 0.0 collective-permute-done.3.p1
  17.1 0.9 %collective-permute-done.2 = f32[512,128]{1,0:T(8,128)S(1)} collective-permute-done((f32[512,128]{1,0:T(8,128)S(1)}, f32[512,128]{1,0:T(8,128)S(1)}, u32[]{:S(2)}, u32[]{:S(2)}) %collective-permute-start.2) | collective-permute-done | bytes 262176 | tf_op jit(solution)/shard_map/ppermute | solution.py:59
  18.1 1.2 %collective-permute-done.4 = f32[512,128]{1,0:T(8,128)S(1)} collective-permute-done((f32[512,128]{1,0:T(8,128)S(1)}, f32[512,128]{1,0:T(8,128)S(1)}, u32[]{:S(2)}, u32[]{:S(2)}) %collective-permute-start.4) | collective-permute-done | bytes 262176 | tf_op jit(solution)/shard_map/ppermute | solution.py:59
  19.3 0.0 copy-start
  19.3 0.1 collective-permute-start.7
  19.5 1.5 %collective-permute-start.9 = (f32[384,128]{1,0:T(8,128)S(1)}, f32[384,128]{1,0:T(8,128)S(1)}, u32[]{:S(2)}, u32[]{:S(2)}) collective-permute-start(f32[384,128]{1,0:T(8,128)S(1)} %get-tuple-element.69), channel_id=1, source_target_pairs={{0,2},{1,3},{2,0},{3,1},{4,6},{5,7},{6,4},{7,5},{8,10},{9,11},{10,... | collective-permute-start | bytes 589832 | tf_op jit(solution)/shard_map/ppermute | solution.py:59
  21.0 0.6 %collective-permute-start.8 = (f32[384,128]{1,0:T(8,128)S(1)}, f32[384,128]{1,0:T(8,128)S(1)}, u32[]{:S(2)}, u32[]{:S(2)}) collective-permute-start(f32[384,128]{1,0:T(8,128)S(1)} %get-tuple-element.70), channel_id=1, source_target_pairs={{0,4},{1,5},{2,6},{3,7},{4,0},{5,1},{6,2},{7,3},{8,12},{9,13},{10,... | collective-permute-start | bytes 589832 | tf_op jit(solution)/shard_map/ppermute | solution.py:59
  21.6 1.0 %shard_map.58 = (f32[256,128]{1,0:T(8,128)S(1)}, bf16[1024,256]{1,0:T(8,128)(2,1)S(1)}) custom-call(s32[8,8]{1,0:T(8,128)S(1)} %copy-done, f32[256,128]{1,0:T(8,128)S(1)} %get-tuple-element.68.p0, f32[256,128]{1,0:T(8,128)S(1)} %collective-permute-done.3.p1, f32[256,128]{1,0:T(8,128)S(1)} %collective-permute-done.6.p3, ...), custom_call_target="tpu_custom_call" | custom-call | flops 1610612736 | bytes 2228480 | tf_op jit(solution)/shard_map/pallas_call | solution.py:332
  22.6 0.9 %shard_map.59 = (f32[512,128]{1,0:T(8,128)S(1)}, f32[8,128]{1,0:T(8,128)S(1)}) custom-call(s32[8,8]{1,0:T(8,128)S(1)} %copy-done, f32[256,128]{1,0:T(8,128)S(1)} %get-tuple-element.38.part_ref, bf16[1024,256]{1,0:T(8,128)(2,1)S(1)} %get-tuple-element.39.pcol, f32[8,256,128]{2,1,0:T(8,128)S(1)} %bitcast_dynamic-update-slice_fusion.ss, ...), custom_call_target="tpu_custom_call" | custom-call | flops 1610612736 | bytes 3019008 | tf_op jit(solution)/shard_map/pallas_call | solution.py:332
  23.6 0.9 %collective-permute-start.14 = (f32[512,128]{1,0:T(8,128)S(1)}, f32[512,128]{1,0:T(8,128)S(1)}, u32[]{:S(2)}, u32[]{:S(2)}) collective-permute-start(f32[512,128]{1,0:T(8,128)S(1)} %get-tuple-element.40.send_ref.q0), channel_id=1, source_target_pairs={{0,16},{24,8},{8,0},{16,24},{1,17},{25,9},{9,1},{17,25},{2,18},{26... | collective-permute-start | bytes 786440 | tf_op jit(solution)/shard_map/ppermute | solution.py:349
  24.5 0.7 %collective-permute-start.13 = (f32[512,128]{1,0:T(8,128)S(1)}, f32[512,128]{1,0:T(8,128)S(1)}, u32[]{:S(2)}, u32[]{:S(2)}) collective-permute-start(f32[512,128]{1,0:T(8,128)S(1)} %get-tuple-element.40.send_ref.q0), channel_id=1, source_target_pairs={{8,16},{16,8},{0,0},{24,24},{9,17},{17,9},{1,1},{25,25},{10,18},{1... | collective-permute-start | bytes 786440 | tf_op jit(solution)/shard_map/ppermute | solution.py:349
  25.2 3.6 %collective-permute-start.12 = (f32[512,128]{1,0:T(8,128)S(1)}, f32[512,128]{1,0:T(8,128)S(1)}, u32[]{:S(2)}, u32[]{:S(2)}) collective-permute-start(f32[512,128]{1,0:T(8,128)S(1)} %get-tuple-element.40.send_ref.q0), channel_id=1, source_target_pairs={{0,8},{24,16},{8,0},{16,24},{1,9},{25,17},{9,1},{17,25},{2,10},{26... | collective-permute-start | bytes 786440 | tf_op jit(solution)/shard_map/ppermute | solution.py:349
  28.8 0.0 collective-permute-done.9
  28.8 0.0 collective-permute-done.8
  28.8 1.0 %collective-permute-start.10 = (f32[768,128]{1,0:T(8,128)S(1)}, f32[768,128]{1,0:T(8,128)S(1)}, u32[]{:S(2)}, u32[]{:S(2)}) collective-permute-start(f32[768,128]{1,0:T(8,128)S(1)} %pad_maximum_fusion.3), channel_id=1, source_target_pairs={{0,2},{1,3},{2,0},{3,1},{4,6},{5,7},{6,4},{7,5},{8,10},{9,11},{10,... | collective-permute-start | bytes 1179656 | tf_op jit(solution)/shard_map/ppermute | solution.py:59
  29.9 1.2 %collective-permute-start.11 = (f32[768,128]{1,0:T(8,128)S(1)}, f32[768,128]{1,0:T(8,128)S(1)}, u32[]{:S(2)}, u32[]{:S(2)}) collective-permute-start(f32[768,128]{1,0:T(8,128)S(1)} %pad_maximum_fusion.4), channel_id=1, source_target_pairs={{0,4},{1,5},{2,6},{3,7},{4,0},{5,1},{6,2},{7,3},{8,12},{9,13},{10,... | collective-permute-start | bytes 1179656 | tf_op jit(solution)/shard_map/ppermute | solution.py:59
  31.0 1.6 %shard_map.60 = (bf16[512,1024]{1,0:T(8,128)(2,1)S(1)}, bf16[512,1024]{1,0:T(8,128)(2,1)S(1)}, f32[256,128]{1,0:T(8,128)}) custom-call(s32[8,8]{1,0:T(8,128)S(1)} %copy-done, f32[8,256,128]{2,1,0:T(8,128)S(1)} %bitcast_dynamic-update-slice_fusion.ss, f32[8,256,128]{2,1,0:T(8,128)S(1)} %collective-permute-done.7.so, ...), custom_call_target="tpu_custom_call" | custom-call | flops 1610612736 | bytes 4591872 | tf_op jit(solution)/shard_map/pallas_call | solution.py:332
  32.6 0.2 collective-permute-done.14.q2
  32.8 4.6 %collective-permute-done.12.q1 = f32[512,128]{1,0:T(8,128)S(1)} collective-permute-done((f32[512,128]{1,0:T(8,128)S(1)}, f32[512,128]{1,0:T(8,128)S(1)}, u32[]{:S(2)}, u32[]{:S(2)}) %collective-permute-start.12) | collective-permute-done | bytes 262176 | tf_op jit(solution)/shard_map/ppermute | solution.py:349
  37.4 0.7 %shard_map.61 = (bf16[1024,256]{1,0:T(8,128)(2,1)S(1)}, f32[512,128]{1,0:T(8,128)S(1)}) custom-call(s32[8,8]{1,0:T(8,128)S(1)} %copy-done, f32[512,128]{1,0:T(8,128)S(1)} %get-tuple-element.40.send_ref.q0, f32[512,128]{1,0:T(8,128)S(1)} %collective-permute-done.12.q1, f32[512,128]{1,0:T(8,128)S(1)} %collective-permute-done.13.q3, ...), custom_call_target="tpu_custom_call" | custom-call | flops 12884901888 | bytes 1835264 | tf_op jit(solution)/shard_map/pallas_call | solution.py:332
  38.1 1.0 %collective-permute-start.17 = (f32[512,128]{1,0:T(8,128)S(1)}, f32[512,128]{1,0:T(8,128)S(1)}, u32[]{:S(2)}, u32[]{:S(2)}) collective-permute-start(f32[512,128]{1,0:T(8,128)S(1)} %get-tuple-element.58), channel_id=1, source_target_pairs={{0,8},{8,0},{16,24},{24,16},{1,9},{9,1},{17,25},{25,17},{2,10},{10... | collective-permute-start | bytes 786440 | tf_op jit(solution)/shard_map/ppermute | solution.py:59
  39.1 0.9 %collective-permute-done.11 = f32[768,128]{1,0:T(8,128)S(1)} collective-permute-done((f32[768,128]{1,0:T(8,128)S(1)}, f32[768,128]{1,0:T(8,128)S(1)}, u32[]{:S(2)}, u32[]{:S(2)}) %collective-permute-start.11) | collective-permute-done | bytes 393248 | tf_op jit(solution)/shard_map/ppermute | solution.py:59
  40.0 0.1 fusion.1
  40.1 0.1 pad_maximum_fusion.1.hi.s_hi
  40.2 0.1 collective-permute-start.16
  40.3 0.1 pad_maximum_fusion.lo.s_lo
  40.3 0.6 %collective-permute-start.15 = (f32[2,768,128]{2,1,0:T(8,128)S(1)}, f32[2,768,128]{2,1,0:T(8,128)S(1)}, u32[]{:S(2)}, u32[]{:S(2)}) collective-permute-start(f32[2,768,128]{2,1,0:T(8,128)S(1)} %pad_maximum_fusion.lo.s_lo), channel_id=1, source_target_pairs={{0,1},{1,0},{2,3},{3,2},{4,5},{5,4},{6,7},{7,6},{8,9},{9,8},{10,11... | collective-permute-start | bytes 2359304 | tf_op jit(solution)/shard_map/ppermute | solution.py:59
  40.9 0.6 %shard_map.62 = (f32[1024,128]{1,0:T(8,128)S(1)}, bf16[512,256]{1,0:T(8,128)(2,1)S(1)}, bf16[512,256]{1,0:T(8,128)(2,1)S(1)}) custom-call(s32[8,8]{1,0:T(8,128)S(1)} %copy-done, bf16[1024,256]{1,0:T(8,128)(2,1)S(1)} %get-tuple-element.51.hcol, f32[8,256,128]{2,1,0:T(8,128)S(1)} %bitcast_dynamic-update-slice_fusion.ss, ...), custom_call_target="tpu_custom_call" | custom-call | flops 12884901888 | bytes 4194560 | tf_op jit(solution)/shard_map/pallas_call | solution.py:332
  41.5 1.0 %collective-permute-done.16.hi.o_hi = f32[2,768,128]{2,1,0:T(8,128)S(1)} collective-permute-done((f32[2,768,128]{2,1,0:T(8,128)S(1)}, f32[2,768,128]{2,1,0:T(8,128)S(1)}, u32[]{:S(2)}, u32[]{:S(2)}) %collective-permute-start.16) | collective-permute-done | bytes 786464 | tf_op jit(solution)/shard_map/ppermute | solution.py:59
  42.6 0.6 %shard_map.63 = (f32[1024,128]{1,0:T(8,128)S(1)}, bf16[512,256]{1,0:T(8,128)(2,1)S(1)}) custom-call(s32[8,8]{1,0:T(8,128)S(1)} %copy-done, bf16[1024,256]{1,0:T(8,128)(2,1)S(1)} %get-tuple-element.51.hcol, f32[8,256,128]{2,1,0:T(8,128)S(1)} %collective-permute-done.7.so, f32[2,768,128]{2,1,0:T(8,128)S(1)} %collective-permute-done.16.hi.o_hi, ...), custom_call_target="tpu_custom_call" | custom-call | flops 1610612736 | bytes 3670272 | tf_op jit(solution)/shard_map/pallas_call | solution.py:332
  43.2 0.5 collective-permute-done.15.lo.o_lo
  43.7 0.7 %shard_map.64 = (f32[256,128]{1,0:T(8,128)S(1)}, f32[256,128]{1,0:T(8,128)S(1)}, bf16[1024,256]{1,0:T(8,128)(2,1)S(1)}) custom-call(s32[8,8]{1,0:T(8,128)S(1)} %copy-done, bf16[1024,256]{1,0:T(8,128)(2,1)S(1)} %get-tuple-element.51.hcol, f32[8,256,128]{2,1,0:T(8,128)S(1)} %collective-permute-done.7.so, f32[2,768,128]{2,1,0:T(8,128)S(1)} %collective-permute-done.15.lo.o_lo, ...), custom_call_target="tpu_custom_call" | custom-call | flops 1610612736 | bytes 4456704 | tf_op jit(solution)/shard_map/pallas_call | solution.py:332
  44.3 1.7 %collective-permute-start.18 = (f32[256,128]{1,0:T(8,128)S(1)}, f32[256,128]{1,0:T(8,128)S(1)}, u32[]{:S(2)}, u32[]{:S(2)}) collective-permute-start(f32[256,128]{1,0:T(8,128)S(1)} %get-tuple-element.62), channel_id=1, source_target_pairs={{0,8},{8,0},{16,24},{24,16},{1,9},{9,1},{17,25},{25,17},{2,10},{10... | collective-permute-start | bytes 393224 | tf_op jit(solution)/shard_map/ppermute | solution.py:59
  46.0 3.3 %shard_map.65 = (f32[256,128]{1,0:T(8,128)}, f32[256,128]{1,0:T(8,128)S(1)}) custom-call(s32[8,8]{1,0:T(8,128)S(1)} %copy-done, bf16[512,1024]{1,0:T(8,128)(2,1)S(1)} %get-tuple-element.44.prow, bf16[512,1024]{1,0:T(8,128)(2,1)S(1)} %get-tuple-element.45.hrow, bf16[1024,256]{1,0:T(8,128)(2,1)S(1)} %get-tuple-element.39.pcol, ...), custom_call_target="tpu_custom_call" | custom-call | flops 1610612736 | bytes 10092800 | tf_op jit(solution)/shard_map/pallas_call | solution.py:332
  49.3 0.6 %collective-permute-done.18 = f32[256,128]{1,0:T(8,128)S(1)} collective-permute-done((f32[256,128]{1,0:T(8,128)S(1)}, f32[256,128]{1,0:T(8,128)S(1)}, u32[]{:S(2)}, u32[]{:S(2)}) %collective-permute-start.18) | collective-permute-done | bytes 131104 | tf_op jit(solution)/shard_map/ppermute | solution.py:59
  49.9 0.7 %add.3 = f32[256,128]{1,0:T(8,128)} add(f32[256,128]{1,0:T(8,128)S(1)} %get-tuple-element.61, f32[256,128]{1,0:T(8,128)S(1)} %collective-permute-done.18) | non-fusion elementwise | flops 32768 | bytes 393216 | tf_op jit(solution)/shard_map/add | solution.py:422
  (23 shorter events, 0.4 us)
Async XLA Ops:
  0.6 13.5 %collective-permute-start.6 = (f32[256,128]{1,0:T(8,128)}, f32[256,128]{1,0:T(8,128)S(1)}, u32[]{:S(2)}, u32[]{:S(2)}) collective-permute-start(f32[256,128]{1,0:T(8,128)} %param.3), channel_id=1, source_target_pairs={{0,24},{8,16},{16,8},{24,0},{1,25},{9,17},{17,9},{25,1},{2,26},{10... | collective-permute-start | bytes 393224 | tf_op jit(solution)/shard_map/ppermute | solution.py:59
  5.7 5.2 %collective-permute-start.1 = (f32[256,128]{1,0:T(8,128)}, f32[256,128]{1,0:T(8,128)S(1)}, u32[]{:S(2)}, u32[]{:S(2)}) collective-permute-start(f32[256,128]{1,0:T(8,128)} %param.3), channel_id=1, source_target_pairs={{0,4},{1,5},{2,6},{3,7},{4,0},{5,1},{6,2},{7,3},{8,12},{9,13},{10,... | collective-permute-start | bytes 393224 | tf_op jit(solution)/shard_map/ppermute | solution.py:59
  7.3 5.3 %collective-permute-start = (f32[256,128]{1,0:T(8,128)}, f32[256,128]{1,0:T(8,128)S(1)}, u32[]{:S(2)}, u32[]{:S(2)}) collective-permute-start(f32[256,128]{1,0:T(8,128)} %param.4), channel_id=1, source_target_pairs={{0,2},{1,3},{2,0},{3,1},{4,6},{5,7},{6,4},{7,5},{8,10},{9,11},{10,... | collective-permute-start | bytes 393224 | tf_op jit(solution)/shard_map/ppermute | solution.py:59
  9.8 7.3 %collective-permute-start.5 = (f32[256,128]{1,0:T(8,128)S(1)}, f32[256,128]{1,0:T(8,128)S(1)}, u32[]{:S(2)}, u32[]{:S(2)}) collective-permute-start(f32[256,128]{1,0:T(8,128)S(1)} %get-tuple-element.68.p0), channel_id=1, source_target_pairs={{0,16},{8,24},{16,0},{24,8},{1,17},{9,25},{17,1},{25,9},{2,18},{10... | collective-permute-start | bytes 393224 | tf_op jit(solution)/shard_map/ppermute | solution.py:59
  9.9 7.3 %collective-permute-start.3 = (f32[256,128]{1,0:T(8,128)S(1)}, f32[256,128]{1,0:T(8,128)S(1)}, u32[]{:S(2)}, u32[]{:S(2)}) collective-permute-start(f32[256,128]{1,0:T(8,128)S(1)} %get-tuple-element.68.p0), channel_id=1, source_target_pairs={{0,8},{8,0},{16,24},{24,16},{1,9},{9,1},{17,25},{25,17},{2,10},{10... | collective-permute-start | bytes 393224 | tf_op jit(solution)/shard_map/ppermute | solution.py:59
  10.9 7.1 %collective-permute-start.2 = (f32[512,128]{1,0:T(8,128)S(1)}, f32[512,128]{1,0:T(8,128)S(1)}, u32[]{:S(2)}, u32[]{:S(2)}) collective-permute-start(f32[512,128]{1,0:T(8,128)S(1)} %pad_maximum_fusion.6), channel_id=1, source_target_pairs={{0,2},{1,3},{2,0},{3,1},{4,6},{5,7},{6,4},{7,5},{8,10},{9,11},{10,... | collective-permute-start | bytes 786440 | tf_op jit(solution)/shard_map/ppermute | solution.py:59
  12.6 6.6 %collective-permute-start.4 = (f32[512,128]{1,0:T(8,128)S(1)}, f32[512,128]{1,0:T(8,128)S(1)}, u32[]{:S(2)}, u32[]{:S(2)}) collective-permute-start(f32[512,128]{1,0:T(8,128)S(1)} %pad_maximum_fusion.7), channel_id=1, source_target_pairs={{0,4},{1,5},{2,6},{3,7},{4,0},{5,1},{6,2},{7,3},{8,12},{9,13},{10,... | collective-permute-start | bytes 786440 | tf_op jit(solution)/shard_map/ppermute | solution.py:59
  19.3 2.2 %copy-start = (s32[8,8]{1,0:T(8,128)S(1)}, s32[8,8]{1,0:T(8,128)}, u32[]{:S(2)}) copy-start(s32[8,8]{1,0:T(8,128)} %mask_ref.15) | copy-start | bytes 772
  19.3 3.3 %collective-permute-start.7 = (f32[8,256,128]{2,1,0:T(8,128)S(1)}, f32[8,256,128]{2,1,0:T(8,128)S(1)}, u32[]{:S(2)}, u32[]{:S(2)}) collective-permute-start(f32[8,256,128]{2,1,0:T(8,128)S(1)} %bitcast_dynamic-update-slice_fusion.ss), channel_id=1, source_target_pairs={{0,1},{1,0},{2,3},{3,2},{4,5},{5,4},{6,7},{7,6},{8,9},{9,8},{10,11... | collective-permute-start | bytes 3145736 | tf_op jit(solution)/shard_map/ppermute | solution.py:59
  19.5 9.3 %collective-permute-start.9 = (f32[384,128]{1,0:T(8,128)S(1)}, f32[384,128]{1,0:T(8,128)S(1)}, u32[]{:S(2)}, u32[]{:S(2)}) collective-permute-start(f32[384,128]{1,0:T(8,128)S(1)} %get-tuple-element.69), channel_id=1, source_target_pairs={{0,2},{1,3},{2,0},{3,1},{4,6},{5,7},{6,4},{7,5},{8,10},{9,11},{10,... | collective-permute-start | bytes 589832 | tf_op jit(solution)/shard_map/ppermute | solution.py:59
  21.0 7.8 %collective-permute-start.8 = (f32[384,128]{1,0:T(8,128)S(1)}, f32[384,128]{1,0:T(8,128)S(1)}, u32[]{:S(2)}, u32[]{:S(2)}) collective-permute-start(f32[384,128]{1,0:T(8,128)S(1)} %get-tuple-element.70), channel_id=1, source_target_pairs={{0,4},{1,5},{2,6},{3,7},{4,0},{5,1},{6,2},{7,3},{8,12},{9,13},{10,... | collective-permute-start | bytes 589832 | tf_op jit(solution)/shard_map/ppermute | solution.py:59
  23.6 9.2 %collective-permute-start.14 = (f32[512,128]{1,0:T(8,128)S(1)}, f32[512,128]{1,0:T(8,128)S(1)}, u32[]{:S(2)}, u32[]{:S(2)}) collective-permute-start(f32[512,128]{1,0:T(8,128)S(1)} %get-tuple-element.40.send_ref.q0), channel_id=1, source_target_pairs={{0,16},{24,8},{8,0},{16,24},{1,17},{25,9},{9,1},{17,25},{2,18},{26... | collective-permute-start | bytes 786440 | tf_op jit(solution)/shard_map/ppermute | solution.py:349
  24.5 8.3 %collective-permute-start.13 = (f32[512,128]{1,0:T(8,128)S(1)}, f32[512,128]{1,0:T(8,128)S(1)}, u32[]{:S(2)}, u32[]{:S(2)}) collective-permute-start(f32[512,128]{1,0:T(8,128)S(1)} %get-tuple-element.40.send_ref.q0), channel_id=1, source_target_pairs={{8,16},{16,8},{0,0},{24,24},{9,17},{17,9},{1,1},{25,25},{10,18},{1... | collective-permute-start | bytes 786440 | tf_op jit(solution)/shard_map/ppermute | solution.py:349
  25.2 12.2 %collective-permute-start.12 = (f32[512,128]{1,0:T(8,128)S(1)}, f32[512,128]{1,0:T(8,128)S(1)}, u32[]{:S(2)}, u32[]{:S(2)}) collective-permute-start(f32[512,128]{1,0:T(8,128)S(1)} %get-tuple-element.40.send_ref.q0), channel_id=1, source_target_pairs={{0,8},{24,16},{8,0},{16,24},{1,9},{25,17},{9,1},{17,25},{2,10},{26... | collective-permute-start | bytes 786440 | tf_op jit(solution)/shard_map/ppermute | solution.py:349
  28.8 10.3 %collective-permute-start.10 = (f32[768,128]{1,0:T(8,128)S(1)}, f32[768,128]{1,0:T(8,128)S(1)}, u32[]{:S(2)}, u32[]{:S(2)}) collective-permute-start(f32[768,128]{1,0:T(8,128)S(1)} %pad_maximum_fusion.3), channel_id=1, source_target_pairs={{0,2},{1,3},{2,0},{3,1},{4,6},{5,7},{6,4},{7,5},{8,10},{9,11},{10,... | collective-permute-start | bytes 1179656 | tf_op jit(solution)/shard_map/ppermute | solution.py:59
  29.9 10.1 %collective-permute-start.11 = (f32[768,128]{1,0:T(8,128)S(1)}, f32[768,128]{1,0:T(8,128)S(1)}, u32[]{:S(2)}, u32[]{:S(2)}) collective-permute-start(f32[768,128]{1,0:T(8,128)S(1)} %pad_maximum_fusion.4), channel_id=1, source_target_pairs={{0,4},{1,5},{2,6},{3,7},{4,0},{5,1},{6,2},{7,3},{8,12},{9,13},{10,... | collective-permute-start | bytes 1179656 | tf_op jit(solution)/shard_map/ppermute | solution.py:59
  38.1 7.9 %collective-permute-start.17 = (f32[512,128]{1,0:T(8,128)S(1)}, f32[512,128]{1,0:T(8,128)S(1)}, u32[]{:S(2)}, u32[]{:S(2)}) collective-permute-start(f32[512,128]{1,0:T(8,128)S(1)} %get-tuple-element.58), channel_id=1, source_target_pairs={{0,8},{8,0},{16,24},{24,16},{1,9},{9,1},{17,25},{25,17},{2,10},{10... | collective-permute-start | bytes 786440 | tf_op jit(solution)/shard_map/ppermute | solution.py:59
  40.2 2.4 %collective-permute-start.16 = (f32[2,768,128]{2,1,0:T(8,128)S(1)}, f32[2,768,128]{2,1,0:T(8,128)S(1)}, u32[]{:S(2)}, u32[]{:S(2)}) collective-permute-start(f32[2,768,128]{2,1,0:T(8,128)S(1)} %pad_maximum_fusion.1.hi.s_hi), channel_id=1, source_target_pairs={{0,1},{1,0},{2,3},{3,2},{4,5},{5,4},{6,7},{7,6},{8,9},{9,8},{10,11... | collective-permute-start | bytes 2359304 | tf_op jit(solution)/shard_map/ppermute | solution.py:59
  40.3 3.3 %collective-permute-start.15 = (f32[2,768,128]{2,1,0:T(8,128)S(1)}, f32[2,768,128]{2,1,0:T(8,128)S(1)}, u32[]{:S(2)}, u32[]{:S(2)}) collective-permute-start(f32[2,768,128]{2,1,0:T(8,128)S(1)} %pad_maximum_fusion.lo.s_lo), channel_id=1, source_target_pairs={{0,1},{1,0},{2,3},{3,2},{4,5},{5,4},{6,7},{7,6},{8,9},{9,8},{10,11... | collective-permute-start | bytes 2359304 | tf_op jit(solution)/shard_map/ppermute | solution.py:59
  44.3 5.6 %collective-permute-start.18 = (f32[256,128]{1,0:T(8,128)S(1)}, f32[256,128]{1,0:T(8,128)S(1)}, u32[]{:S(2)}, u32[]{:S(2)}) collective-permute-start(f32[256,128]{1,0:T(8,128)S(1)} %get-tuple-element.62), channel_id=1, source_target_pairs={{0,8},{8,0},{16,24},{24,16},{1,9},{9,1},{17,25},{25,17},{2,10},{10... | collective-permute-start | bytes 393224 | tf_op jit(solution)/shard_map/ppermute | solution.py:59

commit v7 on v6

--- a/solution.py
+++ b/solution.py
@@ -266,11 +266,14 @@
             if m == 1:
                 back_ref[...] = 3.0 * rows
         there = pattern_of(mask_ref, band_blocks(r, 1), [c])
+        meets_c = any_live(mask_ref, band_blocks(r, 1), c)
         fars = ((0, (own_lo, own_hi)), (1, (other_lo, other_hi)))
         for flip, parts in fars:
             for (_, blocks), far in zip(pairs(c, flip), parts):
 
-                @pl.when(any_live(mask_ref, blocks, c))
+                met = [mask_ref[b, c] * any_live(mask_ref, band_blocks(r, 1), b).astype(jnp.int32) for b in blocks]
+
+                @pl.when(jnp.logical_and(sum(met) != 0, meets_c))
                 def _(blocks=blocks, far=far):
                     term = dot_parts(far[...], rows_at(r, ph2, blocks))
                     back_ref[...] -= 2.0 * there * term

time: 50.8 us -> 50.9 us (level)
  no operation moved by 1% of the time
where the time goes in v7:
time: 50.9 us; the launch traced here: 50.6 us
  starting transfers between devices  25 us (49%)
  waiting for transfers between devices  13.2 us (26%)
  Pallas kernels  9.42 us (19%)
  other arithmetic  1.99 us (4%)
  between operations  0.89 us (2%)
    ppermute x16, starting transfers between devices, swap(): return lax.ppermute(x, axis, [(i, i ^ mask) for i in range(size)])  19.8 us
    pallas_call x8, Pallas kernels, call(): pl.pallas_call(kernel, out_shape=outs, in_specs=[smem] + [vmem] * (len(ar...  9.42 us
    ppermute x16, waiting for transfers between devices, swap(): return lax.ppermute(x, axis, [(i, i ^ mask) for i in range(size)])  8.38 us
    ppermute x3, starting transfers between devices, to_middle(): return [lax.ppermute(x, 'row', pairs) for pairs in routes]  5.19 us
    ppermute x3, waiting for transfers between devices, to_middle(): return [lax.ppermute(x, 'row', pairs) for pairs in routes]  4.79 us
  transfers between devices with their start and end apart: 19, of which 11 were waited for; matrix products, arithmetic and copies ran while one was open for 3% of the time, Pallas kernels for 19%

profile of v7, /device:TPU:0, one launch (start us, length us, event | category | flops | bytes accessed | tf_op | source)
XLA Modules:
  0.0 50.6 jit_solution(1638171104076795255)
XLA Ops:
  0.6 5.1 %collective-permute-start.6 = (f32[256,128]{1,0:T(8,128)}, f32[256,128]{1,0:T(8,128)S(1)}, u32[]{:S(2)}, u32[]{:S(2)}) collective-permute-start(f32[256,128]{1,0:T(8,128)} %param.3), channel_id=1, source_target_pairs={{0,24},{8,16},{16,8},{24,0},{1,25},{9,17},{17,9},{25,1},{2,26},{10... | collective-permute-start | bytes 393224 | tf_op jit(solution)/shard_map/ppermute | solution.py:59
  5.7 1.5 %collective-permute-start.1 = (f32[256,128]{1,0:T(8,128)}, f32[256,128]{1,0:T(8,128)S(1)}, u32[]{:S(2)}, u32[]{:S(2)}) collective-permute-start(f32[256,128]{1,0:T(8,128)} %param.3), channel_id=1, source_target_pairs={{0,4},{1,5},{2,6},{3,7},{4,0},{5,1},{6,2},{7,3},{8,12},{9,13},{10,... | collective-permute-start | bytes 393224 | tf_op jit(solution)/shard_map/ppermute | solution.py:59
  7.3 1.5 %collective-permute-start = (f32[256,128]{1,0:T(8,128)}, f32[256,128]{1,0:T(8,128)S(1)}, u32[]{:S(2)}, u32[]{:S(2)}) collective-permute-start(f32[256,128]{1,0:T(8,128)} %param.4), channel_id=1, source_target_pairs={{0,2},{1,3},{2,0},{3,1},{4,6},{5,7},{6,4},{7,5},{8,10},{9,11},{10,... | collective-permute-start | bytes 393224 | tf_op jit(solution)/shard_map/ppermute | solution.py:59
  8.8 1.0 %pad_maximum_fusion.5 = f32[512,128]{1,0:T(8,128)S(1)} fusion(f32[256,128]{1,0:T(8,128)} %param.4, f32[256,128]{1,0:T(8,128)} %param.3), kind=kLoop, calls=%fused_computation.9 | loop fusion | flops 65536 | bytes 524288 | tf_op jit(solution)/shard_map/concatenate | solution.py:369
  9.8 0.1 collective-permute-start.5
  9.9 0.8 %collective-permute-start.3 = (f32[256,128]{1,0:T(8,128)S(1)}, f32[256,128]{1,0:T(8,128)S(1)}, u32[]{:S(2)}, u32[]{:S(2)}) collective-permute-start(f32[256,128]{1,0:T(8,128)S(1)} %get-tuple-element.68.p0), channel_id=1, source_target_pairs={{0,8},{8,0},{16,24},{24,16},{1,9},{9,1},{17,25},{25,17},{2,10},{10... | collective-permute-start | bytes 393224 | tf_op jit(solution)/shard_map/ppermute | solution.py:59
  10.6 0.3 collective-permute-done.1
  10.9 1.6 %collective-permute-start.2 = (f32[512,128]{1,0:T(8,128)S(1)}, f32[512,128]{1,0:T(8,128)S(1)}, u32[]{:S(2)}, u32[]{:S(2)}) collective-permute-start(f32[512,128]{1,0:T(8,128)S(1)} %pad_maximum_fusion.6), channel_id=1, source_target_pairs={{0,2},{1,3},{2,0},{3,1},{4,6},{5,7},{6,4},{7,5},{8,10},{9,11},{10,... | collective-permute-start | bytes 786440 | tf_op jit(solution)/shard_map/ppermute | solution.py:59
  12.5 0.1 collective-permute-done
  12.6 1.5 %collective-permute-start.4 = (f32[512,128]{1,0:T(8,128)S(1)}, f32[512,128]{1,0:T(8,128)S(1)}, u32[]{:S(2)}, u32[]{:S(2)}) collective-permute-start(f32[512,128]{1,0:T(8,128)S(1)} %pad_maximum_fusion.7), channel_id=1, source_target_pairs={{0,4},{1,5},{2,6},{3,7},{4,0},{5,1},{6,2},{7,3},{8,12},{9,13},{10,... | collective-permute-start | bytes 786440 | tf_op jit(solution)/shard_map/ppermute | solution.py:59
  14.1 0.0 collective-permute-done.6.p3
  14.2 2.9 %collective-permute-done.5.p2 = f32[256,128]{1,0:T(8,128)S(1)} collective-permute-done((f32[256,128]{1,0:T(8,128)S(1)}, f32[256,128]{1,0:T(8,128)S(1)}, u32[]{:S(2)}, u32[]{:S(2)}) %collective-permute-start.5) | collective-permute-done | bytes 131104 | tf_op jit(solution)/shard_map/ppermute | solution.py:59
  17.1 0.0 collective-permute-done.3.p1
  17.1 0.9 %collective-permute-done.2 = f32[512,128]{1,0:T(8,128)S(1)} collective-permute-done((f32[512,128]{1,0:T(8,128)S(1)}, f32[512,128]{1,0:T(8,128)S(1)}, u32[]{:S(2)}, u32[]{:S(2)}) %collective-permute-start.2) | collective-permute-done | bytes 262176 | tf_op jit(solution)/shard_map/ppermute | solution.py:59
  18.1 1.2 %collective-permute-done.4 = f32[512,128]{1,0:T(8,128)S(1)} collective-permute-done((f32[512,128]{1,0:T(8,128)S(1)}, f32[512,128]{1,0:T(8,128)S(1)}, u32[]{:S(2)}, u32[]{:S(2)}) %collective-permute-start.4) | collective-permute-done | bytes 262176 | tf_op jit(solution)/shard_map/ppermute | solution.py:59
  19.3 0.0 copy-start
  19.3 0.1 collective-permute-start.7
  19.5 1.5 %collective-permute-start.9 = (f32[384,128]{1,0:T(8,128)S(1)}, f32[384,128]{1,0:T(8,128)S(1)}, u32[]{:S(2)}, u32[]{:S(2)}) collective-permute-start(f32[384,128]{1,0:T(8,128)S(1)} %get-tuple-element.69), channel_id=1, source_target_pairs={{0,2},{1,3},{2,0},{3,1},{4,6},{5,7},{6,4},{7,5},{8,10},{9,11},{10,... | collective-permute-start | bytes 589832 | tf_op jit(solution)/shard_map/ppermute | solution.py:59
  21.0 0.6 %collective-permute-start.8 = (f32[384,128]{1,0:T(8,128)S(1)}, f32[384,128]{1,0:T(8,128)S(1)}, u32[]{:S(2)}, u32[]{:S(2)}) collective-permute-start(f32[384,128]{1,0:T(8,128)S(1)} %get-tuple-element.70), channel_id=1, source_target_pairs={{0,4},{1,5},{2,6},{3,7},{4,0},{5,1},{6,2},{7,3},{8,12},{9,13},{10,... | collective-permute-start | bytes 589832 | tf_op jit(solution)/shard_map/ppermute | solution.py:59
  21.6 1.0 %shard_map.58 = (f32[256,128]{1,0:T(8,128)S(1)}, bf16[1024,256]{1,0:T(8,128)(2,1)S(1)}) custom-call(s32[8,8]{1,0:T(8,128)S(1)} %copy-done, f32[256,128]{1,0:T(8,128)S(1)} %get-tuple-element.68.p0, f32[256,128]{1,0:T(8,128)S(1)} %collective-permute-done.3.p1, f32[256,128]{1,0:T(8,128)S(1)} %collective-permute-done.6.p3, ...), custom_call_target="tpu_custom_call" | custom-call | flops 1610612736 | bytes 2228480 | tf_op jit(solution)/shard_map/pallas_call | solution.py:335
  22.6 0.9 %shard_map.59 = (f32[512,128]{1,0:T(8,128)S(1)}, f32[8,128]{1,0:T(8,128)S(1)}) custom-call(s32[8,8]{1,0:T(8,128)S(1)} %copy-done, f32[256,128]{1,0:T(8,128)S(1)} %get-tuple-element.38.part_ref, bf16[1024,256]{1,0:T(8,128)(2,1)S(1)} %get-tuple-element.39.pcol, f32[8,256,128]{2,1,0:T(8,128)S(1)} %bitcast_dynamic-update-slice_fusion.ss, ...), custom_call_target="tpu_custom_call" | custom-call | flops 1610612736 | bytes 3019008 | tf_op jit(solution)/shard_map/pallas_call | solution.py:335
  23.6 0.9 %collective-permute-start.14 = (f32[512,128]{1,0:T(8,128)S(1)}, f32[512,128]{1,0:T(8,128)S(1)}, u32[]{:S(2)}, u32[]{:S(2)}) collective-permute-start(f32[512,128]{1,0:T(8,128)S(1)} %get-tuple-element.40.send_ref.q0), channel_id=1, source_target_pairs={{0,16},{24,8},{8,0},{16,24},{1,17},{25,9},{9,1},{17,25},{2,18},{26... | collective-permute-start | bytes 786440 | tf_op jit(solution)/shard_map/ppermute | solution.py:352
  24.5 0.7 %collective-permute-start.13 = (f32[512,128]{1,0:T(8,128)S(1)}, f32[512,128]{1,0:T(8,128)S(1)}, u32[]{:S(2)}, u32[]{:S(2)}) collective-permute-start(f32[512,128]{1,0:T(8,128)S(1)} %get-tuple-element.40.send_ref.q0), channel_id=1, source_target_pairs={{8,16},{16,8},{0,0},{24,24},{9,17},{17,9},{1,1},{25,25},{10,18},{1... | collective-permute-start | bytes 786440 | tf_op jit(solution)/shard_map/ppermute | solution.py:352
  25.2 3.6 %collective-permute-start.12 = (f32[512,128]{1,0:T(8,128)S(1)}, f32[512,128]{1,0:T(8,128)S(1)}, u32[]{:S(2)}, u32[]{:S(2)}) collective-permute-start(f32[512,128]{1,0:T(8,128)S(1)} %get-tuple-element.40.send_ref.q0), channel_id=1, source_target_pairs={{0,8},{24,16},{8,0},{16,24},{1,9},{25,17},{9,1},{17,25},{2,10},{26... | collective-permute-start | bytes 786440 | tf_op jit(solution)/shard_map/ppermute | solution.py:352
  28.8 1.0 %collective-permute-start.10 = (f32[768,128]{1,0:T(8,128)S(1)}, f32[768,128]{1,0:T(8,128)S(1)}, u32[]{:S(2)}, u32[]{:S(2)}) collective-permute-start(f32[768,128]{1,0:T(8,128)S(1)} %pad_maximum_fusion.3), channel_id=1, source_target_pairs={{0,2},{1,3},{2,0},{3,1},{4,6},{5,7},{6,4},{7,5},{8,10},{9,11},{10,... | collective-permute-start | bytes 1179656 | tf_op jit(solution)/shard_map/ppermute | solution.py:59
  29.9 1.2 %collective-permute-start.11 = (f32[768,128]{1,0:T(8,128)S(1)}, f32[768,128]{1,0:T(8,128)S(1)}, u32[]{:S(2)}, u32[]{:S(2)}) collective-permute-start(f32[768,128]{1,0:T(8,128)S(1)} %pad_maximum_fusion.4), channel_id=1, source_target_pairs={{0,4},{1,5},{2,6},{3,7},{4,0},{5,1},{6,2},{7,3},{8,12},{9,13},{10,... | collective-permute-start | bytes 1179656 | tf_op jit(solution)/shard_map/ppermute | solution.py:59
  31.0 1.6 %shard_map.60 = (bf16[512,1024]{1,0:T(8,128)(2,1)S(1)}, bf16[512,1024]{1,0:T(8,128)(2,1)S(1)}, f32[256,128]{1,0:T(8,128)}) custom-call(s32[8,8]{1,0:T(8,128)S(1)} %copy-done, f32[8,256,128]{2,1,0:T(8,128)S(1)} %bitcast_dynamic-update-slice_fusion.ss, f32[8,256,128]{2,1,0:T(8,128)S(1)} %collective-permute-done.7.so, ...), custom_call_target="tpu_custom_call" | custom-call | flops 1610612736 | bytes 4591872 | tf_op jit(solution)/shard_map/pallas_call | solution.py:335
  32.6 0.2 collective-permute-done.14.q2
  32.8 0.0 collective-permute-done.13.q3
  32.8 4.6 %collective-permute-done.12.q1 = f32[512,128]{1,0:T(8,128)S(1)} collective-permute-done((f32[512,128]{1,0:T(8,128)S(1)}, f32[512,128]{1,0:T(8,128)S(1)}, u32[]{:S(2)}, u32[]{:S(2)}) %collective-permute-start.12) | collective-permute-done | bytes 262176 | tf_op jit(solution)/shard_map/ppermute | solution.py:352
  37.4 0.7 %shard_map.61 = (bf16[1024,256]{1,0:T(8,128)(2,1)S(1)}, f32[512,128]{1,0:T(8,128)S(1)}) custom-call(s32[8,8]{1,0:T(8,128)S(1)} %copy-done, f32[512,128]{1,0:T(8,128)S(1)} %get-tuple-element.40.send_ref.q0, f32[512,128]{1,0:T(8,128)S(1)} %collective-permute-done.12.q1, f32[512,128]{1,0:T(8,128)S(1)} %collective-permute-done.13.q3, ...), custom_call_target="tpu_custom_call" | custom-call | flops 12884901888 | bytes 1835264 | tf_op jit(solution)/shard_map/pallas_call | solution.py:335
  38.1 1.0 %collective-permute-start.17 = (f32[512,128]{1,0:T(8,128)S(1)}, f32[512,128]{1,0:T(8,128)S(1)}, u32[]{:S(2)}, u32[]{:S(2)}) collective-permute-start(f32[512,128]{1,0:T(8,128)S(1)} %get-tuple-element.58), channel_id=1, source_target_pairs={{0,8},{8,0},{16,24},{24,16},{1,9},{9,1},{17,25},{25,17},{2,10},{10... | collective-permute-start | bytes 786440 | tf_op jit(solution)/shard_map/ppermute | solution.py:59
  39.1 0.0 collective-permute-done.10
  39.1 0.9 %collective-permute-done.11 = f32[768,128]{1,0:T(8,128)S(1)} collective-permute-done((f32[768,128]{1,0:T(8,128)S(1)}, f32[768,128]{1,0:T(8,128)S(1)}, u32[]{:S(2)}, u32[]{:S(2)}) %collective-permute-start.11) | collective-permute-done | bytes 393248 | tf_op jit(solution)/shard_map/ppermute | solution.py:59
  40.0 0.1 fusion.1
  40.1 0.1 pad_maximum_fusion.1.hi.s_hi
  40.2 0.1 collective-permute-start.16
  40.3 0.1 pad_maximum_fusion.lo.s_lo
  40.3 0.6 %collective-permute-start.15 = (f32[2,768,128]{2,1,0:T(8,128)S(1)}, f32[2,768,128]{2,1,0:T(8,128)S(1)}, u32[]{:S(2)}, u32[]{:S(2)}) collective-permute-start(f32[2,768,128]{2,1,0:T(8,128)S(1)} %pad_maximum_fusion.lo.s_lo), channel_id=1, source_target_pairs={{0,1},{1,0},{2,3},{3,2},{4,5},{5,4},{6,7},{7,6},{8,9},{9,8},{10,11... | collective-permute-start | bytes 2359304 | tf_op jit(solution)/shard_map/ppermute | solution.py:59
  40.9 0.6 %shard_map.62 = (f32[1024,128]{1,0:T(8,128)S(1)}, bf16[512,256]{1,0:T(8,128)(2,1)S(1)}, bf16[512,256]{1,0:T(8,128)(2,1)S(1)}) custom-call(s32[8,8]{1,0:T(8,128)S(1)} %copy-done, bf16[1024,256]{1,0:T(8,128)(2,1)S(1)} %get-tuple-element.51.hcol, f32[8,256,128]{2,1,0:T(8,128)S(1)} %bitcast_dynamic-update-slice_fusion.ss, ...), custom_call_target="tpu_custom_call" | custom-call | flops 12884901888 | bytes 4194560 | tf_op jit(solution)/shard_map/pallas_call | solution.py:335
  41.5 1.0 %collective-permute-done.16.hi.o_hi = f32[2,768,128]{2,1,0:T(8,128)S(1)} collective-permute-done((f32[2,768,128]{2,1,0:T(8,128)S(1)}, f32[2,768,128]{2,1,0:T(8,128)S(1)}, u32[]{:S(2)}, u32[]{:S(2)}) %collective-permute-start.16) | collective-permute-done | bytes 786464 | tf_op jit(solution)/shard_map/ppermute | solution.py:59
  42.6 0.6 %shard_map.63 = (f32[1024,128]{1,0:T(8,128)S(1)}, bf16[512,256]{1,0:T(8,128)(2,1)S(1)}) custom-call(s32[8,8]{1,0:T(8,128)S(1)} %copy-done, bf16[1024,256]{1,0:T(8,128)(2,1)S(1)} %get-tuple-element.51.hcol, f32[8,256,128]{2,1,0:T(8,128)S(1)} %collective-permute-done.7.so, f32[2,768,128]{2,1,0:T(8,128)S(1)} %collective-permute-done.16.hi.o_hi, ...), custom_call_target="tpu_custom_call" | custom-call | flops 1610612736 | bytes 3670272 | tf_op jit(solution)/shard_map/pallas_call | solution.py:335
  43.2 0.5 collective-permute-done.15.lo.o_lo
  43.7 0.7 %shard_map.64 = (f32[256,128]{1,0:T(8,128)S(1)}, f32[256,128]{1,0:T(8,128)S(1)}, bf16[1024,256]{1,0:T(8,128)(2,1)S(1)}) custom-call(s32[8,8]{1,0:T(8,128)S(1)} %copy-done, bf16[1024,256]{1,0:T(8,128)(2,1)S(1)} %get-tuple-element.51.hcol, f32[8,256,128]{2,1,0:T(8,128)S(1)} %collective-permute-done.7.so, f32[2,768,128]{2,1,0:T(8,128)S(1)} %collective-permute-done.15.lo.o_lo, ...), custom_call_target="tpu_custom_call" | custom-call | flops 1610612736 | bytes 4456704 | tf_op jit(solution)/shard_map/pallas_call | solution.py:335
  44.3 1.7 %collective-permute-start.18 = (f32[256,128]{1,0:T(8,128)S(1)}, f32[256,128]{1,0:T(8,128)S(1)}, u32[]{:S(2)}, u32[]{:S(2)}) collective-permute-start(f32[256,128]{1,0:T(8,128)S(1)} %get-tuple-element.62), channel_id=1, source_target_pairs={{0,8},{8,0},{16,24},{24,16},{1,9},{9,1},{17,25},{25,17},{2,10},{10... | collective-permute-start | bytes 393224 | tf_op jit(solution)/shard_map/ppermute | solution.py:59
  46.0 3.3 %shard_map.65 = (f32[256,128]{1,0:T(8,128)}, f32[256,128]{1,0:T(8,128)S(1)}) custom-call(s32[8,8]{1,0:T(8,128)S(1)} %copy-done, bf16[512,1024]{1,0:T(8,128)(2,1)S(1)} %get-tuple-element.44.prow, bf16[512,1024]{1,0:T(8,128)(2,1)S(1)} %get-tuple-element.45.hrow, bf16[1024,256]{1,0:T(8,128)(2,1)S(1)} %get-tuple-element.39.pcol, ...), custom_call_target="tpu_custom_call" | custom-call | flops 1610612736 | bytes 10092800 | tf_op jit(solution)/shard_map/pallas_call | solution.py:335
  49.4 0.6 %collective-permute-done.18 = f32[256,128]{1,0:T(8,128)S(1)} collective-permute-done((f32[256,128]{1,0:T(8,128)S(1)}, f32[256,128]{1,0:T(8,128)S(1)}, u32[]{:S(2)}, u32[]{:S(2)}) %collective-permute-start.18) | collective-permute-done | bytes 131104 | tf_op jit(solution)/shard_map/ppermute | solution.py:59
  49.9 0.7 %add.3 = f32[256,128]{1,0:T(8,128)} add(f32[256,128]{1,0:T(8,128)S(1)} %get-tuple-element.61, f32[256,128]{1,0:T(8,128)S(1)} %collective-permute-done.18) | non-fusion elementwise | flops 32768 | bytes 393216 | tf_op jit(solution)/shard_map/add | solution.py:425
  (23 shorter events, 0.4 us)
Async XLA Ops:
  0.6 13.5 %collective-permute-start.6 = (f32[256,128]{1,0:T(8,128)}, f32[256,128]{1,0:T(8,128)S(1)}, u32[]{:S(2)}, u32[]{:S(2)}) collective-permute-start(f32[256,128]{1,0:T(8,128)} %param.3), channel_id=1, source_target_pairs={{0,24},{8,16},{16,8},{24,0},{1,25},{9,17},{17,9},{25,1},{2,26},{10... | collective-permute-start | bytes 393224 | tf_op jit(solution)/shard_map/ppermute | solution.py:59
  5.7 5.2 %collective-permute-start.1 = (f32[256,128]{1,0:T(8,128)}, f32[256,128]{1,0:T(8,128)S(1)}, u32[]{:S(2)}, u32[]{:S(2)}) collective-permute-start(f32[256,128]{1,0:T(8,128)} %param.3), channel_id=1, source_target_pairs={{0,4},{1,5},{2,6},{3,7},{4,0},{5,1},{6,2},{7,3},{8,12},{9,13},{10,... | collective-permute-start | bytes 393224 | tf_op jit(solution)/shard_map/ppermute | solution.py:59
  7.3 5.3 %collective-permute-start = (f32[256,128]{1,0:T(8,128)}, f32[256,128]{1,0:T(8,128)S(1)}, u32[]{:S(2)}, u32[]{:S(2)}) collective-permute-start(f32[256,128]{1,0:T(8,128)} %param.4), channel_id=1, source_target_pairs={{0,2},{1,3},{2,0},{3,1},{4,6},{5,7},{6,4},{7,5},{8,10},{9,11},{10,... | collective-permute-start | bytes 393224 | tf_op jit(solution)/shard_map/ppermute | solution.py:59
  9.8 7.3 %collective-permute-start.5 = (f32[256,128]{1,0:T(8,128)S(1)}, f32[256,128]{1,0:T(8,128)S(1)}, u32[]{:S(2)}, u32[]{:S(2)}) collective-permute-start(f32[256,128]{1,0:T(8,128)S(1)} %get-tuple-element.68.p0), channel_id=1, source_target_pairs={{0,16},{8,24},{16,0},{24,8},{1,17},{9,25},{17,1},{25,9},{2,18},{10... | collective-permute-start | bytes 393224 | tf_op jit(solution)/shard_map/ppermute | solution.py:59
  9.9 7.3 %collective-permute-start.3 = (f32[256,128]{1,0:T(8,128)S(1)}, f32[256,128]{1,0:T(8,128)S(1)}, u32[]{:S(2)}, u32[]{:S(2)}) collective-permute-start(f32[256,128]{1,0:T(8,128)S(1)} %get-tuple-element.68.p0), channel_id=1, source_target_pairs={{0,8},{8,0},{16,24},{24,16},{1,9},{9,1},{17,25},{25,17},{2,10},{10... | collective-permute-start | bytes 393224 | tf_op jit(solution)/shard_map/ppermute | solution.py:59
  10.9 7.1 %collective-permute-start.2 = (f32[512,128]{1,0:T(8,128)S(1)}, f32[512,128]{1,0:T(8,128)S(1)}, u32[]{:S(2)}, u32[]{:S(2)}) collective-permute-start(f32[512,128]{1,0:T(8,128)S(1)} %pad_maximum_fusion.6), channel_id=1, source_target_pairs={{0,2},{1,3},{2,0},{3,1},{4,6},{5,7},{6,4},{7,5},{8,10},{9,11},{10,... | collective-permute-start | bytes 786440 | tf_op jit(solution)/shard_map/ppermute | solution.py:59
  12.6 6.6 %collective-permute-start.4 = (f32[512,128]{1,0:T(8,128)S(1)}, f32[512,128]{1,0:T(8,128)S(1)}, u32[]{:S(2)}, u32[]{:S(2)}) collective-permute-start(f32[512,128]{1,0:T(8,128)S(1)} %pad_maximum_fusion.7), channel_id=1, source_target_pairs={{0,4},{1,5},{2,6},{3,7},{4,0},{5,1},{6,2},{7,3},{8,12},{9,13},{10,... | collective-permute-start | bytes 786440 | tf_op jit(solution)/shard_map/ppermute | solution.py:59
  19.3 2.2 %copy-start = (s32[8,8]{1,0:T(8,128)S(1)}, s32[8,8]{1,0:T(8,128)}, u32[]{:S(2)}) copy-start(s32[8,8]{1,0:T(8,128)} %mask_ref.15) | copy-start | bytes 772
  19.3 3.3 %collective-permute-start.7 = (f32[8,256,128]{2,1,0:T(8,128)S(1)}, f32[8,256,128]{2,1,0:T(8,128)S(1)}, u32[]{:S(2)}, u32[]{:S(2)}) collective-permute-start(f32[8,256,128]{2,1,0:T(8,128)S(1)} %bitcast_dynamic-update-slice_fusion.ss), channel_id=1, source_target_pairs={{0,1},{1,0},{2,3},{3,2},{4,5},{5,4},{6,7},{7,6},{8,9},{9,8},{10,11... | collective-permute-start | bytes 3145736 | tf_op jit(solution)/shard_map/ppermute | solution.py:59
  19.5 9.3 %collective-permute-start.9 = (f32[384,128]{1,0:T(8,128)S(1)}, f32[384,128]{1,0:T(8,128)S(1)}, u32[]{:S(2)}, u32[]{:S(2)}) collective-permute-start(f32[384,128]{1,0:T(8,128)S(1)} %get-tuple-element.69), channel_id=1, source_target_pairs={{0,2},{1,3},{2,0},{3,1},{4,6},{5,7},{6,4},{7,5},{8,10},{9,11},{10,... | collective-permute-start | bytes 589832 | tf_op jit(solution)/shard_map/ppermute | solution.py:59
  21.0 7.8 %collective-permute-start.8 = (f32[384,128]{1,0:T(8,128)S(1)}, f32[384,128]{1,0:T(8,128)S(1)}, u32[]{:S(2)}, u32[]{:S(2)}) collective-permute-start(f32[384,128]{1,0:T(8,128)S(1)} %get-tuple-element.70), channel_id=1, source_target_pairs={{0,4},{1,5},{2,6},{3,7},{4,0},{5,1},{6,2},{7,3},{8,12},{9,13},{10,... | collective-permute-start | bytes 589832 | tf_op jit(solution)/shard_map/ppermute | solution.py:59
  23.6 9.2 %collective-permute-start.14 = (f32[512,128]{1,0:T(8,128)S(1)}, f32[512,128]{1,0:T(8,128)S(1)}, u32[]{:S(2)}, u32[]{:S(2)}) collective-permute-start(f32[512,128]{1,0:T(8,128)S(1)} %get-tuple-element.40.send_ref.q0), channel_id=1, source_target_pairs={{0,16},{24,8},{8,0},{16,24},{1,17},{25,9},{9,1},{17,25},{2,18},{26... | collective-permute-start | bytes 786440 | tf_op jit(solution)/shard_map/ppermute | solution.py:352
  24.5 8.3 %collective-permute-start.13 = (f32[512,128]{1,0:T(8,128)S(1)}, f32[512,128]{1,0:T(8,128)S(1)}, u32[]{:S(2)}, u32[]{:S(2)}) collective-permute-start(f32[512,128]{1,0:T(8,128)S(1)} %get-tuple-element.40.send_ref.q0), channel_id=1, source_target_pairs={{8,16},{16,8},{0,0},{24,24},{9,17},{17,9},{1,1},{25,25},{10,18},{1... | collective-permute-start | bytes 786440 | tf_op jit(solution)/shard_map/ppermute | solution.py:352
  25.2 12.2 %collective-permute-start.12 = (f32[512,128]{1,0:T(8,128)S(1)}, f32[512,128]{1,0:T(8,128)S(1)}, u32[]{:S(2)}, u32[]{:S(2)}) collective-permute-start(f32[512,128]{1,0:T(8,128)S(1)} %get-tuple-element.40.send_ref.q0), channel_id=1, source_target_pairs={{0,8},{24,16},{8,0},{16,24},{1,9},{25,17},{9,1},{17,25},{2,10},{26... | collective-permute-start | bytes 786440 | tf_op jit(solution)/shard_map/ppermute | solution.py:352
  28.8 10.3 %collective-permute-start.10 = (f32[768,128]{1,0:T(8,128)S(1)}, f32[768,128]{1,0:T(8,128)S(1)}, u32[]{:S(2)}, u32[]{:S(2)}) collective-permute-start(f32[768,128]{1,0:T(8,128)S(1)} %pad_maximum_fusion.3), channel_id=1, source_target_pairs={{0,2},{1,3},{2,0},{3,1},{4,6},{5,7},{6,4},{7,5},{8,10},{9,11},{10,... | collective-permute-start | bytes 1179656 | tf_op jit(solution)/shard_map/ppermute | solution.py:59
  29.9 10.1 %collective-permute-start.11 = (f32[768,128]{1,0:T(8,128)S(1)}, f32[768,128]{1,0:T(8,128)S(1)}, u32[]{:S(2)}, u32[]{:S(2)}) collective-permute-start(f32[768,128]{1,0:T(8,128)S(1)} %pad_maximum_fusion.4), channel_id=1, source_target_pairs={{0,4},{1,5},{2,6},{3,7},{4,0},{5,1},{6,2},{7,3},{8,12},{9,13},{10,... | collective-permute-start | bytes 1179656 | tf_op jit(solution)/shard_map/ppermute | solution.py:59
  38.1 7.9 %collective-permute-start.17 = (f32[512,128]{1,0:T(8,128)S(1)}, f32[512,128]{1,0:T(8,128)S(1)}, u32[]{:S(2)}, u32[]{:S(2)}) collective-permute-start(f32[512,128]{1,0:T(8,128)S(1)} %get-tuple-element.58), channel_id=1, source_target_pairs={{0,8},{8,0},{16,24},{24,16},{1,9},{9,1},{17,25},{25,17},{2,10},{10... | collective-permute-start | bytes 786440 | tf_op jit(solution)/shard_map/ppermute | solution.py:59
  40.2 2.4 %collective-permute-start.16 = (f32[2,768,128]{2,1,0:T(8,128)S(1)}, f32[2,768,128]{2,1,0:T(8,128)S(1)}, u32[]{:S(2)}, u32[]{:S(2)}) collective-permute-start(f32[2,768,128]{2,1,0:T(8,128)S(1)} %pad_maximum_fusion.1.hi.s_hi), channel_id=1, source_target_pairs={{0,1},{1,0},{2,3},{3,2},{4,5},{5,4},{6,7},{7,6},{8,9},{9,8},{10,11... | collective-permute-start | bytes 2359304 | tf_op jit(solution)/shard_map/ppermute | solution.py:59
  40.3 3.3 %collective-permute-start.15 = (f32[2,768,128]{2,1,0:T(8,128)S(1)}, f32[2,768,128]{2,1,0:T(8,128)S(1)}, u32[]{:S(2)}, u32[]{:S(2)}) collective-permute-start(f32[2,768,128]{2,1,0:T(8,128)S(1)} %pad_maximum_fusion.lo.s_lo), channel_id=1, source_target_pairs={{0,1},{1,0},{2,3},{3,2},{4,5},{5,4},{6,7},{7,6},{8,9},{9,8},{10,11... | collective-permute-start | bytes 2359304 | tf_op jit(solution)/shard_map/ppermute | solution.py:59
  44.3 5.6 %collective-permute-start.18 = (f32[256,128]{1,0:T(8,128)S(1)}, f32[256,128]{1,0:T(8,128)S(1)}, u32[]{:S(2)}, u32[]{:S(2)}) collective-permute-start(f32[256,128]{1,0:T(8,128)S(1)} %get-tuple-element.62), channel_id=1, source_target_pairs={{0,8},{8,0},{16,24},{24,16},{1,9},{9,1},{17,25},{25,17},{2,10},{10... | collective-permute-start | bytes 393224 | tf_op jit(solution)/shard_map/ppermute | solution.py:59

commit v8 on v6

--- a/solution.py
+++ b/solution.py
@@ -164,11 +164,16 @@
 
 def hp_kernel(mask_ref, part_ref, pcol, ss, so, send_ref, mark_ref):
     r, c = lax.axis_index("row"), lax.axis_index("col")
-    total = part_ref[...]
+    send_ref[0:BAND] = part_ref[...]
     for j, blocks in pairs(c, 1):
-        total += dot_parts(left_pair(mask_ref, r, blocks, so, j), rows_at(r, pcol, blocks))
+
+        @pl.when(any_live(mask_ref, blocks, c))
+        def _(j=j, blocks=blocks):
+            left = left_pair(mask_ref, r, blocks, so, j)
+            send_ref[0:BAND] += dot_parts(left, rows_at(r, pcol, blocks))
+
     own = pattern_of(mask_ref, band_blocks(r, 0), [c])
-    send_ref[0:BAND] = total * own
+    send_ref[0:BAND] = send_ref[0:BAND] * own
     send_ref[BAND:] = ss[0] * own
     mark_ref[...] = jnp.zeros_like(mark_ref)
 

time: 50.8 us -> 50.7 us (level)
  waiting for transfers between devices: 13.2 us -> 14.8 us
  Pallas kernels: 9.44 us -> 8.46 us
  starting transfers between devices: 24.9 us -> 24.3 us
    ppermute x16, waiting for transfers between devices: 8.4 us -> 10.2 us  [swap(): return lax.ppermute(x, axis, [(i, i ^ mask) for i in range(size)])]
    pallas_call x8, Pallas kernels: 9.44 us -> 8.46 us  [call(): pl.pallas_call(kernel, out_shape=outs, in_specs=[smem] + [vmem] * (len(ar...]
    ppermute x16, starting transfers between devices: 19.7 us -> 19.1 us  [swap(): return lax.ppermute(x, axis, [(i, i ^ mask) for i in range(size)])]
  transfers between devices with their start and end apart: 19 -> 19, of which waited for: 11 -> 11; matrix products, arithmetic and copies ran while one was open for 3% -> 3% of each run, Pallas kernels for 19% -> 17%
where the time goes in v8:
time: 50.7 us; the launch traced here: 50.6 us
  starting transfers between devices  24.3 us (48%)
  waiting for transfers between devices  14.8 us (29%)
  Pallas kernels  8.46 us (17%)
  other arithmetic  1.99 us (4%)
  between operations  0.89 us (2%)
    ppermute x16, starting transfers between devices, swap(): return lax.ppermute(x, axis, [(i, i ^ mask) for i in range(size)])  19.1 us
    ppermute x16, waiting for transfers between devices, swap(): return lax.ppermute(x, axis, [(i, i ^ mask) for i in range(size)])  10.2 us
    pallas_call x8, Pallas kernels, call(): pl.pallas_call(kernel, out_shape=outs, in_specs=[smem] + [vmem] * (len(ar...  8.46 us
    ppermute x3, starting transfers between devices, to_middle(): return [lax.ppermute(x, 'row', pairs) for pairs in routes]  5.19 us
    ppermute x3, waiting for transfers between devices, to_middle(): return [lax.ppermute(x, 'row', pairs) for pairs in routes]  4.56 us
  transfers between devices with their start and end apart: 19, of which 11 were waited for; matrix products, arithmetic and copies ran while one was open for 3% of the time, Pallas kernels for 17%

profile of v8, /device:TPU:0, one launch (start us, length us, event | category | flops | bytes accessed | tf_op | source)
XLA Modules:
  0.0 50.6 jit_solution(15165590476205808796)
XLA Ops:
  0.6 5.1 %collective-permute-start.6 = (f32[256,128]{1,0:T(8,128)}, f32[256,128]{1,0:T(8,128)S(1)}, u32[]{:S(2)}, u32[]{:S(2)}) collective-permute-start(f32[256,128]{1,0:T(8,128)} %param.3), channel_id=1, source_target_pairs={{0,24},{8,16},{16,8},{24,0},{1,25},{9,17},{17,9},{25,1},{2,26},{10... | collective-permute-start | bytes 393224 | tf_op jit(solution)/shard_map/ppermute | solution.py:59
  5.7 1.5 %collective-permute-start.1 = (f32[256,128]{1,0:T(8,128)}, f32[256,128]{1,0:T(8,128)S(1)}, u32[]{:S(2)}, u32[]{:S(2)}) collective-permute-start(f32[256,128]{1,0:T(8,128)} %param.3), channel_id=1, source_target_pairs={{0,4},{1,5},{2,6},{3,7},{4,0},{5,1},{6,2},{7,3},{8,12},{9,13},{10,... | collective-permute-start | bytes 393224 | tf_op jit(solution)/shard_map/ppermute | solution.py:59
  7.3 1.5 %collective-permute-start = (f32[256,128]{1,0:T(8,128)}, f32[256,128]{1,0:T(8,128)S(1)}, u32[]{:S(2)}, u32[]{:S(2)}) collective-permute-start(f32[256,128]{1,0:T(8,128)} %param.4), channel_id=1, source_target_pairs={{0,2},{1,3},{2,0},{3,1},{4,6},{5,7},{6,4},{7,5},{8,10},{9,11},{10,... | collective-permute-start | bytes 393224 | tf_op jit(solution)/shard_map/ppermute | solution.py:59
  8.8 1.0 %pad_maximum_fusion.5 = f32[512,128]{1,0:T(8,128)S(1)} fusion(f32[256,128]{1,0:T(8,128)} %param.4, f32[256,128]{1,0:T(8,128)} %param.3), kind=kLoop, calls=%fused_computation.9 | loop fusion | flops 65536 | bytes 524288 | tf_op jit(solution)/shard_map/concatenate | solution.py:371
  9.8 0.1 collective-permute-start.5
  9.9 0.8 %collective-permute-start.3 = (f32[256,128]{1,0:T(8,128)S(1)}, f32[256,128]{1,0:T(8,128)S(1)}, u32[]{:S(2)}, u32[]{:S(2)}) collective-permute-start(f32[256,128]{1,0:T(8,128)S(1)} %get-tuple-element.68.p0), channel_id=1, source_target_pairs={{0,8},{8,0},{16,24},{24,16},{1,9},{9,1},{17,25},{25,17},{2,10},{10... | collective-permute-start | bytes 393224 | tf_op jit(solution)/shard_map/ppermute | solution.py:59
  10.6 0.3 collective-permute-done.1
  10.9 1.6 %collective-permute-start.2 = (f32[512,128]{1,0:T(8,128)S(1)}, f32[512,128]{1,0:T(8,128)S(1)}, u32[]{:S(2)}, u32[]{:S(2)}) collective-permute-start(f32[512,128]{1,0:T(8,128)S(1)} %pad_maximum_fusion.6), channel_id=1, source_target_pairs={{0,2},{1,3},{2,0},{3,1},{4,6},{5,7},{6,4},{7,5},{8,10},{9,11},{10,... | collective-permute-start | bytes 786440 | tf_op jit(solution)/shard_map/ppermute | solution.py:59
  12.5 0.1 collective-permute-done
  12.6 1.5 %collective-permute-start.4 = (f32[512,128]{1,0:T(8,128)S(1)}, f32[512,128]{1,0:T(8,128)S(1)}, u32[]{:S(2)}, u32[]{:S(2)}) collective-permute-start(f32[512,128]{1,0:T(8,128)S(1)} %pad_maximum_fusion.7), channel_id=1, source_target_pairs={{0,4},{1,5},{2,6},{3,7},{4,0},{5,1},{6,2},{7,3},{8,12},{9,13},{10,... | collective-permute-start | bytes 786440 | tf_op jit(solution)/shard_map/ppermute | solution.py:59
  14.2 2.9 %collective-permute-done.5.p2 = f32[256,128]{1,0:T(8,128)S(1)} collective-permute-done((f32[256,128]{1,0:T(8,128)S(1)}, f32[256,128]{1,0:T(8,128)S(1)}, u32[]{:S(2)}, u32[]{:S(2)}) %collective-permute-start.5) | collective-permute-done | bytes 131104 | tf_op jit(solution)/shard_map/ppermute | solution.py:59
  17.1 0.0 collective-permute-done.3.p1
  17.1 0.9 %collective-permute-done.2 = f32[512,128]{1,0:T(8,128)S(1)} collective-permute-done((f32[512,128]{1,0:T(8,128)S(1)}, f32[512,128]{1,0:T(8,128)S(1)}, u32[]{:S(2)}, u32[]{:S(2)}) %collective-permute-start.2) | collective-permute-done | bytes 262176 | tf_op jit(solution)/shard_map/ppermute | solution.py:59
  18.1 1.2 %collective-permute-done.4 = f32[512,128]{1,0:T(8,128)S(1)} collective-permute-done((f32[512,128]{1,0:T(8,128)S(1)}, f32[512,128]{1,0:T(8,128)S(1)}, u32[]{:S(2)}, u32[]{:S(2)}) %collective-permute-start.4) | collective-permute-done | bytes 262176 | tf_op jit(solution)/shard_map/ppermute | solution.py:59
  19.3 0.0 copy-start
  19.3 0.1 collective-permute-start.7
  19.5 1.5 %collective-permute-start.9 = (f32[384,128]{1,0:T(8,128)S(1)}, f32[384,128]{1,0:T(8,128)S(1)}, u32[]{:S(2)}, u32[]{:S(2)}) collective-permute-start(f32[384,128]{1,0:T(8,128)S(1)} %get-tuple-element.69), channel_id=1, source_target_pairs={{0,2},{1,3},{2,0},{3,1},{4,6},{5,7},{6,4},{7,5},{8,10},{9,11},{10,... | collective-permute-start | bytes 589832 | tf_op jit(solution)/shard_map/ppermute | solution.py:59
  21.0 0.6 %collective-permute-start.8 = (f32[384,128]{1,0:T(8,128)S(1)}, f32[384,128]{1,0:T(8,128)S(1)}, u32[]{:S(2)}, u32[]{:S(2)}) collective-permute-start(f32[384,128]{1,0:T(8,128)S(1)} %get-tuple-element.70), channel_id=1, source_target_pairs={{0,4},{1,5},{2,6},{3,7},{4,0},{5,1},{6,2},{7,3},{8,12},{9,13},{10,... | collective-permute-start | bytes 589832 | tf_op jit(solution)/shard_map/ppermute | solution.py:59
  21.6 1.0 %shard_map.58 = (f32[256,128]{1,0:T(8,128)S(1)}, bf16[1024,256]{1,0:T(8,128)(2,1)S(1)}) custom-call(s32[8,8]{1,0:T(8,128)S(1)} %copy-done, f32[256,128]{1,0:T(8,128)S(1)} %get-tuple-element.68.p0, f32[256,128]{1,0:T(8,128)S(1)} %collective-permute-done.3.p1, f32[256,128]{1,0:T(8,128)S(1)} %collective-permute-done.6.p3, ...), custom_call_target="tpu_custom_call" | custom-call | flops 1610612736 | bytes 2228480 | tf_op jit(solution)/shard_map/pallas_call | solution.py:337
  22.6 0.0 collective-permute-done.7.so
  22.6 0.7 %shard_map.59 = (f32[512,128]{1,0:T(8,128)S(1)}, f32[8,128]{1,0:T(8,128)S(1)}) custom-call(s32[8,8]{1,0:T(8,128)S(1)} %copy-done, f32[256,128]{1,0:T(8,128)S(1)} %get-tuple-element.38.part_ref, bf16[1024,256]{1,0:T(8,128)(2,1)S(1)} %get-tuple-element.39.pcol, f32[8,256,128]{2,1,0:T(8,128)S(1)} %bitcast_dynamic-update-slice_fusion.ss, ...), custom_call_target="tpu_custom_call" | custom-call | flops 1610612736 | bytes 3019008 | tf_op jit(solution)/shard_map/pallas_call | solution.py:337
  23.3 0.9 %collective-permute-start.14 = (f32[512,128]{1,0:T(8,128)S(1)}, f32[512,128]{1,0:T(8,128)S(1)}, u32[]{:S(2)}, u32[]{:S(2)}) collective-permute-start(f32[512,128]{1,0:T(8,128)S(1)} %get-tuple-element.40.send_ref.q0), channel_id=1, source_target_pairs={{0,16},{24,8},{8,0},{16,24},{1,17},{25,9},{9,1},{17,25},{2,18},{26... | collective-permute-start | bytes 786440 | tf_op jit(solution)/shard_map/ppermute | solution.py:354
  24.2 0.7 %collective-permute-start.13 = (f32[512,128]{1,0:T(8,128)S(1)}, f32[512,128]{1,0:T(8,128)S(1)}, u32[]{:S(2)}, u32[]{:S(2)}) collective-permute-start(f32[512,128]{1,0:T(8,128)S(1)} %get-tuple-element.40.send_ref.q0), channel_id=1, source_target_pairs={{8,16},{16,8},{0,0},{24,24},{9,17},{17,9},{1,1},{25,25},{10,18},{1... | collective-permute-start | bytes 786440 | tf_op jit(solution)/shard_map/ppermute | solution.py:354
  24.9 3.6 %collective-permute-start.12 = (f32[512,128]{1,0:T(8,128)S(1)}, f32[512,128]{1,0:T(8,128)S(1)}, u32[]{:S(2)}, u32[]{:S(2)}) collective-permute-start(f32[512,128]{1,0:T(8,128)S(1)} %get-tuple-element.40.send_ref.q0), channel_id=1, source_target_pairs={{0,8},{24,16},{8,0},{16,24},{1,9},{25,17},{9,1},{17,25},{2,10},{26... | collective-permute-start | bytes 786440 | tf_op jit(solution)/shard_map/ppermute | solution.py:354
  28.5 0.0 collective-permute-done.9
  28.5 0.0 collective-permute-done.8
  28.5 1.0 %collective-permute-start.10 = (f32[768,128]{1,0:T(8,128)S(1)}, f32[768,128]{1,0:T(8,128)S(1)}, u32[]{:S(2)}, u32[]{:S(2)}) collective-permute-start(f32[768,128]{1,0:T(8,128)S(1)} %pad_maximum_fusion.3), channel_id=1, source_target_pairs={{0,2},{1,3},{2,0},{3,1},{4,6},{5,7},{6,4},{7,5},{8,10},{9,11},{10,... | collective-permute-start | bytes 1179656 | tf_op jit(solution)/shard_map/ppermute | solution.py:59
  29.6 1.4 %collective-permute-start.11 = (f32[768,128]{1,0:T(8,128)S(1)}, f32[768,128]{1,0:T(8,128)S(1)}, u32[]{:S(2)}, u32[]{:S(2)}) collective-permute-start(f32[768,128]{1,0:T(8,128)S(1)} %pad_maximum_fusion.4), channel_id=1, source_target_pairs={{0,4},{1,5},{2,6},{3,7},{4,0},{5,1},{6,2},{7,3},{8,12},{9,13},{10,... | collective-permute-start | bytes 1179656 | tf_op jit(solution)/shard_map/ppermute | solution.py:59
  31.0 1.6 %shard_map.60 = (bf16[512,1024]{1,0:T(8,128)(2,1)S(1)}, bf16[512,1024]{1,0:T(8,128)(2,1)S(1)}, f32[256,128]{1,0:T(8,128)}) custom-call(s32[8,8]{1,0:T(8,128)S(1)} %copy-done, f32[8,256,128]{2,1,0:T(8,128)S(1)} %bitcast_dynamic-update-slice_fusion.ss, f32[8,256,128]{2,1,0:T(8,128)S(1)} %collective-permute-done.7.so, ...), custom_call_target="tpu_custom_call" | custom-call | flops 1610612736 | bytes 4591872 | tf_op jit(solution)/shard_map/pallas_call | solution.py:337
  32.6 4.6 %collective-permute-done.12.q1 = f32[512,128]{1,0:T(8,128)S(1)} collective-permute-done((f32[512,128]{1,0:T(8,128)S(1)}, f32[512,128]{1,0:T(8,128)S(1)}, u32[]{:S(2)}, u32[]{:S(2)}) %collective-permute-start.12) | collective-permute-done | bytes 262176 | tf_op jit(solution)/shard_map/ppermute | solution.py:354
  37.1 0.7 %shard_map.61 = (bf16[1024,256]{1,0:T(8,128)(2,1)S(1)}, f32[512,128]{1,0:T(8,128)S(1)}) custom-call(s32[8,8]{1,0:T(8,128)S(1)} %copy-done, f32[512,128]{1,0:T(8,128)S(1)} %get-tuple-element.40.send_ref.q0, f32[512,128]{1,0:T(8,128)S(1)} %collective-permute-done.12.q1, f32[512,128]{1,0:T(8,128)S(1)} %collective-permute-done.13.q3, ...), custom_call_target="tpu_custom_call" | custom-call | flops 12884901888 | bytes 1835264 | tf_op jit(solution)/shard_map/pallas_call | solution.py:337
  37.8 1.0 %collective-permute-start.17 = (f32[512,128]{1,0:T(8,128)S(1)}, f32[512,128]{1,0:T(8,128)S(1)}, u32[]{:S(2)}, u32[]{:S(2)}) collective-permute-start(f32[512,128]{1,0:T(8,128)S(1)} %get-tuple-element.58), channel_id=1, source_target_pairs={{0,8},{8,0},{16,24},{24,16},{1,9},{9,1},{17,25},{25,17},{2,10},{10... | collective-permute-start | bytes 786440 | tf_op jit(solution)/shard_map/ppermute | solution.py:59
  38.9 1.1 %collective-permute-done.11 = f32[768,128]{1,0:T(8,128)S(1)} collective-permute-done((f32[768,128]{1,0:T(8,128)S(1)}, f32[768,128]{1,0:T(8,128)S(1)}, u32[]{:S(2)}, u32[]{:S(2)}) %collective-permute-start.11) | collective-permute-done | bytes 393248 | tf_op jit(solution)/shard_map/ppermute | solution.py:59
  39.9 0.1 fusion.1
  40.1 0.1 pad_maximum_fusion.1.hi.s_hi
  40.2 0.1 collective-permute-start.16
  40.2 0.1 pad_maximum_fusion.lo.s_lo
  40.3 0.6 %collective-permute-start.15 = (f32[2,768,128]{2,1,0:T(8,128)S(1)}, f32[2,768,128]{2,1,0:T(8,128)S(1)}, u32[]{:S(2)}, u32[]{:S(2)}) collective-permute-start(f32[2,768,128]{2,1,0:T(8,128)S(1)} %pad_maximum_fusion.lo.s_lo), channel_id=1, source_target_pairs={{0,1},{1,0},{2,3},{3,2},{4,5},{5,4},{6,7},{7,6},{8,9},{9,8},{10,11... | collective-permute-start | bytes 2359304 | tf_op jit(solution)/shard_map/ppermute | solution.py:59
  40.9 0.6 %shard_map.62 = (f32[1024,128]{1,0:T(8,128)S(1)}, bf16[512,256]{1,0:T(8,128)(2,1)S(1)}, bf16[512,256]{1,0:T(8,128)(2,1)S(1)}) custom-call(s32[8,8]{1,0:T(8,128)S(1)} %copy-done, bf16[1024,256]{1,0:T(8,128)(2,1)S(1)} %get-tuple-element.51.hcol, f32[8,256,128]{2,1,0:T(8,128)S(1)} %bitcast_dynamic-update-slice_fusion.ss, ...), custom_call_target="tpu_custom_call" | custom-call | flops 12884901888 | bytes 4194560 | tf_op jit(solution)/shard_map/pallas_call | solution.py:337
  41.5 1.0 %collective-permute-done.16.hi.o_hi = f32[2,768,128]{2,1,0:T(8,128)S(1)} collective-permute-done((f32[2,768,128]{2,1,0:T(8,128)S(1)}, f32[2,768,128]{2,1,0:T(8,128)S(1)}, u32[]{:S(2)}, u32[]{:S(2)}) %collective-permute-start.16) | collective-permute-done | bytes 786464 | tf_op jit(solution)/shard_map/ppermute | solution.py:59
  42.5 0.6 %shard_map.63 = (f32[1024,128]{1,0:T(8,128)S(1)}, bf16[512,256]{1,0:T(8,128)(2,1)S(1)}) custom-call(s32[8,8]{1,0:T(8,128)S(1)} %copy-done, bf16[1024,256]{1,0:T(8,128)(2,1)S(1)} %get-tuple-element.51.hcol, f32[8,256,128]{2,1,0:T(8,128)S(1)} %collective-permute-done.7.so, f32[2,768,128]{2,1,0:T(8,128)S(1)} %collective-permute-done.16.hi.o_hi, ...), custom_call_target="tpu_custom_call" | custom-call | flops 1610612736 | bytes 3670272 | tf_op jit(solution)/shard_map/pallas_call | solution.py:337
  43.1 0.5 collective-permute-done.15.lo.o_lo
  43.6 0.7 %shard_map.64 = (f32[256,128]{1,0:T(8,128)S(1)}, f32[256,128]{1,0:T(8,128)S(1)}, bf16[1024,256]{1,0:T(8,128)(2,1)S(1)}) custom-call(s32[8,8]{1,0:T(8,128)S(1)} %copy-done, bf16[1024,256]{1,0:T(8,128)(2,1)S(1)} %get-tuple-element.51.hcol, f32[8,256,128]{2,1,0:T(8,128)S(1)} %collective-permute-done.7.so, f32[2,768,128]{2,1,0:T(8,128)S(1)} %collective-permute-done.15.lo.o_lo, ...), custom_call_target="tpu_custom_call" | custom-call | flops 1610612736 | bytes 4456704 | tf_op jit(solution)/shard_map/pallas_call | solution.py:337
  44.3 0.8 %collective-permute-start.18 = (f32[256,128]{1,0:T(8,128)S(1)}, f32[256,128]{1,0:T(8,128)S(1)}, u32[]{:S(2)}, u32[]{:S(2)}) collective-permute-start(f32[256,128]{1,0:T(8,128)S(1)} %get-tuple-element.62), channel_id=1, source_target_pairs={{0,8},{8,0},{16,24},{24,16},{1,9},{9,1},{17,25},{25,17},{2,10},{10... | collective-permute-start | bytes 393224 | tf_op jit(solution)/shard_map/ppermute | solution.py:59
  45.1 0.3 collective-permute-done.17.q23
  45.3 2.6 %shard_map.65 = (f32[256,128]{1,0:T(8,128)}, f32[256,128]{1,0:T(8,128)S(1)}) custom-call(s32[8,8]{1,0:T(8,128)S(1)} %copy-done, bf16[512,1024]{1,0:T(8,128)(2,1)S(1)} %get-tuple-element.44.prow, bf16[512,1024]{1,0:T(8,128)(2,1)S(1)} %get-tuple-element.45.hrow, bf16[1024,256]{1,0:T(8,128)(2,1)S(1)} %get-tuple-element.39.pcol, ...), custom_call_target="tpu_custom_call" | custom-call | flops 1610612736 | bytes 10092800 | tf_op jit(solution)/shard_map/pallas_call | solution.py:337
  48.0 1.9 %collective-permute-done.18 = f32[256,128]{1,0:T(8,128)S(1)} collective-permute-done((f32[256,128]{1,0:T(8,128)S(1)}, f32[256,128]{1,0:T(8,128)S(1)}, u32[]{:S(2)}, u32[]{:S(2)}) %collective-permute-start.18) | collective-permute-done | bytes 131104 | tf_op jit(solution)/shard_map/ppermute | solution.py:59
  49.9 0.7 %add.3 = f32[256,128]{1,0:T(8,128)} add(f32[256,128]{1,0:T(8,128)S(1)} %get-tuple-element.61, f32[256,128]{1,0:T(8,128)S(1)} %collective-permute-done.18) | non-fusion elementwise | flops 32768 | bytes 393216 | tf_op jit(solution)/shard_map/add | solution.py:427
  (23 shorter events, 0.4 us)
Async XLA Ops:
  0.6 13.5 %collective-permute-start.6 = (f32[256,128]{1,0:T(8,128)}, f32[256,128]{1,0:T(8,128)S(1)}, u32[]{:S(2)}, u32[]{:S(2)}) collective-permute-start(f32[256,128]{1,0:T(8,128)} %param.3), channel_id=1, source_target_pairs={{0,24},{8,16},{16,8},{24,0},{1,25},{9,17},{17,9},{25,1},{2,26},{10... | collective-permute-start | bytes 393224 | tf_op jit(solution)/shard_map/ppermute | solution.py:59
  5.7 5.2 %collective-permute-start.1 = (f32[256,128]{1,0:T(8,128)}, f32[256,128]{1,0:T(8,128)S(1)}, u32[]{:S(2)}, u32[]{:S(2)}) collective-permute-start(f32[256,128]{1,0:T(8,128)} %param.3), channel_id=1, source_target_pairs={{0,4},{1,5},{2,6},{3,7},{4,0},{5,1},{6,2},{7,3},{8,12},{9,13},{10,... | collective-permute-start | bytes 393224 | tf_op jit(solution)/shard_map/ppermute | solution.py:59
  7.3 5.3 %collective-permute-start = (f32[256,128]{1,0:T(8,128)}, f32[256,128]{1,0:T(8,128)S(1)}, u32[]{:S(2)}, u32[]{:S(2)}) collective-permute-start(f32[256,128]{1,0:T(8,128)} %param.4), channel_id=1, source_target_pairs={{0,2},{1,3},{2,0},{3,1},{4,6},{5,7},{6,4},{7,5},{8,10},{9,11},{10,... | collective-permute-start | bytes 393224 | tf_op jit(solution)/shard_map/ppermute | solution.py:59
  9.8 7.3 %collective-permute-start.5 = (f32[256,128]{1,0:T(8,128)S(1)}, f32[256,128]{1,0:T(8,128)S(1)}, u32[]{:S(2)}, u32[]{:S(2)}) collective-permute-start(f32[256,128]{1,0:T(8,128)S(1)} %get-tuple-element.68.p0), channel_id=1, source_target_pairs={{0,16},{8,24},{16,0},{24,8},{1,17},{9,25},{17,1},{25,9},{2,18},{10... | collective-permute-start | bytes 393224 | tf_op jit(solution)/shard_map/ppermute | solution.py:59
  9.9 7.3 %collective-permute-start.3 = (f32[256,128]{1,0:T(8,128)S(1)}, f32[256,128]{1,0:T(8,128)S(1)}, u32[]{:S(2)}, u32[]{:S(2)}) collective-permute-start(f32[256,128]{1,0:T(8,128)S(1)} %get-tuple-element.68.p0), channel_id=1, source_target_pairs={{0,8},{8,0},{16,24},{24,16},{1,9},{9,1},{17,25},{25,17},{2,10},{10... | collective-permute-start | bytes 393224 | tf_op jit(solution)/shard_map/ppermute | solution.py:59
  10.9 7.1 %collective-permute-start.2 = (f32[512,128]{1,0:T(8,128)S(1)}, f32[512,128]{1,0:T(8,128)S(1)}, u32[]{:S(2)}, u32[]{:S(2)}) collective-permute-start(f32[512,128]{1,0:T(8,128)S(1)} %pad_maximum_fusion.6), channel_id=1, source_target_pairs={{0,2},{1,3},{2,0},{3,1},{4,6},{5,7},{6,4},{7,5},{8,10},{9,11},{10,... | collective-permute-start | bytes 786440 | tf_op jit(solution)/shard_map/ppermute | solution.py:59
  12.6 6.6 %collective-permute-start.4 = (f32[512,128]{1,0:T(8,128)S(1)}, f32[512,128]{1,0:T(8,128)S(1)}, u32[]{:S(2)}, u32[]{:S(2)}) collective-permute-start(f32[512,128]{1,0:T(8,128)S(1)} %pad_maximum_fusion.7), channel_id=1, source_target_pairs={{0,4},{1,5},{2,6},{3,7},{4,0},{5,1},{6,2},{7,3},{8,12},{9,13},{10,... | collective-permute-start | bytes 786440 | tf_op jit(solution)/shard_map/ppermute | solution.py:59
  19.3 2.2 %copy-start = (s32[8,8]{1,0:T(8,128)S(1)}, s32[8,8]{1,0:T(8,128)}, u32[]{:S(2)}) copy-start(s32[8,8]{1,0:T(8,128)} %mask_ref.15) | copy-start | bytes 772
  19.3 3.3 %collective-permute-start.7 = (f32[8,256,128]{2,1,0:T(8,128)S(1)}, f32[8,256,128]{2,1,0:T(8,128)S(1)}, u32[]{:S(2)}, u32[]{:S(2)}) collective-permute-start(f32[8,256,128]{2,1,0:T(8,128)S(1)} %bitcast_dynamic-update-slice_fusion.ss), channel_id=1, source_target_pairs={{0,1},{1,0},{2,3},{3,2},{4,5},{5,4},{6,7},{7,6},{8,9},{9,8},{10,11... | collective-permute-start | bytes 3145736 | tf_op jit(solution)/shard_map/ppermute | solution.py:59
  19.5 9.1 %collective-permute-start.9 = (f32[384,128]{1,0:T(8,128)S(1)}, f32[384,128]{1,0:T(8,128)S(1)}, u32[]{:S(2)}, u32[]{:S(2)}) collective-permute-start(f32[384,128]{1,0:T(8,128)S(1)} %get-tuple-element.69), channel_id=1, source_target_pairs={{0,2},{1,3},{2,0},{3,1},{4,6},{5,7},{6,4},{7,5},{8,10},{9,11},{10,... | collective-permute-start | bytes 589832 | tf_op jit(solution)/shard_map/ppermute | solution.py:59
  21.0 7.6 %collective-permute-start.8 = (f32[384,128]{1,0:T(8,128)S(1)}, f32[384,128]{1,0:T(8,128)S(1)}, u32[]{:S(2)}, u32[]{:S(2)}) collective-permute-start(f32[384,128]{1,0:T(8,128)S(1)} %get-tuple-element.70), channel_id=1, source_target_pairs={{0,4},{1,5},{2,6},{3,7},{4,0},{5,1},{6,2},{7,3},{8,12},{9,13},{10,... | collective-permute-start | bytes 589832 | tf_op jit(solution)/shard_map/ppermute | solution.py:59
  23.3 9.3 %collective-permute-start.14 = (f32[512,128]{1,0:T(8,128)S(1)}, f32[512,128]{1,0:T(8,128)S(1)}, u32[]{:S(2)}, u32[]{:S(2)}) collective-permute-start(f32[512,128]{1,0:T(8,128)S(1)} %get-tuple-element.40.send_ref.q0), channel_id=1, source_target_pairs={{0,16},{24,8},{8,0},{16,24},{1,17},{25,9},{9,1},{17,25},{2,18},{26... | collective-permute-start | bytes 786440 | tf_op jit(solution)/shard_map/ppermute | solution.py:354
  24.2 8.3 %collective-permute-start.13 = (f32[512,128]{1,0:T(8,128)S(1)}, f32[512,128]{1,0:T(8,128)S(1)}, u32[]{:S(2)}, u32[]{:S(2)}) collective-permute-start(f32[512,128]{1,0:T(8,128)S(1)} %get-tuple-element.40.send_ref.q0), channel_id=1, source_target_pairs={{8,16},{16,8},{0,0},{24,24},{9,17},{17,9},{1,1},{25,25},{10,18},{1... | collective-permute-start | bytes 786440 | tf_op jit(solution)/shard_map/ppermute | solution.py:354
  24.9 12.2 %collective-permute-start.12 = (f32[512,128]{1,0:T(8,128)S(1)}, f32[512,128]{1,0:T(8,128)S(1)}, u32[]{:S(2)}, u32[]{:S(2)}) collective-permute-start(f32[512,128]{1,0:T(8,128)S(1)} %get-tuple-element.40.send_ref.q0), channel_id=1, source_target_pairs={{0,8},{24,16},{8,0},{16,24},{1,9},{25,17},{9,1},{17,25},{2,10},{26... | collective-permute-start | bytes 786440 | tf_op jit(solution)/shard_map/ppermute | solution.py:354
  28.5 10.3 %collective-permute-start.10 = (f32[768,128]{1,0:T(8,128)S(1)}, f32[768,128]{1,0:T(8,128)S(1)}, u32[]{:S(2)}, u32[]{:S(2)}) collective-permute-start(f32[768,128]{1,0:T(8,128)S(1)} %pad_maximum_fusion.3), channel_id=1, source_target_pairs={{0,2},{1,3},{2,0},{3,1},{4,6},{5,7},{6,4},{7,5},{8,10},{9,11},{10,... | collective-permute-start | bytes 1179656 | tf_op jit(solution)/shard_map/ppermute | solution.py:59
  29.6 10.3 %collective-permute-start.11 = (f32[768,128]{1,0:T(8,128)S(1)}, f32[768,128]{1,0:T(8,128)S(1)}, u32[]{:S(2)}, u32[]{:S(2)}) collective-permute-start(f32[768,128]{1,0:T(8,128)S(1)} %pad_maximum_fusion.4), channel_id=1, source_target_pairs={{0,4},{1,5},{2,6},{3,7},{4,0},{5,1},{6,2},{7,3},{8,12},{9,13},{10,... | collective-permute-start | bytes 1179656 | tf_op jit(solution)/shard_map/ppermute | solution.py:59
  37.8 7.5 %collective-permute-start.17 = (f32[512,128]{1,0:T(8,128)S(1)}, f32[512,128]{1,0:T(8,128)S(1)}, u32[]{:S(2)}, u32[]{:S(2)}) collective-permute-start(f32[512,128]{1,0:T(8,128)S(1)} %get-tuple-element.58), channel_id=1, source_target_pairs={{0,8},{8,0},{16,24},{24,16},{1,9},{9,1},{17,25},{25,17},{2,10},{10... | collective-permute-start | bytes 786440 | tf_op jit(solution)/shard_map/ppermute | solution.py:59
  40.2 2.4 %collective-permute-start.16 = (f32[2,768,128]{2,1,0:T(8,128)S(1)}, f32[2,768,128]{2,1,0:T(8,128)S(1)}, u32[]{:S(2)}, u32[]{:S(2)}) collective-permute-start(f32[2,768,128]{2,1,0:T(8,128)S(1)} %pad_maximum_fusion.1.hi.s_hi), channel_id=1, source_target_pairs={{0,1},{1,0},{2,3},{3,2},{4,5},{5,4},{6,7},{7,6},{8,9},{9,8},{10,11... | collective-permute-start | bytes 2359304 | tf_op jit(solution)/shard_map/ppermute | solution.py:59
  40.3 3.3 %collective-permute-start.15 = (f32[2,768,128]{2,1,0:T(8,128)S(1)}, f32[2,768,128]{2,1,0:T(8,128)S(1)}, u32[]{:S(2)}, u32[]{:S(2)}) collective-permute-start(f32[2,768,128]{2,1,0:T(8,128)S(1)} %pad_maximum_fusion.lo.s_lo), channel_id=1, source_target_pairs={{0,1},{1,0},{2,3},{3,2},{4,5},{5,4},{6,7},{7,6},{8,9},{9,8},{10,11... | collective-permute-start | bytes 2359304 | tf_op jit(solution)/shard_map/ppermute | solution.py:59
  44.3 5.6 %collective-permute-start.18 = (f32[256,128]{1,0:T(8,128)S(1)}, f32[256,128]{1,0:T(8,128)S(1)}, u32[]{:S(2)}, u32[]{:S(2)}) collective-permute-start(f32[256,128]{1,0:T(8,128)S(1)} %get-tuple-element.62), channel_id=1, source_target_pairs={{0,8},{8,0},{16,24},{24,16},{1,9},{9,1},{17,25},{25,17},{2,10},{10... | collective-permute-start | bytes 393224 | tf_op jit(solution)/shard_map/ppermute | solution.py:59
